TPU v7x, 32 devices: a whole 2x2x4 slice. The times are simulated.
32 devices in a mesh: groups: 2 (over y), adapter: 4 (over z), tensor: 4 (over x, core).
Axes of the slice: x: 2, y: 2, z: 4, core: 2. Of those that a mesh axis runs over, the one named last changes fastest.
Arguments:
- queries: bfloat16 [256, 8192], P(('groups', 'adapter'), 'tensor'), parts along dimension 0, may hold values from -11 to 11
- cache_keys: bfloat16 [256, 64, 1024], P(('groups', 'adapter'), None, 'tensor'), parts along dimension 0, may hold values from -11 to 11
- cached_value_rows: bfloat16 [256, 64, 1024], P(('groups', 'adapter'), None, 'tensor'), parts along dimension 0, may hold values from -6 to 6
- new_keys: bfloat16 [256, 1024], P(('groups', 'adapter'), 'tensor'), parts along dimension 0, may hold values from -11 to 11
- fresh_value_rows: bfloat16 [256, 1024], P(('groups', 'adapter'), 'tensor'), parts along dimension 0, may hold values from -6 to 6
- lengths: int32 [256], P(('groups', 'adapter')), parts along dimension 0, may hold values from 1 to 64, as said below
- adapter_ids: int32 [256], P('groups'), parts along dimension 0, may hold values from 0 to 7, as said below
- adapter_slots: int32 [8], replicated, may hold values from 0 to 7, each once
- out_weight: bfloat16 [8192, 8192], P('tensor', 'adapter'), may hold values from -0.0625 to 0.0625
- shrink_weight: bfloat16 [8, 8192, 64], P('adapter', 'tensor'), may hold values from -0.0625 to 0.0625
- expand_weight: bfloat16 [8, 64, 8192], P('adapter', 'tensor'), may hold values from -0.75 to 0.75
Outputs:
- mixed: bfloat16 [256, 8192], P('groups', 'adapter'), parts along dimension 0
There are 2 independent parts, one for each index of `groups`. A program takes and returns all parts, laid end to end along the dimension named above; an argument that names none is the same for every part. Nothing has to cross between parts.
Inputs may be any that keep to these rules, and one draw needn't show every extreme that they name: `adapter_ids`: within each part, at most 32 requests name one adapter, and some adapter is named by exactly 32 requests. `lengths`: some request has length 64.
All inputs are finite; a program needn't handle non-finite values.
Results may differ from a plain program's by a relative error of at most 0.0085.
Values may be sent and summed in bfloat16 or wider, within the bound.
No kernel may reach another device: no remote copies, remote signals or barrier semaphores. Data moves between devices by JAX's collectives and lax.ppermute only.
A program may use at most 64 MiB of HBM per device.

v0:
```python
import math

import jax
import jax.numpy as jnp
from jax import lax
from jax.sharding import PartitionSpec as P

HEAD_SIZE = 128
SLOTS = 32


adapter_scale = 2.0


def shards(
    queries,
    cache_keys,
    cached_value_rows,
    new_keys,
    fresh_value_rows,
    lengths,
    adapter_ids,
    adapter_slots,
    out_weight,
    shrink_weight,
    expand_weight,
):
    requests = queries.shape[0]
    positions = cache_keys.shape[1]
    kv_local = cache_keys.shape[2] // HEAD_SIZE
    heads_local = queries.shape[1] // HEAD_SIZE
    group_size = heads_local // kv_local
    factor_term = 1.0 / math.sqrt(HEAD_SIZE)
    query_head_count = queries.reshape(requests, kv_local, group_size, HEAD_SIZE)
    key_head_count = cache_keys.reshape(requests, positions, kv_local, HEAD_SIZE)
    value_head_count = cached_value_rows.reshape(requests, positions, kv_local, HEAD_SIZE)
    scores = (
        jnp.einsum(
            "rkgd,rckd->rkgc", query_head_count, key_head_count, preferred_element_type=jnp.float32
        )
        * factor_term
    )
    request_own_score = (
        jnp.einsum(
            "ivhz,ivz->ivh",
            query_head_count,
            new_keys.reshape(requests, kv_local, HEAD_SIZE),
            preferred_element_type=jnp.float32,
        )
        * factor_term
    )
    valid = jnp.arange(positions)[None, None, None, :] < lengths[:, None, None, None]
    scores = jnp.where(valid, scores, -jnp.inf)
    row_top = jnp.maximum(jnp.max(scores, axis=-1), request_own_score)
    powers = jnp.exp(scores - row_top[..., None])
    own_power = jnp.exp(request_own_score - row_top)
    row_total = jnp.sum(powers, axis=-1) + own_power
    weights = (powers / row_total[..., None]).astype(jnp.bfloat16)
    request_own_weight = (own_power / row_total).astype(jnp.bfloat16)
    blended_values = jnp.einsum(
        "rkgc,rckd->rkgd", weights, value_head_count, preferred_element_type=jnp.float32
    )
    blended_values = blended_values + request_own_weight.astype(jnp.float32)[
        ..., None
    ] * fresh_value_rows.reshape(requests, kv_local, 1, HEAD_SIZE).astype(jnp.float32)
    attended = blended_values.reshape(requests, heads_local * HEAD_SIZE).astype(jnp.bfloat16)
    adapters = adapter_slots.shape[0]
    per_owner = shrink_weight.shape[0]
    owner_index = lax.axis_index("adapter")
    matches = (adapter_ids[:, None] == jnp.arange(adapters, dtype=jnp.int32)[None, :]).astype(
        jnp.int32
    )
    rank_within = jnp.sum(jnp.cumsum(matches, axis=0) * matches, axis=1) - 1
    stored = jnp.sum(matches * adapter_slots[None, :], axis=1)
    local_slot = (stored - owner_index * per_owner) * SLOTS + rank_within
    select = (
        jnp.arange(per_owner * SLOTS, dtype=jnp.int32)[:, None] == local_slot[None, :]
    ).astype(jnp.bfloat16)
    shard_rows = lax.all_gather(attended, "adapter", axis=0, tiled=True)
    projected = jnp.dot(shard_rows, out_weight, preferred_element_type=jnp.float32)
    base_rows = projected
    picked = jnp.dot(select, shard_rows, preferred_element_type=jnp.float32)
    base_rows, picked = (base_rows, picked)
    gathered = picked.astype(jnp.bfloat16).reshape(per_owner, SLOTS, attended.shape[1])
    shrink_part = jnp.einsum(
        "asd,adn->asn", gathered, shrink_weight, preferred_element_type=jnp.float32
    )
    shrunk = lax.psum_scatter(shrink_part, "tensor", scatter_dimension=2, tiled=True).astype(
        jnp.bfloat16
    )
    own_blocks = jnp.einsum(
        "asn,anc->asc", shrunk, expand_weight, preferred_element_type=jnp.float32
    )
    term_blocks = lax.all_to_all(own_blocks, "adapter", split_axis=2, concat_axis=0, tiled=True)
    flat_blocks = term_blocks.reshape(adapters * SLOTS, term_blocks.shape[2])
    delta_rows = jnp.take(flat_blocks, stored * SLOTS + rank_within, axis=0)
    summed = base_rows + adapter_scale * delta_rows
    return lax.psum(summed, "tensor").astype(jnp.bfloat16)


def solution(mesh):
    in_specs = (
        P(("groups", "adapter"), "tensor"),
        P(("groups", "adapter"), None, "tensor"),
        P(("groups", "adapter"), None, "tensor"),
        P(("groups", "adapter"), "tensor"),
        P(("groups", "adapter"), "tensor"),
        P(("groups", "adapter")),
        P("groups"),
        P(),
        P("tensor", "adapter"),
        P("adapter", "tensor", None),
        P("adapter", "tensor", None),
    )
    out_specs = P("groups", "adapter")
    return jax.shard_map(shards, mesh=mesh, in_specs=in_specs, out_specs=out_specs, check_vma=False)
```

profile of v0, /device:TPU:0, one launch (start us, length us, event | category | flops | bytes accessed | tf_op | source)
XLA Modules:
  0.0 195.1 jit_solution(15409147592215165532)
XLA Ops:
  6.5 1.0 copy.39
  7.6 0.7 iota_compare_fusion.3
  8.3 2.0 %fusion.17 = (f32[32,2,8]{2,1,0:T(2,128)S(1)}, f32[32,2,8,64]{3,2,1,0:T(8,128)S(1)}) fusion(bf16[32,2,8,128]{3,2,1,0:T(8,128)(2,1)S(1)} %bitcast.64, pred[32,64]{1,0:T(8,128)(4,1)S(1)} %iota_compare_fusion.3, bf16[32,64,256]{2,1,0:T(8,128)(2,1)} %param.12), kind=kOutput, calls=%fused_computation.39 | convolution fusion | flops 8486400 | bytes 1314816 | tf_op jit(solution)/shard_map/rkgd,rckd->rkgc/dot_general | solution.py:38
  10.3 0.1 copy.27
  10.4 0.7 reshape.120
  11.1 0.2 fusion.18
  11.3 0.1 copy.36
  11.4 0.1 copy.28
  11.5 0.3 fusion.6
  11.8 0.1 copy.30
  11.9 0.1 copy.32
  12.1 0.5 fusion.1
  12.6 17.4 %all_gather.3 = bf16[128,2048]{1,0:T(8,128)(2,1)S(1)} all-gather(bf16[32,2048]{1,0:T(8,128)(2,1)S(1)} %bitcast.66), channel_id=1, replica_groups=mesh['groups'=2,'adapter'=4,'tensor'=4] {'adapter'}, dimensions={0}, use_global_device_ids=true | all-gather | bytes 655360 | tf_op jit(solution)/shard_map/all_gather | solution.py:79
  30.0 0.1 fusion.9
  30.1 0.2 reduce_window_sum.11
  30.3 0.2 select_reduce_fusion
  30.4 0.2 convolution_convert_fusion
  30.7 0.9 fusion.19
  31.6 21.3 %reduce-scatter.2.cloned.1.call-done = f32[2,32,16]{1,2,0:T(8,128)} async-done(((f32[2,32,64]{1,2,0:T(8,128)}), f32[2,32,16]{1,2,0:T(8,128)}) %reduce-scatter.2.cloned.1.call-update) | async-done | bytes 4112 | tf_op jit(solution)/shard_map/reduce_scatter | solution.py:88
  53.0 1.5 fusion.11
  54.5 7.9 %copy.33 = f32[2,32,8192]{1,0,2:T(2,128)} copy(f32[2,32,8192]{2,1,0:T(8,128)S(1)} %fusion.11) | data formatting | bytes 4194304 | tf_op jit(solution)/shard_map/asn,anc->asc/dot_general | solution.py:91
  62.3 10.6 %reshape.121 = f32[4,1,131072]{2,1,0:T(1,128)} reshape(f32[8192,2,32]{2,1,0:T(2,128)} %bitcast.61) | data formatting | bytes 4194304
  72.9 4.6 %all-to-all-start = ((f32[4,1,131072]{2,1,0:T(1,128)}), f32[4,1,131072]{2,1,0:T(1,128)S(1)}, u32[]{:S(2)}, u32[]{:S(2)}) async-start(f32[4,1,131072]{2,1,0:T(1,128)} %reshape.121), calls=%async_computation.1 | async-start | bytes 4194304 | tf_op jit(solution)/shard_map/all_to_all | solution.py:94
  77.6 47.7 %all-to-all-done = f32[4,1,131072]{2,1,0:T(1,128)S(1)} async-done(((f32[4,1,131072]{2,1,0:T(1,128)}), f32[4,1,131072]{2,1,0:T(1,128)S(1)}, u32[]{:S(2)}, u32[]{:S(2)}) %all-to-all-start) | async-done | bytes 2097184 | tf_op jit(solution)/shard_map/all_to_all | solution.py:94
  125.3 1.3 copy-done.1
  126.6 0.5 broadcast.107
  127.1 7.7 %reduce = f32[4,131072]{1,0:T(4,128)S(1)} reduce(f32[4,1,131072]{2,1,0:T(1,128)} %copy-done.1, f32[]{:T(128)} %broadcast.107), dimensions={1}, to_apply=%all_to_all.11.reduce_sub_computation | reduce | bytes 4194308 | tf_op jit(solution)/shard_map/all_to_all | solution.py:94
  134.8 10.7 %reshape.122 = f32[8192,2,32]{2,1,0:T(2,128)} reshape(f32[4,131072]{1,0:T(4,128)S(1)} %reduce) | data formatting | bytes 4194304
  145.5 10.2 %copy.34 = f32[2,32,4,2048]{3,1,0,2:T(8,128)S(1)} copy(f32[2,32,4,2048]{1,0,3,2:T(2,128)} %bitcast.62) | data formatting | bytes 4194304 | tf_op jit(solution)/shard_map/all_to_all | solution.py:94
  155.7 1.9 gather_fusion
  157.7 5.1 %convolution_add_fusion = f32[128,2048]{1,0:T(8,128)S(1)} fusion(bf16[128,2048]{1,0:T(8,128)(2,1)} %copy-done.2, bf16[2048,2048]{1,0:T(8,128)(2,1)} %param.19, f32[128,2048]{1,0:T(8,128)} %gather_fusion, pred[128]{0:T(512)(128)(4,1)S(1)} %compare_and_fusion), kind=kOutput, calls=%fused_computation.1 | convolution fusion | flops 1074528256 | bytes 11010176 | tf_op jit(solution)/shard_map/dot_general | solution.py:80
  162.7 25.5 %all-reduce.1 = bf16[128,2048]{1,0:T(8,128)(2,1)} all-reduce(f32[128,2048]{1,0:T(8,128)S(1)} %convolution_add_fusion), channel_id=1, replica_groups=mesh['groups'=2,'adapter'=4,'tensor'=4] {'tensor'}, use_global_device_ids=true, to_apply=%region_6.7 | all-reduce | flops 262144 | bytes 1572864 | tf_op jit(solution)/shard_map/psum | solution.py:98
  (24 shorter events, 0.2 us)
Async XLA Ops:
  6.5 5.5 %copy-start = (bf16[32,64,256]{2,1,0:T(8,128)(2,1)S(1)}, bf16[32,64,256]{2,1,0:T(8,128)(2,1)}, u32[]{:S(2)}) copy-start(bf16[32,64,256]{2,1,0:T(8,128)(2,1)} %param.13) | copy-start | bytes 3145732
  6.5 5.5 %copy-start.4 = (bf16[32,256]{1,0:T(8,128)(2,1)S(1)}, bf16[32,256]{1,0:T(8,128)(2,1)}, u32[]{:S(2)}) copy-start(bf16[32,256]{1,0:T(8,128)(2,1)} %param.15) | copy-start | bytes 49156
  6.5 46.4 %reduce-scatter.2.cloned.1.call-start = ((), (), s32[]{:S(2)}) async-start(), calls=%async_computation.2 | async-start | bytes 81920 | tf_op jit(solution)/shard_map/reduce_scatter | solution.py:88
  12.1 17.9 %copy-start.5 = (s32[128]{0:T(128)S(1)}, s32[128]{0:T(128)}, u32[]{:S(2)}) copy-start(s32[128]{0:T(128)} %param.17) | copy-start | bytes 1540
  12.1 18.2 %copy-start.6 = (s32[8]{0:T(128)S(1)}, s32[8]{0:T(128)}, u32[]{:S(2)}) copy-start(s32[8]{0:T(128)} %param.18) | copy-start | bytes 100
  12.1 18.6 %copy-start.3 = (bf16[2,2048,64]{1,2,0:T(8,128)(2,1)S(1)}, bf16[2,2048,64]{1,2,0:T(8,128)(2,1)}, u32[]{:S(2)}) copy-start(bf16[2,2048,64]{1,2,0:T(8,128)(2,1)} %param.20) | copy-start | bytes 1572868
  30.0 1.6 copy-start.2
  72.9 52.3 %all-to-all-start = ((f32[4,1,131072]{2,1,0:T(1,128)}), f32[4,1,131072]{2,1,0:T(1,128)S(1)}, u32[]{:S(2)}, u32[]{:S(2)}) async-start(f32[4,1,131072]{2,1,0:T(1,128)} %reshape.121), calls=%async_computation.1 | async-start | bytes 4194304 | tf_op jit(solution)/shard_map/all_to_all | solution.py:94
  125.3 1.4 copy-start.1
Sparse Core Ops, SparseCore 0:
  31.7 21.1 reduce-scatter.1
where the time goes:
time: 196 us; the launch traced here: 195 us
  waiting for transfers between devices  69 us (35%)
  local copies, waits for them, and re-layouts  45.5 us (23%)
  blocking collectives  42.9 us (22%)
  between operations  13.6 us (7%)
  matrix products  10.3 us (5%)
  other arithmetic  9.19 us (5%)
  starting transfers between devices  4.6 us (2%)
    all_to_all x1, waiting for transfers between devices, shards(): lax.all_to_all(own_blocks, 'adapter', split_axis=2, concat_axis=0, tiled=...  47.7 us
    psum x1, blocking collectives, shards(): return lax.psum(summed, 'tensor').astype(jnp.bfloat16)  25.5 us
    unnamed x18, local copies, waits for them, and re-layouts  23.8 us
    reduce_scatter x1, waiting for transfers between devices, shards(): lax.psum_scatter(shrink_part, 'tensor', scatter_dimension=2, tiled=True)  21.3 us
    all_gather x1, blocking collectives, shards(): shard_rows = lax.all_gather(attended, 'adapter', axis=0, tiled=True)  17.4 us
    all_to_all x2, local copies, waits for them, and re-layouts, shards(): lax.all_to_all(own_blocks, 'adapter', split_axis=2, concat_axis=0, tiled=...  10.7 us
    dot_general x1, local copies, waits for them, and re-layouts, shards(): jnp.einsum('asn,anc->asc', shrunk, expand_weight, preferred_element_type=...  7.86 us
    all_to_all x1, other arithmetic, shards(): lax.all_to_all(own_blocks, 'adapter', split_axis=2, concat_axis=0, tiled=...  7.69 us
  transfers between devices with their start and end apart: 2, of which 2 were waited for; matrix products, arithmetic and copies ran while one was open for 0% of the time, Pallas kernels for 0%

commit v1 on v0

v1 whole, which is shorter than its diff:
```python
import math

import jax
import jax.numpy as jnp
from jax import lax
from jax.sharding import PartitionSpec as P

HEAD_SIZE = 128
SLOTS = 32
ADAPTER_SCALE = 2.0
BF = jnp.bfloat16
F32 = jnp.float32


def attend(queries, cache_keys, cached_value_rows, new_keys, fresh_value_rows, lengths):
    requests = queries.shape[0]
    positions = cache_keys.shape[1]
    kv_local = cache_keys.shape[2] // HEAD_SIZE
    heads_local = queries.shape[1] // HEAD_SIZE
    group_size = heads_local // kv_local
    factor_term = 1.0 / math.sqrt(HEAD_SIZE)
    q = queries.reshape(requests, kv_local, group_size, HEAD_SIZE)
    k = cache_keys.reshape(requests, positions, kv_local, HEAD_SIZE)
    v = cached_value_rows.reshape(requests, positions, kv_local, HEAD_SIZE)
    scores = jnp.einsum("rkgd,rckd->rkgc", q, k, preferred_element_type=F32) * factor_term
    own = (
        jnp.einsum(
            "ivhz,ivz->ivh",
            q,
            new_keys.reshape(requests, kv_local, HEAD_SIZE),
            preferred_element_type=F32,
        )
        * factor_term
    )
    valid = jnp.arange(positions)[None, None, None, :] < lengths[:, None, None, None]
    scores = jnp.where(valid, scores, -jnp.inf)
    row_top = jnp.maximum(jnp.max(scores, axis=-1), own)
    powers = jnp.exp(scores - row_top[..., None])
    own_power = jnp.exp(own - row_top)
    row_total = jnp.sum(powers, axis=-1) + own_power
    weights = (powers / row_total[..., None]).astype(BF)
    own_weight = (own_power / row_total).astype(BF)
    blended = jnp.einsum("rkgc,rckd->rkgd", weights, v, preferred_element_type=F32)
    blended = blended + own_weight.astype(F32)[..., None] * fresh_value_rows.reshape(
        requests, kv_local, 1, HEAD_SIZE
    ).astype(F32)
    return blended.reshape(requests, heads_local * HEAD_SIZE).astype(BF)


def make_shards(n_adapter, n_tensor):
    def swap(x, axis, n, k):
        return lax.ppermute(x, axis, [(i, i ^ k) for i in range(n)])

    def shards(
        queries,
        cache_keys,
        cached_value_rows,
        new_keys,
        fresh_value_rows,
        lengths,
        adapter_ids,
        adapter_slots,
        out_weight,
        shrink_weight,
        expand_weight,
    ):
        a = lax.axis_index("adapter")
        t = lax.axis_index("tensor")
        low = t % 2
        adapters = adapter_slots.shape[0]
        per_owner, rank_part, width = expand_weight.shape
        rank = shrink_weight.shape[2]
        columns = out_weight.shape[1]
        half = columns // 2
        requests = queries.shape[0]
        tokens = adapter_ids.shape[0]
        owned = per_owner * SLOTS

        up = expand_weight.reshape(per_owner, rank_part, n_adapter, 2, half)
        up_keep = lax.dynamic_index_in_dim(up, low, 3, keepdims=False)
        up_send = lax.dynamic_index_in_dim(up, 1 - low, 3, keepdims=False)
        up = jnp.concatenate([up_keep, swap(up_send, "tensor", n_tensor, 1)], axis=1)
        step = 2
        while step < n_tensor:
            up = jnp.concatenate([up, swap(up, "tensor", n_tensor, step)], axis=1)
            step *= 2
        up = up.reshape(per_owner * rank, n_adapter * half)

        attended = attend(
            queries, cache_keys, cached_value_rows, new_keys, fresh_value_rows, lengths
        )

        matches = adapter_ids[:, None] == jnp.arange(adapters, dtype=jnp.int32)[None, :]
        counts = matches.astype(jnp.int32)
        rank_within = jnp.sum(jnp.cumsum(counts, axis=0) * counts, axis=1) - 1
        stored = jnp.sum(counts * adapter_slots[None, :], axis=1)
        owner = stored // per_owner
        slot = (stored % per_owner) * SLOTS + rank_within

        blocks = [attended] + [swap(attended, "adapter", n_adapter, k) for k in range(1, n_adapter)]
        rows = jnp.zeros((tokens, queries.shape[1]), BF)
        for k, block in enumerate(blocks):
            rows = lax.dynamic_update_slice(rows, block, ((a ^ k) * requests, 0))

        parts = jnp.einsum("rd,adn->arn", rows, shrink_weight, preferred_element_type=F32)
        here = stored[None, :] - a * per_owner == jnp.arange(per_owner, dtype=jnp.int32)[:, None]
        shrunk = jnp.sum(jnp.where(here[:, :, None], parts, 0.0), axis=0)
        step = 1
        while step < n_tensor:
            shrunk = shrunk + swap(shrunk, "tensor", n_tensor, step)
            step *= 2
        shrunk = shrunk.astype(BF)

        base = jnp.dot(rows, out_weight, preferred_element_type=F32)
        base_keep = lax.dynamic_slice_in_dim(base, low * half, half, 1)
        base_send = lax.dynamic_slice_in_dim(base, (1 - low) * half, half, 1).astype(BF)
        base = (base_keep + swap(base_send, "tensor", n_tensor, 1).astype(F32)).astype(BF)
        total = base.astype(F32)
        step = 2
        while step < n_tensor:
            total = total + swap(total.astype(BF), "tensor", n_tensor, step).astype(F32)
            step *= 2

        positions = jnp.arange(rank, dtype=jnp.int32)
        source = ((positions // rank_part) ^ t) * rank_part + positions % rank_part
        reorder = (jnp.arange(rank, dtype=jnp.int32)[:, None] == source[None, :]).astype(BF)
        select = (
            (jnp.arange(owned, dtype=jnp.int32)[:, None] == slot[None, :]) & (owner[None, :] == a)
        ).astype(BF)
        held = jnp.dot(jnp.dot(select, shrunk).astype(BF), reorder).astype(BF)
        in_block = (
            jnp.arange(owned, dtype=jnp.int32)[:, None] // SLOTS
            == jnp.arange(per_owner, dtype=jnp.int32)[None, :]
        )
        wide = jnp.where(in_block[:, :, None], held[:, None, :], 0).reshape(owned, -1)
        terms = jnp.dot(wide.astype(BF), up, preferred_element_type=F32).astype(BF)
        received = []
        for k in range(n_adapter):
            piece = lax.dynamic_slice_in_dim(terms, (a ^ k) * half, half, 1)
            received.append(swap(piece, "adapter", n_adapter, k) if k else piece)
        received = jnp.concatenate(received, axis=0)
        place = (
            ((owner ^ a) * owned + slot)[:, None]
            == jnp.arange(n_adapter * owned, dtype=jnp.int32)[None, :]
        ).astype(BF)
        delta = jnp.dot(place, received, preferred_element_type=F32)
        mine = (total + ADAPTER_SCALE * delta).astype(BF)
        other = swap(mine, "tensor", n_tensor, 1)
        return jnp.where(
            low == 0,
            jnp.concatenate([mine, other], axis=1),
            jnp.concatenate([other, mine], axis=1),
        )

    return shards


def solution(mesh):
    in_specs = (
        P(("groups", "adapter"), "tensor"),
        P(("groups", "adapter"), None, "tensor"),
        P(("groups", "adapter"), None, "tensor"),
        P(("groups", "adapter"), "tensor"),
        P(("groups", "adapter"), "tensor"),
        P(("groups", "adapter")),
        P("groups"),
        P(),
        P("tensor", "adapter"),
        P("adapter", "tensor", None),
        P("adapter", "tensor", None),
    )
    out_specs = P("groups", "adapter")
    shards = make_shards(mesh.shape["adapter"], mesh.shape["tensor"])
    return jax.shard_map(shards, mesh=mesh, in_specs=in_specs, out_specs=out_specs, check_vma=False)
```

time: 196 us -> 64.7 us (0.33)
  waiting for transfers between devices: 69 us -> 25.6 us
  blocking collectives: 42.9 us -> 0 us
  local copies, waits for them, and re-layouts: 45.5 us -> 9.96 us
  between operations: 13.6 us -> 0.47 us
  starting transfers between devices: 4.6 us -> 13.9 us
  other arithmetic: 9.19 us -> 5.95 us
    all_to_all x1 -> x0, waiting for transfers between devices: 47.7 us -> none  [shards(): lax.all_to_all(own_blocks, 'adapter', split_axis=2, concat_axis=0, tiled=...]
    ppermute x0 -> x13, waiting for transfers between devices: none -> 25.6 us  [swap(): return lax.ppermute(x, axis, [(i, i ^ k) for i in range(n)])]
    psum x1 -> x0, blocking collectives: 25.5 us -> none  [shards(): return lax.psum(summed, 'tensor').astype(jnp.bfloat16)]
    unnamed x18 -> x19, local copies, waits for them, and re-layouts: 23.8 us -> 2.14 us
    reduce_scatter x1 -> x0, waiting for transfers between devices: 21.3 us -> none  [shards(): lax.psum_scatter(shrink_part, 'tensor', scatter_dimension=2, tiled=True)]
    all_gather x1 -> x0, blocking collectives: 17.4 us -> none  [shards(): shard_rows = lax.all_gather(attended, 'adapter', axis=0, tiled=True)]
    ppermute x0 -> x13, starting transfers between devices: none -> 13.9 us  [swap(): return lax.ppermute(x, axis, [(i, i ^ k) for i in range(n)])]
    all_to_all x2 -> x0, local copies, waits for them, and re-layouts: 10.7 us -> none  [shards(): lax.all_to_all(own_blocks, 'adapter', split_axis=2, concat_axis=0, tiled=...]
  transfers between devices with their start and end apart: 2 -> 13, of which waited for: 2 -> 5; matrix products, arithmetic and copies ran while one was open for 0% -> 26% of each run, Pallas kernels for 0% -> 0%
where the time goes in v1:
time: 64.7 us; the launch traced here: 64.3 us
  waiting for transfers between devices  25.6 us (40%)
  starting transfers between devices  13.9 us (21%)
  local copies, waits for them, and re-layouts  9.96 us (15%)
  matrix products  8.38 us (13%)
  other arithmetic  5.95 us (9%)
    ppermute x13, waiting for transfers between devices, swap(): return lax.ppermute(x, axis, [(i, i ^ k) for i in range(n)])  25.6 us
    ppermute x13, starting transfers between devices, swap(): return lax.ppermute(x, axis, [(i, i ^ k) for i in range(n)])  13.9 us
    dot_general x1, matrix products, shards(): base = jnp.dot(rows, out_weight, preferred_element_type=F32)  4.63 us
    dynamic_update_slice x4, local copies, waits for them, and re-layouts, shards(): rows = lax.dynamic_update_slice(rows, block, ((a ^ k) * requests, 0))  2.78 us
    unnamed x19, local copies, waits for them, and re-layouts  2.14 us
    dot_general x1, matrix products, attend(): jnp.einsum('rkgd,rckd->rkgc', q, k, preferred_element_type=F32)  1.97 us
    dynamic_slice x2, local copies, waits for them, and re-layouts, shards(): up_keep = lax.dynamic_index_in_dim(up, low, 3, keepdims=False)  1.4 us
  transfers between devices with their start and end apart: 13, of which 5 were waited for; matrix products, arithmetic and copies ran while one was open for 26% of the time, Pallas kernels for 0%

profile of v1, /device:TPU:0, one launch (start us, length us, event | category | flops | bytes accessed | tf_op | source)
XLA Modules:
  0.0 64.3 jit_solution(12468138611606283094)
XLA Ops:
  0.0 1.0 %copy.48 = bf16[4,8,16,128]{3,2,1,0:T(8,128)(2,1)S(1)} copy(bf16[4,8,16,128]{3,1,2,0:T(8,128)(2,1)} %bitcast.77) | data formatting | bytes 262144
  1.0 0.7 %iota_compare_fusion.7 = pred[32,64]{1,0:T(8,128)(4,1)S(1)} fusion(s32[32]{0:T(128)} %param.16), kind=kLoop, calls=%fused_computation.48 | loop fusion | flops 2048 | bytes 2176 | tf_op jit(solution)/shard_map/lt | solution.py:35
  1.8 2.0 %fusion.41 = (f32[32,2,8]{2,1,0:T(2,128)S(1)}, f32[32,2,8,64]{3,2,1,0:T(8,128)S(1)}) fusion(bf16[32,2,8,128]{3,2,1,0:T(8,128)(2,1)S(1)} %bitcast.70, pred[32,64]{1,0:T(8,128)(4,1)S(1)} %iota_compare_fusion.7, bf16[32,64,256]{2,1,0:T(8,128)(2,1)} %param.12), kind=kOutput, calls=%fused_computation.89 | convolution fusion | flops 8486400 | bytes 1314816 | tf_op jit(solution)/shard_map/rkgd,rckd->rkgc/dot_general | solution.py:25
  3.8 0.7 %reshape.258 = bf16[32,2,128,1]{2,3,1,0:T(2,128)(2,1)S(1)} reshape(bf16[32,256]{1,0:T(8,128)(2,1)} %param.14) | data formatting | bytes 32768 | tf_op jit(solution)/shard_map/reshape | solution.py:30
  5.6 0.5 fusion.1
  6.0 0.7 %copy.68 = bf16[4,8,16,128]{3,1,2,0:T(8,128)(2,1)} copy(bf16[4,8,16,128]{3,2,1,0:T(8,128)(2,1)S(1)} %bitcast.73) | data formatting | bytes 262144
  6.7 3.0 %collective-permute-start = (bf16[32,2048]{1,0:T(8,128)(2,1)}, bf16[32,2048]{1,0:T(8,128)(2,1)}, u32[]{:S(2)}, u32[]{:S(2)}) collective-permute-start(bf16[32,2048]{1,0:T(8,128)(2,1)} %bitcast.65), channel_id=1, source_target_pairs={{0,4},{4,0},{8,12},{12,8},{1,5},{5,1},{9,13},{13,9},{2,6},{6,2},{1... | collective-permute-start | bytes 393224 | tf_op jit(solution)/shard_map/ppermute | solution.py:52
  9.7 2.6 %collective-permute-start.1 = (bf16[32,2048]{1,0:T(8,128)(2,1)}, bf16[32,2048]{1,0:T(8,128)(2,1)}, u32[]{:S(2)}, u32[]{:S(2)}) collective-permute-start(bf16[32,2048]{1,0:T(8,128)(2,1)} %bitcast.65), channel_id=1, source_target_pairs={{0,8},{4,12},{8,0},{12,4},{1,9},{5,13},{9,1},{13,5},{2,10},{6,14},... | collective-permute-start | bytes 393224 | tf_op jit(solution)/shard_map/ppermute | solution.py:52
  12.7 1.1 %constant_dynamic-slice_fusion.4 = (bf16[2,16,4,1,1024]{4,3,2,1,0:T(2,128)(2,1)S(1)}, bf16[2,16,4,1,1024]{4,3,2,1,0:T(2,128)(2,1)S(1)}) fusion(bf16[2,16,4,2,1024]{4,3,2,1,0:T(2,128)(2,1)S(1)} %reshape.250, s32[]{:T(128)S(6)} %select_n.147, s32[]{:T(128)S(6)} %select_n.148), kind=kLoop, calls=%fused_computation.59 | loop fusion | bytes 1048584 | tf_op jit(solution)/shard_map/jit(dynamic_index_in_dim)/dynamic_slice | solution.py:80
  15.0 0.6 multiply_add_fusion
  15.8 0.6 broadcast_compare_fusion
  16.4 0.9 %constant_dynamic-update-slice_fusion.2 = bf16[128,2048]{1,0:T(8,128)(2,1)S(1)} fusion(bf16[128,2048]{1,0:T(8,128)(2,1)S(1)} %constant_dynamic-update-slice_fusion.3, bf16[32,2048]{1,0:T(8,128)(2,1)} %collective-permute-done, s32[]{:T(128)S(6)} %select_n.134), kind=kLoop, calls=%fused_computation.63 | loop fusion | bytes 262148 | tf_op jit(solution)/shard_map/dynamic_update_slice | solution.py:103
  17.3 5.7 %collective-permute-done.1 = bf16[32,2048]{1,0:T(8,128)(2,1)} collective-permute-done((bf16[32,2048]{1,0:T(8,128)(2,1)}, bf16[32,2048]{1,0:T(8,128)(2,1)}, u32[]{:S(2)}, u32[]{:S(2)}) %collective-permute-start.1) | collective-permute-done | bytes 131104 | tf_op jit(solution)/shard_map/ppermute | solution.py:52
  23.0 0.9 %constant_dynamic-update-slice_fusion.1 = bf16[128,2048]{1,0:T(8,128)(2,1)S(1)} fusion(bf16[128,2048]{1,0:T(8,128)(2,1)S(1)} %constant_dynamic-update-slice_fusion.2, bf16[32,2048]{1,0:T(8,128)(2,1)} %collective-permute-done.1, s32[]{:T(128)S(6)} %select_n.135), kind=kLoop, calls=%fused_computation.62 | loop fusion | bytes 262148 | tf_op jit(solution)/shard_map/dynamic_update_slice | solution.py:103
  23.9 0.9 %constant_dynamic-update-slice_fusion = bf16[128,2048]{1,0:T(8,128)(2,1)S(1)} fusion(bf16[128,2048]{1,0:T(8,128)(2,1)S(1)} %constant_dynamic-update-slice_fusion.1, bf16[32,2048]{1,0:T(8,128)(2,1)} %collective-permute-done.2, s32[]{:T(128)S(6)} %select_n.136), kind=kLoop, calls=%fused_computation.61 | loop fusion | bytes 262148 | tf_op jit(solution)/shard_map/dynamic_update_slice | solution.py:103
  25.3 4.6 %fusion.43 = f32[128,2048]{1,0:T(8,128)S(1)} fusion(bf16[128,2048]{1,0:T(8,128)(2,1)S(1)} %constant_dynamic-update-slice_fusion, bf16[2048,2048]{1,0:T(8,128)(2,1)} %param.19), kind=kOutput, calls=%fused_computation.91 | convolution fusion | flops 1073741824 | bytes 9961472 | tf_op jit(solution)/shard_map/dot_general | solution.py:114
  29.9 0.7 %dynamic-slice_convert_fusion = bf16[128,1024]{1,0:T(8,128)(2,1)} fusion(f32[128,2048]{1,0:T(8,128)S(1)} %fusion.43, s32[]{:T(128)S(6)} %select_n.138), kind=kLoop, calls=%fused_computation.24 | loop fusion | bytes 524292 | tf_op jit(solution)/shard_map/convert_element_type | solution.py:116
  30.7 0.5 collective-permute-start.3
  31.2 1.6 %collective-permute-start.6 = (f32[128,64]{0,1:T(8,128)S(1)}, f32[128,64]{0,1:T(8,128)S(1)}, u32[]{:S(2)}, u32[]{:S(2)}) collective-permute-start(f32[128,64]{0,1:T(8,128)S(1)} %add.155), channel_id=1, source_target_pairs={{0,2},{1,3},{2,0},{3,1},{4,6},{5,7},{6,4},{7,5},{8,10},{9,11},{10,... | collective-permute-start | bytes 98312 | tf_op jit(solution)/shard_map/ppermute | solution.py:52
  32.8 0.6 collective-permute-start.8
  33.4 1.8 %collective-permute-done.6 = f32[128,64]{0,1:T(8,128)S(1)} collective-permute-done((f32[128,64]{0,1:T(8,128)S(1)}, f32[128,64]{0,1:T(8,128)S(1)}, u32[]{:S(2)}, u32[]{:S(2)}) %collective-permute-start.6) | collective-permute-done | bytes 32800 | tf_op jit(solution)/shard_map/ppermute | solution.py:52
  35.6 1.0 %add_convert_fusion.1 = bf16[128,1024]{1,0:T(8,128)(2,1)S(1)} fusion(bf16[128,1024]{1,0:T(8,128)(2,1)} %collective-permute-done.3, f32[128,2048]{1,0:T(8,128)S(1)} %fusion.43, s32[]{:T(128)S(6)} %select_n.137), kind=kLoop, calls=%fused_computation.23 | loop fusion | flops 393216 | bytes 1048580 | tf_op jit(solution)/shard_map/convert_element_type | solution.py:117
  36.7 1.9 %collective-permute-start.4 = (bf16[128,1024]{1,0:T(8,128)(2,1)S(1)}, bf16[128,1024]{1,0:T(8,128)(2,1)S(1)}, u32[]{:S(2)}, u32[]{:S(2)}) collective-permute-start(bf16[128,1024]{1,0:T(8,128)(2,1)S(1)} %add_convert_fusion.1), channel_id=1, source_target_pairs={{0,2},{1,3},{2,0},{3,1},{4,6},{5,7},{6,4},{7,5},{8,10},{9,11},{10,... | collective-permute-start | bytes 786440 | tf_op jit(solution)/shard_map/ppermute | solution.py:52
  38.5 9.2 %collective-permute-done.8 = bf16[2,32,4,1024]{3,1,2,0:T(8,128)(2,1)} collective-permute-done((bf16[2,32,4,1024]{3,1,2,0:T(8,128)(2,1)S(1)}, bf16[2,32,4,1024]{3,1,2,0:T(8,128)(2,1)}, u32[]{:S(2)}, u32[]{:S(2)}) %collective-permute-start.8) | collective-permute-done | bytes 524320 | tf_op jit(solution)/shard_map/ppermute | solution.py:52
  47.8 1.1 %pad_maximum_fusion = bf16[2,64,4,1024]{3,1,2,0:T(8,128)(2,1)S(1)} fusion(bf16[2,32,4,1024]{3,1,2,0:T(8,128)(2,1)} %collective-permute-done.8, bf16[2,16,4,1024]{3,1,2,0:T(8,128)(2,1)S(1)} %collective-permute-done.7, bf16[2,16,4,1024]{3,1,2,0:T(8,128)(2,1)S(1)} %bitcast.69), kind=kLoop, calls=%fused_computation.12 | loop fusion | flops 3145728 | bytes 2097152 | tf_op jit(solution)/shard_map/concatenate | solution.py:85
  48.9 0.8 %copy.43 = bf16[2,64,4,1024]{3,2,1,0:T(4,128)(2,1)S(1)} copy(bf16[2,64,4,1024]{3,1,2,0:T(8,128)(2,1)S(1)} %pad_maximum_fusion) | data formatting | bytes 2097152 | tf_op jit(solution)/shard_map/concatenate | solution.py:85
  49.7 0.4 copy.50
  50.5 2.1 %collective-permute-start.10 = (bf16[64,1024]{1,0:T(8,128)(2,1)S(1)}, bf16[64,1024]{1,0:T(8,128)(2,1)S(1)}, u32[]{:S(2)}, u32[]{:S(2)}) collective-permute-start(bf16[64,1024]{1,0:T(8,128)(2,1)S(1)} %get-tuple-element.12), channel_id=1, source_target_pairs={{0,8},{4,12},{8,0},{12,4},{1,9},{5,13},{9,1},{13,5},{2,10},{6,14},... | collective-permute-start | bytes 393224 | tf_op jit(solution)/shard_map/ppermute | solution.py:52
  52.6 1.4 %collective-permute-start.11 = (bf16[64,1024]{1,0:T(8,128)(2,1)S(1)}, bf16[64,1024]{1,0:T(8,128)(2,1)S(1)}, u32[]{:S(2)}, u32[]{:S(2)}) collective-permute-start(bf16[64,1024]{1,0:T(8,128)(2,1)S(1)} %get-tuple-element.11), channel_id=1, source_target_pairs={{0,12},{4,8},{8,4},{12,0},{1,13},{5,9},{9,5},{13,1},{2,14},{6,10},... | collective-permute-start | bytes 393224 | tf_op jit(solution)/shard_map/ppermute | solution.py:52
  54.0 7.4 %collective-permute-done.10 = bf16[64,1024]{1,0:T(8,128)(2,1)S(1)} collective-permute-done((bf16[64,1024]{1,0:T(8,128)(2,1)S(1)}, bf16[64,1024]{1,0:T(8,128)(2,1)S(1)}, u32[]{:S(2)}, u32[]{:S(2)}) %collective-permute-start.10) | collective-permute-done | bytes 131104 | tf_op jit(solution)/shard_map/ppermute | solution.py:52
  61.8 1.5 %collective-permute-done.12 = bf16[128,1024]{1,0:T(8,128)(2,1)S(1)} collective-permute-done((bf16[128,1024]{1,0:T(8,128)(2,1)S(1)}, bf16[128,1024]{1,0:T(8,128)(2,1)S(1)}, u32[]{:S(2)}, u32[]{:S(2)}) %collective-permute-start.12) | collective-permute-done | bytes 262176 | tf_op jit(solution)/shard_map/ppermute | solution.py:52
  63.4 0.9 %maximum_select_fusion = bf16[128,2048]{1,0:T(8,128)(2,1)} fusion(bf16[128,1024]{1,0:T(8,128)(2,1)S(1)} %collective-permute-done.12, bf16[128,1024]{1,0:T(8,128)(2,1)S(1)} %add_convert_fusion, pred[]{:T(512)S(6)} %eq.104), kind=kLoop, calls=%fused_computation.21 | loop fusion | flops 2359296 | bytes 1048577 | tf_op jit(solution)/shard_map/jit(_where)/select_n | solution.py:149
  (61 shorter events, 4.4 us)
Async XLA Ops:
  0.0 5.5 %copy-start = (bf16[32,64,256]{2,1,0:T(8,128)(2,1)S(1)}, bf16[32,64,256]{2,1,0:T(8,128)(2,1)}, u32[]{:S(2)}) copy-start(bf16[32,64,256]{2,1,0:T(8,128)(2,1)} %param.13) | copy-start | bytes 3145732
  0.0 5.5 %copy-start.3 = (bf16[32,256]{1,0:T(8,128)(2,1)S(1)}, bf16[32,256]{1,0:T(8,128)(2,1)}, u32[]{:S(2)}) copy-start(bf16[32,256]{1,0:T(8,128)(2,1)} %param.15) | copy-start | bytes 49156
  5.5 6.8 %copy-start.1 = (bf16[2,16,8192]{2,1,0:T(8,128)(2,1)S(1)}, bf16[2,16,8192]{2,1,0:T(8,128)(2,1)}, u32[]{:S(2)}) copy-start(bf16[2,16,8192]{2,1,0:T(8,128)(2,1)} %param.21) | copy-start | bytes 1572868
  6.7 9.7 %collective-permute-start = (bf16[32,2048]{1,0:T(8,128)(2,1)}, bf16[32,2048]{1,0:T(8,128)(2,1)}, u32[]{:S(2)}, u32[]{:S(2)}) collective-permute-start(bf16[32,2048]{1,0:T(8,128)(2,1)} %bitcast.65), channel_id=1, source_target_pairs={{0,4},{4,0},{8,12},{12,8},{1,5},{5,1},{9,13},{13,9},{2,6},{6,2},{1... | collective-permute-start | bytes 393224 | tf_op jit(solution)/shard_map/ppermute | solution.py:52
  9.7 13.3 %collective-permute-start.1 = (bf16[32,2048]{1,0:T(8,128)(2,1)}, bf16[32,2048]{1,0:T(8,128)(2,1)}, u32[]{:S(2)}, u32[]{:S(2)}) collective-permute-start(bf16[32,2048]{1,0:T(8,128)(2,1)} %bitcast.65), channel_id=1, source_target_pairs={{0,8},{4,12},{8,0},{12,4},{1,9},{5,13},{9,1},{13,5},{2,10},{6,14},... | collective-permute-start | bytes 393224 | tf_op jit(solution)/shard_map/ppermute | solution.py:52
  12.3 11.6 %collective-permute-start.2 = (bf16[32,2048]{1,0:T(8,128)(2,1)}, bf16[32,2048]{1,0:T(8,128)(2,1)}, u32[]{:S(2)}, u32[]{:S(2)}) collective-permute-start(bf16[32,2048]{1,0:T(8,128)(2,1)} %bitcast.65), channel_id=1, source_target_pairs={{0,12},{4,8},{8,4},{12,0},{1,13},{5,9},{9,5},{13,1},{2,14},{6,10},... | collective-permute-start | bytes 393224 | tf_op jit(solution)/shard_map/ppermute | solution.py:52
  12.7 1.9 %copy-start.4 = (s32[128]{0:T(128)S(1)}, s32[128]{0:T(128)}, u32[]{:S(2)}) copy-start(s32[128]{0:T(128)} %param.17) | copy-start | bytes 1540
  12.7 2.1 %copy-start.5 = (s32[8]{0:T(128)S(1)}, s32[8]{0:T(128)}, u32[]{:S(2)}) copy-start(s32[8]{0:T(128)} %param.18) | copy-start | bytes 100
  13.9 11.0 %copy-start.2 = (bf16[2,2048,64]{1,2,0:T(8,128)(2,1)S(1)}, bf16[2,2048,64]{1,2,0:T(8,128)(2,1)}, u32[]{:S(2)}) copy-start(bf16[2,2048,64]{1,2,0:T(8,128)(2,1)} %param.20) | copy-start | bytes 1572868
  14.2 18.6 %collective-permute-start.7 = (bf16[2,16,4,1024]{3,1,2,0:T(8,128)(2,1)S(1)}, bf16[2,16,4,1024]{3,1,2,0:T(8,128)(2,1)S(1)}, u32[]{:S(2)}, u32[]{:S(2)}) collective-permute-start(bf16[2,16,4,1024]{3,1,2,0:T(8,128)(2,1)S(1)} %bitcast.75), channel_id=1, source_target_pairs={{0,1},{1,0},{2,3},{3,2},{4,5},{5,4},{6,7},{7,6},{8,9},{9,8},{10,11... | collective-permute-start | bytes 786440 | tf_op jit(solution)/shard_map/ppermute | solution.py:52
  25.2 10.0 %copy-start.6 = (pred[128]{0:T(512)(128)(4,1)S(1)}, pred[128]{0:T(512)(128)(4,1)}, u32[]{:S(2)}) copy-start(pred[128]{0:T(512)(128)(4,1)} %broadcast_compare_fusion) | copy-start | bytes 388
  25.2 6.0 %collective-permute-start.5 = (f32[128,64]{0,1:T(8,128)S(1)}, f32[128,64]{0,1:T(8,128)S(1)}, u32[]{:S(2)}, u32[]{:S(2)}) collective-permute-start(f32[128,64]{0,1:T(8,128)S(1)} %select_reduce_fusion), channel_id=1, source_target_pairs={{0,1},{1,0},{2,3},{3,2},{4,5},{5,4},{6,7},{7,6},{8,9},{9,8},{10,11... | collective-permute-start | bytes 98312 | tf_op jit(solution)/shard_map/ppermute | solution.py:52
  30.7 5.0 %collective-permute-start.3 = (bf16[128,1024]{1,0:T(8,128)(2,1)}, bf16[128,1024]{1,0:T(8,128)(2,1)}, u32[]{:S(2)}, u32[]{:S(2)}) collective-permute-start(bf16[128,1024]{1,0:T(8,128)(2,1)} %dynamic-slice_convert_fusion), channel_id=1, source_target_pairs={{0,1},{1,0},{2,3},{3,2},{4,5},{5,4},{6,7},{7,6},{8,9},{9,8},{10,11... | collective-permute-start | bytes 786440 | tf_op jit(solution)/shard_map/ppermute | solution.py:52
  31.2 4.0 %collective-permute-start.6 = (f32[128,64]{0,1:T(8,128)S(1)}, f32[128,64]{0,1:T(8,128)S(1)}, u32[]{:S(2)}, u32[]{:S(2)}) collective-permute-start(f32[128,64]{0,1:T(8,128)S(1)} %add.155), channel_id=1, source_target_pairs={{0,2},{1,3},{2,0},{3,1},{4,6},{5,7},{6,4},{7,5},{8,10},{9,11},{10,... | collective-permute-start | bytes 98312 | tf_op jit(solution)/shard_map/ppermute | solution.py:52
  32.8 15.0 %collective-permute-start.8 = (bf16[2,32,4,1024]{3,1,2,0:T(8,128)(2,1)S(1)}, bf16[2,32,4,1024]{3,1,2,0:T(8,128)(2,1)}, u32[]{:S(2)}, u32[]{:S(2)}) collective-permute-start(bf16[2,32,4,1024]{3,1,2,0:T(8,128)(2,1)S(1)} %pad_maximum_fusion.1), channel_id=1, source_target_pairs={{0,2},{1,3},{2,0},{3,1},{4,6},{5,7},{6,4},{7,5},{8,10},{9,11},{10,... | collective-permute-start | bytes 1572872 | tf_op jit(solution)/shard_map/ppermute | solution.py:52
  36.7 17.4 %collective-permute-start.4 = (bf16[128,1024]{1,0:T(8,128)(2,1)S(1)}, bf16[128,1024]{1,0:T(8,128)(2,1)S(1)}, u32[]{:S(2)}, u32[]{:S(2)}) collective-permute-start(bf16[128,1024]{1,0:T(8,128)(2,1)S(1)} %add_convert_fusion.1), channel_id=1, source_target_pairs={{0,2},{1,3},{2,0},{3,1},{4,6},{5,7},{6,4},{7,5},{8,10},{9,11},{10,... | collective-permute-start | bytes 786440 | tf_op jit(solution)/shard_map/ppermute | solution.py:52
  49.7 11.7 %copy-start.7 = (s32[128]{0:T(128)S(1)}, s32[128]{0:T(128)}, u32[]{:S(2)}) copy-start(s32[128]{0:T(128)} %get-tuple-element.7) | copy-start | bytes 1540
  50.5 11.0 %collective-permute-start.10 = (bf16[64,1024]{1,0:T(8,128)(2,1)S(1)}, bf16[64,1024]{1,0:T(8,128)(2,1)S(1)}, u32[]{:S(2)}, u32[]{:S(2)}) collective-permute-start(bf16[64,1024]{1,0:T(8,128)(2,1)S(1)} %get-tuple-element.12), channel_id=1, source_target_pairs={{0,8},{4,12},{8,0},{12,4},{1,9},{5,13},{9,1},{13,5},{2,10},{6,14},... | collective-permute-start | bytes 393224 | tf_op jit(solution)/shard_map/ppermute | solution.py:52
  52.6 8.9 %collective-permute-start.11 = (bf16[64,1024]{1,0:T(8,128)(2,1)S(1)}, bf16[64,1024]{1,0:T(8,128)(2,1)S(1)}, u32[]{:S(2)}, u32[]{:S(2)}) collective-permute-start(bf16[64,1024]{1,0:T(8,128)(2,1)S(1)} %get-tuple-element.11), channel_id=1, source_target_pairs={{0,12},{4,8},{8,4},{12,0},{1,13},{5,9},{9,5},{13,1},{2,14},{6,10},... | collective-permute-start | bytes 393224 | tf_op jit(solution)/shard_map/ppermute | solution.py:52
  53.9 7.5 %collective-permute-start.9 = (bf16[64,1024]{1,0:T(8,128)(2,1)S(1)}, bf16[64,1024]{1,0:T(8,128)(2,1)S(1)}, u32[]{:S(2)}, u32[]{:S(2)}) collective-permute-start(bf16[64,1024]{1,0:T(8,128)(2,1)S(1)} %get-tuple-element.13), channel_id=1, source_target_pairs={{0,4},{4,0},{8,12},{12,8},{1,5},{5,1},{9,13},{13,9},{2,6},{6,2},{1... | collective-permute-start | bytes 393224 | tf_op jit(solution)/shard_map/ppermute | solution.py:52
  61.8 1.6 %collective-permute-start.12 = (bf16[128,1024]{1,0:T(8,128)(2,1)S(1)}, bf16[128,1024]{1,0:T(8,128)(2,1)S(1)}, u32[]{:S(2)}, u32[]{:S(2)}) collective-permute-start(bf16[128,1024]{1,0:T(8,128)(2,1)S(1)} %add_convert_fusion), channel_id=1, source_target_pairs={{0,1},{1,0},{2,3},{3,2},{4,5},{5,4},{6,7},{7,6},{8,9},{9,8},{10,11... | collective-permute-start | bytes 786440 | tf_op jit(solution)/shard_map/ppermute | solution.py:52

commit v2 on v1

--- a/solution.py
+++ b/solution.py
@@ -1,8 +1,11 @@
+import functools
 import math
 
 import jax
 import jax.numpy as jnp
 from jax import lax
+from jax.experimental import pallas as pl
+from jax.experimental.pallas import tpu as pltpu
 from jax.sharding import PartitionSpec as P
 
 HEAD_SIZE = 128
@@ -10,9 +13,413 @@
 ADAPTER_SCALE = 2.0
 BF = jnp.bfloat16
 F32 = jnp.float32
+VMEM = pl.BlockSpec(memory_space=pltpu.VMEM)
+SMEM = pl.BlockSpec(memory_space=pltpu.SMEM)
+ANY = pl.BlockSpec(memory_space=pl.ANY)
+
+
+def attend_kernel(
+    chunk, length_ref, q_hbm, k_hbm, v_hbm, nk_hbm, nv_hbm, out_ref, q_ref, k_ref, v_ref, nk_ref, nv_ref, sems
+):
+    requests, positions, kv_width = k_ref.shape
+    heads = q_ref.shape[1] // HEAD_SIZE
+    kv_heads = kv_width // HEAD_SIZE
+    group = heads // kv_heads
+    factor = 1.0 / math.sqrt(HEAD_SIZE)
+    extended = positions + chunk
+
+    small = [
+        pltpu.make_async_copy(source, target, sems.at[2, i])
+        for i, (source, target) in enumerate(((q_hbm, q_ref), (nk_hbm, nk_ref), (nv_hbm, nv_ref)))
+    ]
+    parts = [pl.ds(first, chunk) for first in range(0, requests, chunk)]
+    keys = [
+        pltpu.make_async_copy(k_hbm.at[part], k_ref.at[part], sems.at[0, i])
+        for i, part in enumerate(parts)
+    ]
+    values = [
+        pltpu.make_async_copy(v_hbm.at[part], v_ref.at[part], sems.at[1, i])
+        for i, part in enumerate(parts)
+    ]
+    for copy in small:
+        copy.start()
+    for key, value in zip(keys, values):
+        key.start()
+        value.start()
+
+    row_group = lax.broadcasted_iota(jnp.int32, (heads, kv_width), 0) // group
+    lane_group = lax.broadcasted_iota(jnp.int32, (heads, kv_width), 1) // HEAD_SIZE
+    diagonal = row_group == lane_group
+    place = lax.broadcasted_iota(jnp.int32, (heads, extended), 1)
+    ones = jnp.ones((extended, HEAD_SIZE), BF)
+    for copy in small:
+        copy.wait()
+    for c, first in enumerate(range(0, requests, chunk)):
+        q = q_ref[first : first + chunk].reshape(chunk, heads, HEAD_SIZE)
+        new_keys = nk_ref[first : first + chunk]
+        new_values = nv_ref[first : first + chunk]
+        keys[c].wait()
+        scores = []
+        for i in range(chunk):
+            r = first + i
+            wide = jnp.where(
+                diagonal, jnp.concatenate([q[i]] * kv_heads, axis=1), jnp.zeros((), BF)
+            )
+            score = lax.dot_general(
+                wide,
+                jnp.concatenate([k_ref[r], new_keys], axis=0),
+                (((1,), (1,)), ((), ())),
+                preferred_element_type=F32,
+            )
+            valid = (place < length_ref[r]) | (place == positions + i)
+            scores.append(jnp.where(valid, score * factor, -jnp.inf))
+        scores = jnp.stack(scores).reshape(chunk * heads, extended)
+        powers = jnp.exp(scores - jnp.max(scores, axis=1, keepdims=True)).astype(BF)
+        inverse = 1.0 / jnp.dot(powers, ones, preferred_element_type=F32)
+        values[c].wait()
+        outs = []
+        for i in range(chunk):
+            rows = slice(i * heads, (i + 1) * heads)
+            blend = jnp.dot(
+                powers[rows],
+                jnp.concatenate([v_ref[first + i], new_values], axis=0),
+                preferred_element_type=F32,
+            )
+            blend = jnp.concatenate(
+                [
+                    blend[g * group : (g + 1) * group, g * HEAD_SIZE : (g + 1) * HEAD_SIZE]
+                    for g in range(kv_heads)
+                ],
+                axis=0,
+            )
+            outs.append((blend * inverse[rows]).astype(BF))
+        out_ref[first : first + chunk] = jnp.stack(outs).reshape(chunk, heads * HEAD_SIZE)
 
 
 def attend(queries, cache_keys, cached_value_rows, new_keys, fresh_value_rows, lengths):
+    requests = queries.shape[0]
+    chunk = 16 if requests % 16 == 0 else requests
+    moved = (queries, cache_keys, cached_value_rows, new_keys, fresh_value_rows)
+    return pl.pallas_call(
+        functools.partial(attend_kernel, chunk),
+        out_shape=jax.ShapeDtypeStruct(queries.shape, BF),
+        in_specs=[SMEM] + [ANY] * 5,
+        out_specs=VMEM,
+        scratch_shapes=[pltpu.VMEM(x.shape, BF) for x in moved]
+        + [pltpu.SemaphoreType.DMA((3, max(3, requests // chunk)))],
+        compiler_params=pltpu.CompilerParams(vmem_limit_bytes=60 << 20),
+        cost_estimate=pl.CostEstimate(
+            flops=8 * queries.size * cache_keys.shape[1],
+            bytes_accessed=4 * cache_keys.size,
+            transcendentals=queries.size,
+        ),
+        name="attend",
+    )(lengths, *moved)
+
+
+def split_kernel(up_hbm, low_ref, high_ref, sems):
+    half = low_ref.shape[3]
+    low = lax.rem(lax.axis_index("tensor"), 2)
+    copies = []
+    for b in range(low_ref.shape[0]):
+        for i, (ref, part) in enumerate(((low_ref, low), (high_ref, 1 - low))):
+            start = pl.multiple_of((2 * b + part) * half, half)
+            copies.append(
+                pltpu.make_async_copy(up_hbm.at[:, :, pl.ds(start, half)], ref.at[b], sems.at[b, i])
+            )
+    for copy in copies:
+        copy.start()
+    for copy in copies:
+        copy.wait()
+
+
+def blockwise(position, count, size, index):
+    moved = jnp.zeros_like(position)
+    for k in range(count):
+        inside = (position >= k * size) & (position < (k + 1) * size)
+        moved = jnp.where(inside, position + ((index ^ k) - k) * size, moved)
+    return moved
+
+
+def ids_kernel(n_adapter, n_tensor, ids_ref, slots_ref, here_ref, select_ref, place_ref, order_ref):
+    tokens, per_owner = here_ref.shape
+    owned = select_ref.shape[0]
+    rank = order_ref.shape[0]
+    a = lax.axis_index("adapter")
+    t = lax.axis_index("tensor")
+    down = lax.broadcasted_iota(jnp.int32, (tokens, tokens), 0)
+    across = lax.broadcasted_iota(jnp.int32, (tokens, tokens), 1)
+    ids_row = ids_ref[...].astype(F32)
+    ids_column = jnp.sum(jnp.where(down == across, ids_row, 0.0), axis=1, keepdims=True)
+    same = ids_row == ids_column
+
+    def stored(ids):
+        return sum(
+            jnp.where(ids == j, slots_ref[j].astype(F32), 0.0) for j in range(slots_ref.shape[0])
+        )
+
+    earlier = jnp.where(same & (across < down), 1.0, 0.0)
+    stored_column = stored(ids_column)
+    key_column = stored_column * SLOTS + jnp.sum(earlier, axis=1, keepdims=True)
+    earlier = jnp.where(same & (down < across), 1.0, 0.0)
+    key_row = stored(ids_row) * SLOTS + jnp.sum(earlier, axis=0, keepdims=True)
+    key_column, key_row = key_column.astype(jnp.int32), key_row.astype(jnp.int32)
+    adapter = lax.broadcasted_iota(jnp.int32, here_ref.shape, 1) + a * per_owner
+    here_ref[...] = jnp.where(adapter == stored_column.astype(jnp.int32), 1.0, 0.0)
+    slot = lax.broadcasted_iota(jnp.int32, select_ref.shape, 0) + a * owned
+    select_ref[...] = jnp.where(slot == key_row, 1.0, 0.0).astype(BF)
+    slot = lax.broadcasted_iota(jnp.int32, place_ref.shape, 1)
+    slot = blockwise(slot, n_adapter, owned, a)
+    place_ref[...] = jnp.where(slot == key_column, 1.0, 0.0).astype(BF)
+    source = lax.broadcasted_iota(jnp.int32, order_ref.shape, 1)
+    source = blockwise(source, n_tensor, rank // n_tensor, t)
+    target = lax.broadcasted_iota(jnp.int32, order_ref.shape, 0)
+    order_ref[...] = jnp.where(source == target, 1.0, 0.0).astype(BF)
+
+
+def block_rows(k, requests):
+    return pl.ds(pl.multiple_of((lax.axis_index("adapter") ^ k) * requests, requests), requests)
+
+
+def shrink_kernel(*refs):
+    *blocks, mask_ref, maps_ref, out_ref, total_ref = refs
+    requests = blocks[0].shape[0]
+    x = jnp.concatenate([b[...] for b in blocks], axis=0)
+    mask = jnp.concatenate(
+        [mask_ref[block_rows(k, requests), :] for k in range(len(blocks))], axis=0
+    )
+    total = None
+    for j in range(maps_ref.shape[0]):
+        part = lax.dot_general(x, maps_ref[j], (((1,), (1,)), ((), ())), preferred_element_type=F32)
+        part = jnp.where(mask[:, j : j + 1] > 0, part, 0.0)
+        total = part if total is None else total + part
+    for k in range(len(blocks)):
+        total_ref[block_rows(k, requests), :] = total[k * requests : (k + 1) * requests]
+    middle = total.shape[0] // 2
+    out_ref[...] = jnp.concatenate([total_ref[:middle], total_ref[middle:]], axis=1).astype(BF)
+
+
+def load_kernel(*refs):
+    *pairs, sems = refs
+    count = len(pairs) // 2
+    copies = [
+        pltpu.make_async_copy(source, target, sems.at[i])
+        for i, (source, target) in enumerate(zip(pairs[:count], pairs[count:]))
+    ]
+    for copy in copies:
+        copy.start()
+    for copy in copies:
+        copy.wait()
+
+
+def project_kernel(other, *refs):
+    *blocks, weight_ref, out_ref = refs
+    half = out_ref.shape[1]
+    tile = 256 if half % 256 == 0 else 128
+    side = lax.rem(lax.axis_index("tensor") + other, 2)
+    x = jnp.concatenate([b[...] for b in blocks], axis=0)
+    for i in range(half // tile):
+        start = pl.multiple_of(side * half + i * tile, tile)
+        part = jnp.dot(x, weight_ref[:, pl.ds(start, tile)], preferred_element_type=F32)
+        out_ref[:, i * tile : (i + 1) * tile] = part.astype(out_ref.dtype)
+
+
+def join_kernel(keep_ref, came_ref, out_ref):
+    out_ref[...] = (keep_ref[...] + came_ref[...].astype(F32)).astype(BF)
+
+
+def terms_kernel(n_adapter, n_tensor, *refs):
+    parts = refs[:n_tensor]
+    select_ref, order_ref = refs[n_tensor : n_tensor + 2]
+    maps = refs[n_tensor + 2 : -n_adapter]
+    outs = refs[-n_adapter:]
+    per_owner = maps[0].shape[1]
+    a = lax.axis_index("adapter")
+    sums = [p[...].astype(F32) for p in parts]
+    while len(sums) > 1:
+        sums = [x + y for x, y in zip(sums[::2], sums[1::2])]
+    rank = sums[0].shape[1] // 2
+    shrunk = jnp.concatenate([sums[0][:, :rank], sums[0][:, rank:]], axis=0).astype(BF)
+    held = jnp.dot(select_ref[...], shrunk, preferred_element_type=F32)
+    held = jnp.dot(held.astype(BF), order_ref[...], preferred_element_type=F32)
+    slot_of = lax.broadcasted_iota(jnp.int32, held.shape, 0) // SLOTS
+    wide = jnp.concatenate(
+        [jnp.where(slot_of == j, held, 0.0) for j in range(per_owner)], axis=1
+    ).astype(BF)
+    for k in range(n_adapter):
+        up = jnp.concatenate([m[a ^ k, j] for j in range(per_owner) for m in maps], axis=0)
+        outs[k][...] = jnp.dot(wide, up, preferred_element_type=F32).astype(BF)
+
+
+def finish_kernel(requests, place_ref, *refs):
+    *base, out_ref = refs
+    base, pieces = base[:2], base[2:]
+    blocks = range(out_ref.shape[0] // requests)
+    received = jnp.concatenate([p[...] for p in pieces], axis=0)
+    place = jnp.concatenate([place_ref[block_rows(k, requests), :] for k in blocks], axis=0)
+    delta = jnp.dot(place, received, preferred_element_type=F32)
+    total = base[0][...].astype(F32) + base[1][...].astype(F32)
+    total = (total + ADAPTER_SCALE * delta).astype(BF)
+    for k in blocks:
+        out_ref[block_rows(k, requests), :] = total[k * requests : (k + 1) * requests]
+
+
+def make_shards(n_adapter, n_tensor):
+    def swap(x, axis, n, k):
+        return lax.ppermute(x, axis, [(i, i ^ k) for i in range(n)])
+
+    def shards(
+        queries,
+        cache_keys,
+        cached_value_rows,
+        new_keys,
+        fresh_value_rows,
+        lengths,
+        adapter_ids,
+        adapter_slots,
+        out_weight,
+        shrink_weight,
+        expand_weight,
+    ):
+        low = lax.axis_index("tensor") % 2
+        per_owner, rank_part, width = expand_weight.shape
+        rank = shrink_weight.shape[2]
+        columns = out_weight.shape[1]
+        half = columns // 2
+        requests = queries.shape[0]
+        tokens = adapter_ids.shape[0]
+        owned = per_owner * SLOTS
+
+        attended = attend(
+            queries, cache_keys, cached_value_rows, new_keys, fresh_value_rows, lengths
+        )
+        blocks = [swap(attended, "adapter", n_adapter, k) for k in range(1, n_adapter)]
+
+        up_shape = jax.ShapeDtypeStruct((n_adapter, per_owner, rank_part, half), BF)
+        expand_weight, ids, _ = lax.optimization_barrier(
+            (expand_weight, adapter_ids.reshape(1, tokens), attended)
+        )
+        up_low, up_high = pl.pallas_call(
+            split_kernel,
+            out_shape=(up_shape, up_shape),
+            in_specs=[ANY],
+            out_specs=(VMEM, VMEM),
+            scratch_shapes=[pltpu.SemaphoreType.DMA((n_adapter, 2))],
+            compiler_params=pltpu.CompilerParams(vmem_limit_bytes=16 << 20),
+            name="split",
+        )(expand_weight)
+        maps = [up_low] + [
+            swap((up_low, up_high)[k % 2], "tensor", n_tensor, k) for k in range(1, n_tensor)
+        ]
+        ids, blocks[0] = lax.optimization_barrier((ids, blocks[0]))
+        out_weight, maps[1] = lax.optimization_barrier((out_weight, maps[1]))
+
+        loads = (attended, out_weight, jnp.swapaxes(shrink_weight, 1, 2))
+        here_block, weight, down = pl.pallas_call(
+            load_kernel,
+            out_shape=[jax.ShapeDtypeStruct(x.shape, BF) for x in loads],
+            in_specs=[ANY] * 3,
+            out_specs=[VMEM] * 3,
+            scratch_shapes=[pltpu.SemaphoreType.DMA((3,))],
+            compiler_params=pltpu.CompilerParams(vmem_limit_bytes=44 << 20),
+            cost_estimate=pl.CostEstimate(
+                flops=0, bytes_accessed=4 * out_weight.size, transcendentals=0
+            ),
+            name="load",
+        )(*loads)
+        blocks = [here_block] + blocks
+
+        here, select, place, reorder = pl.pallas_call(
+            functools.partial(ids_kernel, n_adapter, n_tensor),
+            out_shape=[
+                jax.ShapeDtypeStruct((tokens, per_owner), F32),
+                jax.ShapeDtypeStruct((owned, tokens), BF),
+                jax.ShapeDtypeStruct((tokens, n_adapter * owned), BF),
+                jax.ShapeDtypeStruct((rank, rank), BF),
+            ],
+            in_specs=[VMEM, SMEM],
+            out_specs=[VMEM] * 4,
+            compiler_params=pltpu.CompilerParams(vmem_limit_bytes=16 << 20),
+            name="ids",
+        )(ids, adapter_slots)
+
+        shrunk = pl.pallas_call(
+            shrink_kernel,
+            out_shape=jax.ShapeDtypeStruct((tokens // 2, 2 * rank), BF),
+            in_specs=[VMEM] * (n_adapter + 2),
+            out_specs=VMEM,
+            scratch_shapes=[pltpu.VMEM((tokens, rank), F32)],
+            compiler_params=pltpu.CompilerParams(vmem_limit_bytes=24 << 20),
+            name="shrink",
+        )(*blocks, here, down)
+        shrunk, *blocks = lax.optimization_barrier((shrunk, *blocks))
+        shrunk = [shrunk] + [swap(shrunk, "tensor", n_tensor, k) for k in range(1, n_tensor)]
+
+        blocks[0], *maps[2:] = lax.optimization_barrier((blocks[0], *maps[2:]))
+
+        def project(other, dtype):
+            return pl.pallas_call(
+                functools.partial(project_kernel, other),
+                out_shape=jax.ShapeDtypeStruct((tokens, half), dtype),
+                in_specs=[VMEM] * (n_adapter + 1),
+                out_specs=VMEM,
+                compiler_params=pltpu.CompilerParams(vmem_limit_bytes=24 << 20),
+                cost_estimate=pl.CostEstimate(
+                    flops=tokens * out_weight.size,
+                    bytes_accessed=2 * out_weight.size,
+                    transcendentals=0,
+                ),
+                name="project",
+            )(*blocks, weight)
+
+        came = swap(project(1, BF), "tensor", n_tensor, 1)
+        base = pl.pallas_call(
+            join_kernel,
+            out_shape=jax.ShapeDtypeStruct((tokens, half), BF),
+            in_specs=[VMEM] * 2,
+            out_specs=VMEM,
+            compiler_params=pltpu.CompilerParams(vmem_limit_bytes=16 << 20),
+            name="join",
+        )(project(0, F32), came)
+        base, *shrunk = lax.optimization_barrier((base, *shrunk))
+        step = 2
+        while step * 2 < n_tensor:
+            other = swap(base, "tensor", n_tensor, step)
+            base = (base.astype(F32) + other.astype(F32)).astype(BF)
+            step *= 2
+        base = [base, swap(base, "tensor", n_tensor, step)]
+
+        terms = pl.pallas_call(
+            functools.partial(terms_kernel, n_adapter, n_tensor),
+            out_shape=[jax.ShapeDtypeStruct((owned, half), BF)] * n_adapter,
+            in_specs=[VMEM] * (2 + n_tensor + len(maps)),
+            out_specs=[VMEM] * n_adapter,
+            compiler_params=pltpu.CompilerParams(vmem_limit_bytes=24 << 20),
+            name="terms",
+        )(*shrunk, select, reorder, *maps)
+        received = [terms[0]] + [
+            swap(terms[k], "adapter", n_adapter, k) for k in range(1, n_adapter)
+        ]
+
+        mine = pl.pallas_call(
+            functools.partial(finish_kernel, requests),
+            out_shape=jax.ShapeDtypeStruct((tokens, half), BF),
+            in_specs=[VMEM] * (3 + n_adapter),
+            out_specs=VMEM,
+            compiler_params=pltpu.CompilerParams(vmem_limit_bytes=24 << 20),
+            name="finish",
+        )(place, *base, *received)
+        other = swap(mine, "tensor", n_tensor, 1)
+        return jnp.where(
+            low == 0,
+            jnp.concatenate([mine, other], axis=1),
+            jnp.concatenate([other, mine], axis=1),
+        )
+
+    return shards
+
+
+def plain_attend(queries, cache_keys, cached_value_rows, new_keys, fresh_value_rows, lengths):
     requests = queries.shape[0]
     positions = cache_keys.shape[1]
     kv_local = cache_keys.shape[2] // HEAD_SIZE
@@ -47,7 +454,7 @@
     return blended.reshape(requests, heads_local * HEAD_SIZE).astype(BF)
 
 
-def make_shards(n_adapter, n_tensor):
+def make_plain_shards(n_adapter, n_tensor):
     def swap(x, axis, n, k):
         return lax.ppermute(x, axis, [(i, i ^ k) for i in range(n)])
 
@@ -86,7 +493,7 @@
             step *= 2
         up = up.reshape(per_owner * rank, n_adapter * half)
 
-        attended = attend(
+        attended = plain_attend(
             queries, cache_keys, cached_value_rows, new_keys, fresh_value_rows, lengths
         )
 
@@ -170,5 +577,10 @@
         P("adapter", "tensor", None),
     )
     out_specs = P("groups", "adapter")
-    shards = make_shards(mesh.shape["adapter"], mesh.shape["tensor"])
+    sizes = mesh.shape["adapter"], mesh.shape["tensor"]
+    fast, plain = make_shards(*sizes), make_plain_shards(*sizes)
+
+    def shards(*arrays):
+        return (plain if arrays[8].shape[1] % 256 else fast)(*arrays)
+
     return jax.shard_map(shards, mesh=mesh, in_specs=in_specs, out_specs=out_specs, check_vma=False)

time: 64.7 us -> 50.1 us (0.77)
  Pallas kernels: 0 us -> 11.5 us
  waiting for transfers between devices: 25.6 us -> 14.6 us
  matrix products: 8.38 us -> 0 us
  local copies, waits for them, and re-layouts: 9.96 us -> 4.29 us
  other arithmetic: 5.95 us -> 0.92 us
  starting transfers between devices: 13.9 us -> 18.3 us
    pallas_call x0 -> x10, Pallas kernels: none -> 11.5 us  [the longest x1 4.01 us: attend(): pl.pallas_call(functools.partial(attend_kernel, chunk), out_shape=jax.Sha...]
    ppermute x13 -> x15, waiting for transfers between devices: 25.6 us -> 14.6 us  [swap(): return lax.ppermute(x, axis, [(i, i ^ k) for i in range(n)])]
    dot_general x7 -> x0, matrix products: 8.08 us -> none  [the longest x1 4.63 us: shards(): base = jnp.dot(rows, out_weight, preferred_element_type=F32)]
    ppermute x13 -> x15, starting transfers between devices: 13.9 us -> 18.3 us  [swap(): return lax.ppermute(x, axis, [(i, i ^ k) for i in range(n)])]
    dynamic_update_slice x4 -> x0, local copies, waits for them, and re-layouts: 2.78 us -> none  [shards(): rows = lax.dynamic_update_slice(rows, block, ((a ^ k) * requests, 0))]
    unnamed x19 -> x10, local copies, waits for them, and re-layouts: 2.14 us -> 4.29 us
    dynamic_slice x4 -> x0, local copies, waits for them, and re-layouts: 1.73 us -> none  [the longest x2 1.4 us: shards(): up_keep = lax.dynamic_index_in_dim(up, low, 3, keepdims=False)]
    concatenate x2 -> x0, other arithmetic: 1.17 us -> none  [the longest x1 1.13 us: shards(): up = jnp.concatenate([up, swap(up, 'tensor', n_tensor, step)], axis=1)]
  transfers between devices with their start and end apart: 13 -> 15, of which waited for: 5 -> 6; matrix products, arithmetic and copies ran while one was open for 26% -> 0% of each run, Pallas kernels for 0% -> 13%
where the time goes in v2:
time: 50.1 us; the launch traced here: 49.8 us
  starting transfers between devices  18.3 us (37%)
  waiting for transfers between devices  14.6 us (29%)
  Pallas kernels  11.5 us (23%)
  local copies, waits for them, and re-layouts  4.29 us (9%)
  other arithmetic  0.92 us (2%)
    ppermute x15, starting transfers between devices, swap(): return lax.ppermute(x, axis, [(i, i ^ k) for i in range(n)])  18.3 us
    ppermute x15, waiting for transfers between devices, swap(): return lax.ppermute(x, axis, [(i, i ^ k) for i in range(n)])  14.6 us
    unnamed x10, local copies, waits for them, and re-layouts  4.29 us
    pallas_call x1, Pallas kernels, attend(): pl.pallas_call(functools.partial(attend_kernel, chunk), out_shape=jax.Sha...  4.01 us
    pallas_call x1, Pallas kernels, shards(): pl.pallas_call(load_kernel, out_shape=[jax.ShapeDtypeStruct(x.shape, BF)...  3.54 us
    pallas_call x2, Pallas kernels, project(): pl.pallas_call(functools.partial(project_kernel, other), out_shape=jax.Sh...  1.54 us
  transfers between devices with their start and end apart: 15, of which 6 were waited for; matrix products, arithmetic and copies ran while one was open for 0% of the time, Pallas kernels for 13%

profile of v2, /device:TPU:0, one launch (start us, length us, event | category | flops | bytes accessed | tf_op | source)
XLA Modules:
  0.0 49.8 jit_solution(11581631061589734216)
XLA Ops:
  0.0 4.0 %attend.1.refs_0_ = bf16[32,2048]{1,0:T(8,128)(2,1)} custom-call(s32[32]{0:T(128)} %length_ref.1, bf16[32,2048]{1,0:T(8,128)(2,1)} %q_hbm.1, bf16[32,64,256]{2,1,0:T(8,128)(2,1)} %k_hbm.1, bf16[32,64,256]{2,1,0:T(8,128)(2,1)} %v_hbm.1, bf16[32,256]{1,0:T(8,128)(2,1)} %nk_hbm.1, bf16[32,256]{1,0:T(8,128)(2,1)} %nv_hbm.1), custom_call_target="tpu_custom_call" | custom-call | flops 33554432 | bytes 2097152 | tf_op jit(solution)/shard_map/attend/pallas_call | solution.py:103
  4.0 1.0 %copy-done.2 = bf16[2,16,8192]{2,1,0:T(8,128)(2,1)S(1)} copy-done((bf16[2,16,8192]{2,1,0:T(8,128)(2,1)S(1)}, bf16[2,16,8192]{2,1,0:T(8,128)(2,1)}, u32[]{:S(2)}) %copy-start.2) | copy-done | bytes 524312
  5.1 0.2 split.1
  5.3 0.5 %collective-permute-start.1 = (bf16[4,2,16,1024]{3,2,1,0:T(8,128)(2,1)S(1)}, bf16[4,2,16,1024]{3,2,1,0:T(8,128)(2,1)S(1)}, u32[]{:S(2)}, u32[]{:S(2)}) collective-permute-start(bf16[4,2,16,1024]{3,2,1,0:T(8,128)(2,1)S(1)} %get-tuple-element.41), channel_id=1, source_target_pairs={{0,1},{1,0},{2,3},{3,2},{4,5},{5,4},{6,7},{7,6},{8,9},{9,8},{10,11... | collective-permute-start | bytes 786440 | tf_op jit(solution)/shard_map/ppermute | solution.py:269
  5.8 2.6 %collective-permute-start = (bf16[32,2048]{1,0:T(8,128)(2,1)}, bf16[32,2048]{1,0:T(8,128)(2,1)S(1)}, u32[]{:S(2)}, u32[]{:S(2)}) collective-permute-start(bf16[32,2048]{1,0:T(8,128)(2,1)} %attend.1.refs_0_), channel_id=1, source_target_pairs={{0,4},{4,0},{8,12},{12,8},{1,5},{5,1},{9,13},{13,9},{2,6},{6,2},{1... | collective-permute-start | bytes 393224 | tf_op jit(solution)/shard_map/ppermute | solution.py:269
  8.5 1.5 %collective-permute-start.4 = (bf16[4,2,16,1024]{3,2,1,0:T(8,128)(2,1)S(1)}, bf16[4,2,16,1024]{3,2,1,0:T(8,128)(2,1)S(1)}, u32[]{:S(2)}, u32[]{:S(2)}) collective-permute-start(bf16[4,2,16,1024]{3,2,1,0:T(8,128)(2,1)S(1)} %get-tuple-element.48.refs_6_), channel_id=1, source_target_pairs={{0,2},{1,3},{2,0},{3,1},{4,6},{5,7},{6,4},{7,5},{8,10},{9,11},{10,... | collective-permute-start | bytes 786440 | tf_op jit(solution)/shard_map/ppermute | solution.py:269
  10.0 2.6 %collective-permute-start.2 = (bf16[32,2048]{1,0:T(8,128)(2,1)}, bf16[32,2048]{1,0:T(8,128)(2,1)S(1)}, u32[]{:S(2)}, u32[]{:S(2)}) collective-permute-start(bf16[32,2048]{1,0:T(8,128)(2,1)} %attend.1.refs_0_), channel_id=1, source_target_pairs={{0,8},{4,12},{8,0},{12,4},{1,9},{5,13},{9,1},{13,5},{2,10},{6,14},... | collective-permute-start | bytes 393224 | tf_op jit(solution)/shard_map/ppermute | solution.py:269
  12.6 0.2 collective-permute-done.refs_1_
  12.8 3.8 %collective-permute-start.3 = (bf16[32,2048]{1,0:T(8,128)(2,1)}, bf16[32,2048]{1,0:T(8,128)(2,1)S(1)}, u32[]{:S(2)}, u32[]{:S(2)}) collective-permute-start(bf16[32,2048]{1,0:T(8,128)(2,1)} %attend.1.refs_0_), channel_id=1, source_target_pairs={{0,12},{4,8},{8,4},{12,0},{1,13},{5,9},{9,5},{13,1},{2,14},{6,10},... | collective-permute-start | bytes 393224 | tf_op jit(solution)/shard_map/ppermute | solution.py:269
  16.6 0.7 %copy-done.3 = s32[128]{0:T(128)S(1)} copy-done((s32[128]{0:T(128)S(1)}, s32[128]{0:T(128)}, u32[]{:S(2)}) %copy-start.3) | copy-done | bytes 536
  17.2 0.7 %copy-done.4 = s32[8]{0:T(128)S(1)} copy-done((s32[8]{0:T(128)S(1)}, s32[8]{0:T(128)}, u32[]{:S(2)}) %copy-start.4) | copy-done | bytes 56
  17.9 0.7 %ids.1 = (f32[128,2]{1,0:T(8,128)S(1)}, bf16[64,128]{1,0:T(8,128)(2,1)S(1)}, bf16[128,256]{1,0:T(8,128)(2,1)S(1)}, bf16[64,64]{1,0:T(8,128)(2,1)S(1)}) custom-call(s32[1,128]{1,0:T(1,128)S(1)} %bitcast.3, s32[8]{0:T(128)S(1)} %copy-done.4), custom_call_target="tpu_custom_call" | custom-call | tf_op jit(solution)/shard_map/ids/pallas_call | solution.py:332
  18.6 0.9 %copy-done = bf16[32,2048]{1,0:T(8,128)(2,1)S(1)} copy-done((bf16[32,2048]{1,0:T(8,128)(2,1)S(1)}, bf16[32,2048]{1,0:T(8,128)(2,1)}, u32[]{:S(2)}) %copy-start) | copy-done | bytes 131096
  19.5 1.0 %copy-done.1 = bf16[2,2048,64]{1,2,0:T(8,128)(2,1)S(1)} copy-done((bf16[2,2048,64]{1,2,0:T(8,128)(2,1)S(1)}, bf16[2,2048,64]{1,2,0:T(8,128)(2,1)}, u32[]{:S(2)}) %copy-start.1) | copy-done | bytes 524312
  20.6 3.5 %load.1 = (bf16[32,2048]{1,0:T(8,128)(2,1)S(1)}, bf16[2048,2048]{1,0:T(8,128)(2,1)S(1)}, bf16[2,64,2048]{2,1,0:T(8,128)(2,1)S(1)}) custom-call(bf16[32,2048]{1,0:T(8,128)(2,1)S(1)} %copy-done, bf16[2048,2048]{1,0:T(8,128)(2,1)} %refs_1_, bf16[2,64,2048]{2,1,0:T(8,128)(2,1)S(1)} %bitcast.2), custom_call_target="tpu_custom_call" | custom-call | bytes 16777216 | tf_op jit(solution)/shard_map/load/pallas_call | solution.py:318
  24.1 0.5 shrink.1.refs_0_
  24.6 0.8 %project.3 = bf16[128,1024]{1,0:T(8,128)(2,1)S(1)} custom-call(bf16[32,2048]{1,0:T(8,128)(2,1)S(1)} %get-tuple-element.49.refs_0_, bf16[32,2048]{1,0:T(8,128)(2,1)S(1)} %collective-permute-done.refs_1_, bf16[32,2048]{1,0:T(8,128)(2,1)S(1)} %collective-permute-done.2.refs_2_, bf16[32,2048]{1,0:T(8,128)(2,1)S(1)} %collective-permute-done.3.refs_3_, ...), custom_call_target="tpu_custom_call" | custom-call | flops 536870912 | bytes 8388608 | tf_op jit(solution)/shard_map/project/pallas_call | solution.py:361
  25.5 0.5 collective-permute-start.7
  26.0 1.5 %collective-permute-start.8 = (bf16[64,128]{1,0:T(8,128)(2,1)S(1)}, bf16[64,128]{1,0:T(8,128)(2,1)S(1)}, u32[]{:S(2)}, u32[]{:S(2)}) collective-permute-start(bf16[64,128]{1,0:T(8,128)(2,1)S(1)} %shrink.1.refs_0_), channel_id=1, source_target_pairs={{0,2},{1,3},{2,0},{3,1},{4,6},{5,7},{6,4},{7,5},{8,10},{9,11},{10,... | collective-permute-start | bytes 49160 | tf_op jit(solution)/shard_map/ppermute | solution.py:269
  27.5 0.8 %project.2.keep_ref = f32[128,1024]{1,0:T(8,128)S(1)} custom-call(bf16[32,2048]{1,0:T(8,128)(2,1)S(1)} %get-tuple-element.49.refs_0_, bf16[32,2048]{1,0:T(8,128)(2,1)S(1)} %collective-permute-done.refs_1_, bf16[32,2048]{1,0:T(8,128)(2,1)S(1)} %collective-permute-done.2.refs_2_, bf16[32,2048]{1,0:T(8,128)(2,1)S(1)} %collective-permute-done.3.refs_3_, ...), custom_call_target="tpu_custom_call" | custom-call | flops 536870912 | bytes 8388608 | tf_op jit(solution)/shard_map/project/pallas_call | solution.py:361
  28.3 1.4 %collective-permute-done.8.refs_2_ = bf16[64,128]{1,0:T(8,128)(2,1)S(1)} collective-permute-done((bf16[64,128]{1,0:T(8,128)(2,1)S(1)}, bf16[64,128]{1,0:T(8,128)(2,1)S(1)}, u32[]{:S(2)}, u32[]{:S(2)}) %collective-permute-start.8) | collective-permute-done | bytes 16416 | tf_op jit(solution)/shard_map/ppermute | solution.py:269
  29.7 1.1 %collective-permute-done.9.refs_3_ = bf16[64,128]{1,0:T(8,128)(2,1)S(1)} collective-permute-done((bf16[64,128]{1,0:T(8,128)(2,1)S(1)}, bf16[64,128]{1,0:T(8,128)(2,1)S(1)}, u32[]{:S(2)}, u32[]{:S(2)}) %collective-permute-start.9) | collective-permute-done | bytes 16416 | tf_op jit(solution)/shard_map/ppermute | solution.py:269
  30.8 0.6 %collective-permute-start.10 = (bf16[128,1024]{1,0:T(8,128)(2,1)S(1)}, bf16[128,1024]{1,0:T(8,128)(2,1)S(1)}, u32[]{:S(2)}, u32[]{:S(2)}) collective-permute-start(bf16[128,1024]{1,0:T(8,128)(2,1)S(1)} %join.1.refs_0_), channel_id=1, source_target_pairs={{0,2},{1,3},{2,0},{3,1},{4,6},{5,7},{6,4},{7,5},{8,10},{9,11},{10,... | collective-permute-start | bytes 786440 | tf_op jit(solution)/shard_map/ppermute | solution.py:269
  31.4 0.7 %terms.1 = (bf16[64,1024]{1,0:T(8,128)(2,1)S(1)}, bf16[64,1024]{1,0:T(8,128)(2,1)S(1)}, bf16[64,1024]{1,0:T(8,128)(2,1)S(1)}, bf16[64,1024]{1,0:T(8,128)(2,1)S(1)}) custom-call(bf16[64,128]{1,0:T(8,128)(2,1)S(1)} %shrink.1.refs_0_, bf16[64,128]{1,0:T(8,128)(2,1)S(1)} %collective-permute-done.7.refs_1_, bf16[64,128]{1,0:T(8,128)(2,1)S(1)} %collective-permute-done.8.refs_2_, ...), custom_call_target="tpu_custom_call" | custom-call | tf_op jit(solution)/shard_map/terms/pallas_call | solution.py:392
  32.1 2.1 %collective-permute-start.11 = (bf16[64,1024]{1,0:T(8,128)(2,1)S(1)}, bf16[64,1024]{1,0:T(8,128)(2,1)S(1)}, u32[]{:S(2)}, u32[]{:S(2)}) collective-permute-start(bf16[64,1024]{1,0:T(8,128)(2,1)S(1)} %get-tuple-element.66), channel_id=1, source_target_pairs={{0,4},{4,0},{8,12},{12,8},{1,5},{5,1},{9,13},{13,9},{2,6},{6,2},{1... | collective-permute-start | bytes 393224 | tf_op jit(solution)/shard_map/ppermute | solution.py:269
  34.1 1.1 %collective-permute-start.12 = (bf16[64,1024]{1,0:T(8,128)(2,1)S(1)}, bf16[64,1024]{1,0:T(8,128)(2,1)S(1)}, u32[]{:S(2)}, u32[]{:S(2)}) collective-permute-start(bf16[64,1024]{1,0:T(8,128)(2,1)S(1)} %get-tuple-element.67), channel_id=1, source_target_pairs={{0,8},{4,12},{8,0},{12,4},{1,9},{5,13},{9,1},{13,5},{2,10},{6,14},... | collective-permute-start | bytes 393224 | tf_op jit(solution)/shard_map/ppermute | solution.py:269
  35.2 1.4 %collective-permute-start.13 = (bf16[64,1024]{1,0:T(8,128)(2,1)S(1)}, bf16[64,1024]{1,0:T(8,128)(2,1)S(1)}, u32[]{:S(2)}, u32[]{:S(2)}) collective-permute-start(bf16[64,1024]{1,0:T(8,128)(2,1)S(1)} %get-tuple-element.68), channel_id=1, source_target_pairs={{0,12},{4,8},{8,4},{12,0},{1,13},{5,9},{9,5},{13,1},{2,14},{6,10},... | collective-permute-start | bytes 393224 | tf_op jit(solution)/shard_map/ppermute | solution.py:269
  36.6 2.6 %collective-permute-done.11.refs_3_ = bf16[64,1024]{1,0:T(8,128)(2,1)S(1)} collective-permute-done((bf16[64,1024]{1,0:T(8,128)(2,1)S(1)}, bf16[64,1024]{1,0:T(8,128)(2,1)S(1)}, u32[]{:S(2)}, u32[]{:S(2)}) %collective-permute-start.11) | collective-permute-done | bytes 131104 | tf_op jit(solution)/shard_map/ppermute | solution.py:269
  39.1 7.9 %collective-permute-done.12.refs_4_ = bf16[64,1024]{1,0:T(8,128)(2,1)S(1)} collective-permute-done((bf16[64,1024]{1,0:T(8,128)(2,1)S(1)}, bf16[64,1024]{1,0:T(8,128)(2,1)S(1)}, u32[]{:S(2)}, u32[]{:S(2)}) %collective-permute-start.12) | collective-permute-done | bytes 131104 | tf_op jit(solution)/shard_map/ppermute | solution.py:269
  47.0 0.2 finish.1
  47.4 1.5 %collective-permute-done.14 = bf16[128,1024]{1,0:T(8,128)(2,1)S(1)} collective-permute-done((bf16[128,1024]{1,0:T(8,128)(2,1)S(1)}, bf16[128,1024]{1,0:T(8,128)(2,1)S(1)}, u32[]{:S(2)}, u32[]{:S(2)}) %collective-permute-start.14) | collective-permute-done | bytes 262176 | tf_op jit(solution)/shard_map/ppermute | solution.py:269
  48.9 0.9 %maximum_select_fusion = bf16[128,2048]{1,0:T(8,128)(2,1)} fusion(bf16[128,1024]{1,0:T(8,128)(2,1)S(1)} %collective-permute-done.14, bf16[128,1024]{1,0:T(8,128)(2,1)S(1)} %finish.1, pred[]{:T(512)S(6)} %eq.5), kind=kLoop, calls=%fused_computation | loop fusion | flops 2359296 | bytes 1048577 | tf_op jit(solution)/shard_map/jit(_where)/select_n | solution.py:413
  (19 shorter events, 0.3 us)
Async XLA Ops:
  4.0 1.0 %copy-start.2 = (bf16[2,16,8192]{2,1,0:T(8,128)(2,1)S(1)}, bf16[2,16,8192]{2,1,0:T(8,128)(2,1)}, u32[]{:S(2)}) copy-start(bf16[2,16,8192]{2,1,0:T(8,128)(2,1)} %up_hbm) | copy-start | bytes 1572868
  5.3 13.3 %collective-permute-start.1 = (bf16[4,2,16,1024]{3,2,1,0:T(8,128)(2,1)S(1)}, bf16[4,2,16,1024]{3,2,1,0:T(8,128)(2,1)S(1)}, u32[]{:S(2)}, u32[]{:S(2)}) collective-permute-start(bf16[4,2,16,1024]{3,2,1,0:T(8,128)(2,1)S(1)} %get-tuple-element.41), channel_id=1, source_target_pairs={{0,1},{1,0},{2,3},{3,2},{4,5},{5,4},{6,7},{7,6},{8,9},{9,8},{10,11... | collective-permute-start | bytes 786440 | tf_op jit(solution)/shard_map/ppermute | solution.py:269
  5.8 6.9 %collective-permute-start = (bf16[32,2048]{1,0:T(8,128)(2,1)}, bf16[32,2048]{1,0:T(8,128)(2,1)S(1)}, u32[]{:S(2)}, u32[]{:S(2)}) collective-permute-start(bf16[32,2048]{1,0:T(8,128)(2,1)} %attend.1.refs_0_), channel_id=1, source_target_pairs={{0,4},{4,0},{8,12},{12,8},{1,5},{5,1},{9,13},{13,9},{2,6},{6,2},{1... | collective-permute-start | bytes 393224 | tf_op jit(solution)/shard_map/ppermute | solution.py:269
  8.5 16.1 %collective-permute-start.4 = (bf16[4,2,16,1024]{3,2,1,0:T(8,128)(2,1)S(1)}, bf16[4,2,16,1024]{3,2,1,0:T(8,128)(2,1)S(1)}, u32[]{:S(2)}, u32[]{:S(2)}) collective-permute-start(bf16[4,2,16,1024]{3,2,1,0:T(8,128)(2,1)S(1)} %get-tuple-element.48.refs_6_), channel_id=1, source_target_pairs={{0,2},{1,3},{2,0},{3,1},{4,6},{5,7},{6,4},{7,5},{8,10},{9,11},{10,... | collective-permute-start | bytes 786440 | tf_op jit(solution)/shard_map/ppermute | solution.py:269
  10.0 14.7 %collective-permute-start.5 = (bf16[4,2,16,1024]{3,2,1,0:T(8,128)(2,1)S(1)}, bf16[4,2,16,1024]{3,2,1,0:T(8,128)(2,1)S(1)}, u32[]{:S(2)}, u32[]{:S(2)}) collective-permute-start(bf16[4,2,16,1024]{3,2,1,0:T(8,128)(2,1)S(1)} %get-tuple-element.41), channel_id=1, source_target_pairs={{0,3},{1,2},{2,1},{3,0},{4,7},{5,6},{6,5},{7,4},{8,11},{9,10},{10,... | collective-permute-start | bytes 786440 | tf_op jit(solution)/shard_map/ppermute | solution.py:269
  10.0 14.1 %collective-permute-start.2 = (bf16[32,2048]{1,0:T(8,128)(2,1)}, bf16[32,2048]{1,0:T(8,128)(2,1)S(1)}, u32[]{:S(2)}, u32[]{:S(2)}) collective-permute-start(bf16[32,2048]{1,0:T(8,128)(2,1)} %attend.1.refs_0_), channel_id=1, source_target_pairs={{0,8},{4,12},{8,0},{12,4},{1,9},{5,13},{9,1},{13,5},{2,10},{6,14},... | collective-permute-start | bytes 393224 | tf_op jit(solution)/shard_map/ppermute | solution.py:269
  12.8 11.3 %collective-permute-start.3 = (bf16[32,2048]{1,0:T(8,128)(2,1)}, bf16[32,2048]{1,0:T(8,128)(2,1)S(1)}, u32[]{:S(2)}, u32[]{:S(2)}) collective-permute-start(bf16[32,2048]{1,0:T(8,128)(2,1)} %attend.1.refs_0_), channel_id=1, source_target_pairs={{0,12},{4,8},{8,4},{12,0},{1,13},{5,9},{9,5},{13,1},{2,14},{6,10},... | collective-permute-start | bytes 393224 | tf_op jit(solution)/shard_map/ppermute | solution.py:269
  16.6 0.7 %copy-start.3 = (s32[128]{0:T(128)S(1)}, s32[128]{0:T(128)}, u32[]{:S(2)}) copy-start(s32[128]{0:T(128)} %param.17) | copy-start | bytes 1540
  17.2 0.7 %copy-start.4 = (s32[8]{0:T(128)S(1)}, s32[8]{0:T(128)}, u32[]{:S(2)}) copy-start(s32[8]{0:T(128)} %slots_ref.1) | copy-start | bytes 100
  18.6 0.9 %copy-start = (bf16[32,2048]{1,0:T(8,128)(2,1)S(1)}, bf16[32,2048]{1,0:T(8,128)(2,1)}, u32[]{:S(2)}) copy-start(bf16[32,2048]{1,0:T(8,128)(2,1)} %attend.1.refs_0_) | copy-start | bytes 393220
  19.5 1.0 %copy-start.1 = (bf16[2,2048,64]{1,2,0:T(8,128)(2,1)S(1)}, bf16[2,2048,64]{1,2,0:T(8,128)(2,1)}, u32[]{:S(2)}) copy-start(bf16[2,2048,64]{1,2,0:T(8,128)(2,1)} %param.20) | copy-start | bytes 1572868
  25.4 2.8 %collective-permute-start.6 = (bf16[128,1024]{1,0:T(8,128)(2,1)S(1)}, bf16[128,1024]{1,0:T(8,128)(2,1)S(1)}, u32[]{:S(2)}, u32[]{:S(2)}) collective-permute-start(bf16[128,1024]{1,0:T(8,128)(2,1)S(1)} %project.3), channel_id=1, source_target_pairs={{0,1},{1,0},{2,3},{3,2},{4,5},{5,4},{6,7},{7,6},{8,9},{9,8},{10,11... | collective-permute-start | bytes 786440 | tf_op jit(solution)/shard_map/ppermute | solution.py:269
  25.5 2.8 %collective-permute-start.7 = (bf16[64,128]{1,0:T(8,128)(2,1)S(1)}, bf16[64,128]{1,0:T(8,128)(2,1)S(1)}, u32[]{:S(2)}, u32[]{:S(2)}) collective-permute-start(bf16[64,128]{1,0:T(8,128)(2,1)S(1)} %shrink.1.refs_0_), channel_id=1, source_target_pairs={{0,1},{1,0},{2,3},{3,2},{4,5},{5,4},{6,7},{7,6},{8,9},{9,8},{10,11... | collective-permute-start | bytes 49160 | tf_op jit(solution)/shard_map/ppermute | solution.py:269
  26.0 3.7 %collective-permute-start.8 = (bf16[64,128]{1,0:T(8,128)(2,1)S(1)}, bf16[64,128]{1,0:T(8,128)(2,1)S(1)}, u32[]{:S(2)}, u32[]{:S(2)}) collective-permute-start(bf16[64,128]{1,0:T(8,128)(2,1)S(1)} %shrink.1.refs_0_), channel_id=1, source_target_pairs={{0,2},{1,3},{2,0},{3,1},{4,6},{5,7},{6,4},{7,5},{8,10},{9,11},{10,... | collective-permute-start | bytes 49160 | tf_op jit(solution)/shard_map/ppermute | solution.py:269
  27.5 3.3 %collective-permute-start.9 = (bf16[64,128]{1,0:T(8,128)(2,1)S(1)}, bf16[64,128]{1,0:T(8,128)(2,1)S(1)}, u32[]{:S(2)}, u32[]{:S(2)}) collective-permute-start(bf16[64,128]{1,0:T(8,128)(2,1)S(1)} %shrink.1.refs_0_), channel_id=1, source_target_pairs={{0,3},{1,2},{2,1},{3,0},{4,7},{5,6},{6,5},{7,4},{8,11},{9,10},{10,... | collective-permute-start | bytes 49160 | tf_op jit(solution)/shard_map/ppermute | solution.py:269
  30.8 16.2 %collective-permute-start.10 = (bf16[128,1024]{1,0:T(8,128)(2,1)S(1)}, bf16[128,1024]{1,0:T(8,128)(2,1)S(1)}, u32[]{:S(2)}, u32[]{:S(2)}) collective-permute-start(bf16[128,1024]{1,0:T(8,128)(2,1)S(1)} %join.1.refs_0_), channel_id=1, source_target_pairs={{0,2},{1,3},{2,0},{3,1},{4,6},{5,7},{6,4},{7,5},{8,10},{9,11},{10,... | collective-permute-start | bytes 786440 | tf_op jit(solution)/shard_map/ppermute | solution.py:269
  32.1 7.1 %collective-permute-start.11 = (bf16[64,1024]{1,0:T(8,128)(2,1)S(1)}, bf16[64,1024]{1,0:T(8,128)(2,1)S(1)}, u32[]{:S(2)}, u32[]{:S(2)}) collective-permute-start(bf16[64,1024]{1,0:T(8,128)(2,1)S(1)} %get-tuple-element.66), channel_id=1, source_target_pairs={{0,4},{4,0},{8,12},{12,8},{1,5},{5,1},{9,13},{13,9},{2,6},{6,2},{1... | collective-permute-start | bytes 393224 | tf_op jit(solution)/shard_map/ppermute | solution.py:269
  34.1 12.9 %collective-permute-start.12 = (bf16[64,1024]{1,0:T(8,128)(2,1)S(1)}, bf16[64,1024]{1,0:T(8,128)(2,1)S(1)}, u32[]{:S(2)}, u32[]{:S(2)}) collective-permute-start(bf16[64,1024]{1,0:T(8,128)(2,1)S(1)} %get-tuple-element.67), channel_id=1, source_target_pairs={{0,8},{4,12},{8,0},{12,4},{1,9},{5,13},{9,1},{13,5},{2,10},{6,14},... | collective-permute-start | bytes 393224 | tf_op jit(solution)/shard_map/ppermute | solution.py:269
  35.2 11.8 %collective-permute-start.13 = (bf16[64,1024]{1,0:T(8,128)(2,1)S(1)}, bf16[64,1024]{1,0:T(8,128)(2,1)S(1)}, u32[]{:S(2)}, u32[]{:S(2)}) collective-permute-start(bf16[64,1024]{1,0:T(8,128)(2,1)S(1)} %get-tuple-element.68), channel_id=1, source_target_pairs={{0,12},{4,8},{8,4},{12,0},{1,13},{5,9},{9,5},{13,1},{2,14},{6,10},... | collective-permute-start | bytes 393224 | tf_op jit(solution)/shard_map/ppermute | solution.py:269
  47.3 1.6 %collective-permute-start.14 = (bf16[128,1024]{1,0:T(8,128)(2,1)S(1)}, bf16[128,1024]{1,0:T(8,128)(2,1)S(1)}, u32[]{:S(2)}, u32[]{:S(2)}) collective-permute-start(bf16[128,1024]{1,0:T(8,128)(2,1)S(1)} %finish.1), channel_id=1, source_target_pairs={{0,1},{1,0},{2,3},{3,2},{4,5},{5,4},{6,7},{7,6},{8,9},{9,8},{10,11... | collective-permute-start | bytes 786440 | tf_op jit(solution)/shard_map/ppermute | solution.py:269

commit v3 on v2

--- a/solution.py
+++ b/solution.py
@@ -19,8 +19,39 @@
 
 
 def attend_kernel(
-    chunk, length_ref, q_hbm, k_hbm, v_hbm, nk_hbm, nv_hbm, out_ref, q_ref, k_ref, v_ref, nk_ref, nv_ref, sems
+    chunk,
+    length_ref,
+    q_hbm,
+    k_hbm,
+    v_hbm,
+    nk_hbm,
+    nv_hbm,
+    up_hbm,
+    out_ref,
+    low_hbm,
+    high_hbm,
+    q_ref,
+    k_ref,
+    v_ref,
+    nk_ref,
+    nv_ref,
+    low_ref,
+    high_ref,
+    sems,
+    cut_sems,
+    put_sems,
 ):
+    half = low_ref.shape[3]
+    low = lax.rem(lax.axis_index("tensor"), 2)
+    cuts = []
+    for b in range(low_ref.shape[0]):
+        for i, (ref, side) in enumerate(((low_ref, low), (high_ref, 1 - low))):
+            start = pl.multiple_of((2 * b + side) * half, half)
+            cuts.append(
+                pltpu.make_async_copy(
+                    up_hbm.at[:, :, pl.ds(start, half)], ref.at[b], cut_sems.at[b, i]
+                )
+            )
     requests, positions, kv_width = k_ref.shape
     heads = q_ref.shape[1] // HEAD_SIZE
     kv_heads = kv_width // HEAD_SIZE
@@ -46,6 +77,8 @@
     for key, value in zip(keys, values):
         key.start()
         value.start()
+    for copy in cuts:
+        copy.start()
 
     row_group = lax.broadcasted_iota(jnp.int32, (heads, kv_width), 0) // group
     lane_group = lax.broadcasted_iota(jnp.int32, (heads, kv_width), 1) // HEAD_SIZE
@@ -54,7 +87,16 @@
     ones = jnp.ones((extended, HEAD_SIZE), BF)
     for copy in small:
         copy.wait()
+    puts = [
+        pltpu.make_async_copy(low_ref, low_hbm, put_sems.at[0]),
+        pltpu.make_async_copy(high_ref, high_hbm, put_sems.at[1]),
+    ]
     for c, first in enumerate(range(0, requests, chunk)):
+        if first + chunk >= requests:
+            for copy in cuts:
+                copy.wait()
+            for copy in puts:
+                copy.start()
         q = q_ref[first : first + chunk].reshape(chunk, heads, HEAD_SIZE)
         new_keys = nk_ref[first : first + chunk]
         new_values = nv_ref[first : first + chunk]
@@ -94,19 +136,29 @@
             )
             outs.append((blend * inverse[rows]).astype(BF))
         out_ref[first : first + chunk] = jnp.stack(outs).reshape(chunk, heads * HEAD_SIZE)
-
-
-def attend(queries, cache_keys, cached_value_rows, new_keys, fresh_value_rows, lengths):
+    for copy in puts:
+        copy.wait()
+
+
+def attend(
+    queries, cache_keys, cached_value_rows, new_keys, fresh_value_rows, lengths, up, blocks
+):
     requests = queries.shape[0]
     chunk = 16 if requests % 16 == 0 else requests
+    per_owner, rank_part, width = up.shape
+    part = (blocks, per_owner, rank_part, width // (2 * blocks))
     moved = (queries, cache_keys, cached_value_rows, new_keys, fresh_value_rows)
     return pl.pallas_call(
         functools.partial(attend_kernel, chunk),
-        out_shape=jax.ShapeDtypeStruct(queries.shape, BF),
-        in_specs=[SMEM] + [ANY] * 5,
-        out_specs=VMEM,
-        scratch_shapes=[pltpu.VMEM(x.shape, BF) for x in moved]
-        + [pltpu.SemaphoreType.DMA((3, max(3, requests // chunk)))],
+        out_shape=[jax.ShapeDtypeStruct(shape, BF) for shape in (queries.shape, part, part)],
+        in_specs=[SMEM] + [ANY] * 6,
+        out_specs=[VMEM, ANY, ANY],
+        scratch_shapes=[pltpu.VMEM(shape, BF) for shape in [x.shape for x in moved] + [part, part]]
+        + [
+            pltpu.SemaphoreType.DMA((3, max(3, requests // chunk))),
+            pltpu.SemaphoreType.DMA((blocks, 2)),
+            pltpu.SemaphoreType.DMA((2,)),
+        ],
         compiler_params=pltpu.CompilerParams(vmem_limit_bytes=60 << 20),
         cost_estimate=pl.CostEstimate(
             flops=8 * queries.size * cache_keys.shape[1],
@@ -114,23 +166,7 @@
             transcendentals=queries.size,
         ),
         name="attend",
-    )(lengths, *moved)
-
-
-def split_kernel(up_hbm, low_ref, high_ref, sems):
-    half = low_ref.shape[3]
-    low = lax.rem(lax.axis_index("tensor"), 2)
-    copies = []
-    for b in range(low_ref.shape[0]):
-        for i, (ref, part) in enumerate(((low_ref, low), (high_ref, 1 - low))):
-            start = pl.multiple_of((2 * b + part) * half, half)
-            copies.append(
-                pltpu.make_async_copy(up_hbm.at[:, :, pl.ds(start, half)], ref.at[b], sems.at[b, i])
-            )
-    for copy in copies:
-        copy.start()
-    for copy in copies:
-        copy.wait()
+    )(lengths, *moved, up)
 
 
 def blockwise(position, count, size, index):
@@ -282,7 +318,7 @@
         expand_weight,
     ):
         low = lax.axis_index("tensor") % 2
-        per_owner, rank_part, width = expand_weight.shape
+        per_owner = expand_weight.shape[0]
         rank = shrink_weight.shape[2]
         columns = out_weight.shape[1]
         half = columns // 2
@@ -290,29 +326,39 @@
         tokens = adapter_ids.shape[0]
         owned = per_owner * SLOTS
 
-        attended = attend(
-            queries, cache_keys, cached_value_rows, new_keys, fresh_value_rows, lengths
+        attended, up_low, up_high = attend(
+            queries,
+            cache_keys,
+            cached_value_rows,
+            new_keys,
+            fresh_value_rows,
+            lengths,
+            expand_weight,
+            n_adapter,
         )
         blocks = [swap(attended, "adapter", n_adapter, k) for k in range(1, n_adapter)]
 
-        up_shape = jax.ShapeDtypeStruct((n_adapter, per_owner, rank_part, half), BF)
-        expand_weight, ids, _ = lax.optimization_barrier(
-            (expand_weight, adapter_ids.reshape(1, tokens), attended)
-        )
-        up_low, up_high = pl.pallas_call(
-            split_kernel,
-            out_shape=(up_shape, up_shape),
-            in_specs=[ANY],
-            out_specs=(VMEM, VMEM),
-            scratch_shapes=[pltpu.SemaphoreType.DMA((n_adapter, 2))],
-            compiler_params=pltpu.CompilerParams(vmem_limit_bytes=16 << 20),
-            name="split",
-        )(expand_weight)
         maps = [up_low] + [
             swap((up_low, up_high)[k % 2], "tensor", n_tensor, k) for k in range(1, n_tensor)
         ]
-        ids, blocks[0] = lax.optimization_barrier((ids, blocks[0]))
-        out_weight, maps[1] = lax.optimization_barrier((out_weight, maps[1]))
+        ids = adapter_ids.reshape(1, tokens)
+        ids, maps[1] = lax.optimization_barrier((ids, maps[1]))
+
+        here, select, place, reorder = pl.pallas_call(
+            functools.partial(ids_kernel, n_adapter, n_tensor),
+            out_shape=[
+                jax.ShapeDtypeStruct((tokens, per_owner), F32),
+                jax.ShapeDtypeStruct((owned, tokens), BF),
+                jax.ShapeDtypeStruct((tokens, n_adapter * owned), BF),
+                jax.ShapeDtypeStruct((rank, rank), BF),
+            ],
+            in_specs=[VMEM, SMEM],
+            out_specs=[VMEM] * 4,
+            compiler_params=pltpu.CompilerParams(vmem_limit_bytes=16 << 20),
+            name="ids",
+        )(ids, adapter_slots)
+
+        out_weight, here, blocks[0] = lax.optimization_barrier((out_weight, here, blocks[0]))
 
         loads = (attended, out_weight, jnp.swapaxes(shrink_weight, 1, 2))
         here_block, weight, down = pl.pallas_call(
@@ -329,20 +375,6 @@
         )(*loads)
         blocks = [here_block] + blocks
 
-        here, select, place, reorder = pl.pallas_call(
-            functools.partial(ids_kernel, n_adapter, n_tensor),
-            out_shape=[
-                jax.ShapeDtypeStruct((tokens, per_owner), F32),
-                jax.ShapeDtypeStruct((owned, tokens), BF),
-                jax.ShapeDtypeStruct((tokens, n_adapter * owned), BF),
-                jax.ShapeDtypeStruct((rank, rank), BF),
-            ],
-            in_specs=[VMEM, SMEM],
-            out_specs=[VMEM] * 4,
-            compiler_params=pltpu.CompilerParams(vmem_limit_bytes=16 << 20),
-            name="ids",
-        )(ids, adapter_slots)
-
         shrunk = pl.pallas_call(
             shrink_kernel,
             out_shape=jax.ShapeDtypeStruct((tokens // 2, 2 * rank), BF),
@@ -355,7 +387,6 @@
         shrunk, *blocks = lax.optimization_barrier((shrunk, *blocks))
         shrunk = [shrunk] + [swap(shrunk, "tensor", n_tensor, k) for k in range(1, n_tensor)]
 
-        blocks[0], *maps[2:] = lax.optimization_barrier((blocks[0], *maps[2:]))
 
         def project(other, dtype):
             return pl.pallas_call(
@@ -373,6 +404,7 @@
             )(*blocks, weight)
 
         came = swap(project(1, BF), "tensor", n_tensor, 1)
+        blocks[0], *maps[2:] = lax.optimization_barrier((blocks[0], *maps[2:]))
         base = pl.pallas_call(
             join_kernel,
             out_shape=jax.ShapeDtypeStruct((tokens, half), BF),

time: 50.1 us -> 47.1 us (0.940)
  starting transfers between devices: 18.3 us -> 16.4 us
  local copies, waits for them, and re-layouts: 4.29 us -> 3.26 us
    ppermute x15, starting transfers between devices: 18.3 us -> 16.4 us  [swap(): return lax.ppermute(x, axis, [(i, i ^ k) for i in range(n)])]
    unnamed x10, local copies, waits for them, and re-layouts: 4.29 us -> 3.26 us
    pallas_call x2 -> x1, Pallas kernels: 4.26 us -> 4.28 us  [attend(): pl.pallas_call(functools.partial(attend_kernel, chunk), out_shape=[jax.Sh...]
  transfers between devices with their start and end apart: 15 -> 15, of which waited for: 6 -> 7; matrix products, arithmetic and copies ran while one was open for 0% -> 0% of each run, Pallas kernels for 13% -> 15%
where the time goes in v3:
time: 47.1 us; the launch traced here: 46.9 us
  starting transfers between devices  16.4 us (35%)
  waiting for transfers between devices  14.6 us (31%)
  Pallas kernels  11.5 us (24%)
  local copies, waits for them, and re-layouts  3.26 us (7%)
  other arithmetic  0.92 us (2%)
    ppermute x15, starting transfers between devices, swap(): return lax.ppermute(x, axis, [(i, i ^ k) for i in range(n)])  16.4 us
    ppermute x15, waiting for transfers between devices, swap(): return lax.ppermute(x, axis, [(i, i ^ k) for i in range(n)])  14.6 us
    pallas_call x1, Pallas kernels, attend(): pl.pallas_call(functools.partial(attend_kernel, chunk), out_shape=[jax.Sh...  4.28 us
    pallas_call x1, Pallas kernels, shards(): pl.pallas_call(load_kernel, out_shape=[jax.ShapeDtypeStruct(x.shape, BF)...  3.54 us
    unnamed x10, local copies, waits for them, and re-layouts  3.26 us
    pallas_call x2, Pallas kernels, project(): pl.pallas_call(functools.partial(project_kernel, other), out_shape=jax.Sh...  1.54 us
  transfers between devices with their start and end apart: 15, of which 7 were waited for; matrix products, arithmetic and copies ran while one was open for 0% of the time, Pallas kernels for 15%

profile of v3, /device:TPU:0, one launch (start us, length us, event | category | flops | bytes accessed | tf_op | source)
XLA Modules:
  0.0 46.9 jit_solution(9782184763103699104)
XLA Ops:
  0.0 4.3 %attend.1 = (bf16[32,2048]{1,0:T(8,128)(2,1)}, bf16[4,2,16,1024]{3,2,1,0:T(8,128)(2,1)}, bf16[4,2,16,1024]{3,2,1,0:T(8,128)(2,1)}) custom-call(s32[32]{0:T(128)} %length_ref.1, bf16[32,2048]{1,0:T(8,128)(2,1)} %q_hbm.1, bf16[32,64,256]{2,1,0:T(8,128)(2,1)} %k_hbm.1, bf16[32,64,256]{2,1,0:T(8,128)(2,1)} %v_hbm.1, bf16[32,256]{1,0:T(8,128)(2,1)} %nk_hbm.1, ...), custom_call_target="tpu_custom_call" | custom-call | flops 33554432 | bytes 2097152 | tf_op jit(solution)/shard_map/attend/pallas_call | solution.py:151
  4.3 0.5 %collective-permute-start = (bf16[4,2,16,1024]{3,2,1,0:T(8,128)(2,1)}, bf16[4,2,16,1024]{3,2,1,0:T(8,128)(2,1)S(1)}, u32[]{:S(2)}, u32[]{:S(2)}) collective-permute-start(bf16[4,2,16,1024]{3,2,1,0:T(8,128)(2,1)} %get-tuple-element.37), channel_id=1, source_target_pairs={{0,1},{1,0},{2,3},{3,2},{4,5},{5,4},{6,7},{7,6},{8,9},{9,8},{10,11... | collective-permute-start | bytes 786440 | tf_op jit(solution)/shard_map/ppermute | solution.py:305
  4.8 2.6 %collective-permute-start.1 = (bf16[32,2048]{1,0:T(8,128)(2,1)}, bf16[32,2048]{1,0:T(8,128)(2,1)S(1)}, u32[]{:S(2)}, u32[]{:S(2)}) collective-permute-start(bf16[32,2048]{1,0:T(8,128)(2,1)} %get-tuple-element.40.refs_0_), channel_id=1, source_target_pairs={{0,4},{4,0},{8,12},{12,8},{1,5},{5,1},{9,13},{13,9},{2,6},{6,2},{1... | collective-permute-start | bytes 393224 | tf_op jit(solution)/shard_map/ppermute | solution.py:305
  7.5 2.6 %collective-permute-start.2 = (bf16[32,2048]{1,0:T(8,128)(2,1)}, bf16[32,2048]{1,0:T(8,128)(2,1)S(1)}, u32[]{:S(2)}, u32[]{:S(2)}) collective-permute-start(bf16[32,2048]{1,0:T(8,128)(2,1)} %get-tuple-element.40.refs_0_), channel_id=1, source_target_pairs={{0,8},{4,12},{8,0},{12,4},{1,9},{5,13},{9,1},{13,5},{2,10},{6,14},... | collective-permute-start | bytes 393224 | tf_op jit(solution)/shard_map/ppermute | solution.py:305
  10.0 1.0 %collective-permute-start.5 = (bf16[4,2,16,1024]{3,2,1,0:T(8,128)(2,1)}, bf16[4,2,16,1024]{3,2,1,0:T(8,128)(2,1)S(1)}, u32[]{:S(2)}, u32[]{:S(2)}) collective-permute-start(bf16[4,2,16,1024]{3,2,1,0:T(8,128)(2,1)} %get-tuple-element.37), channel_id=1, source_target_pairs={{0,3},{1,2},{2,1},{3,0},{4,7},{5,6},{6,5},{7,4},{8,11},{9,10},{10,... | collective-permute-start | bytes 786440 | tf_op jit(solution)/shard_map/ppermute | solution.py:305
  11.0 0.8 %collective-permute-start.4 = (bf16[4,2,16,1024]{3,2,1,0:T(8,128)(2,1)}, bf16[4,2,16,1024]{3,2,1,0:T(8,128)(2,1)S(1)}, u32[]{:S(2)}, u32[]{:S(2)}) collective-permute-start(bf16[4,2,16,1024]{3,2,1,0:T(8,128)(2,1)} %get-tuple-element.48.refs_6_), channel_id=1, source_target_pairs={{0,2},{1,3},{2,0},{3,1},{4,6},{5,7},{6,4},{7,5},{8,10},{9,11},{10,... | collective-permute-start | bytes 786440 | tf_op jit(solution)/shard_map/ppermute | solution.py:305
  11.8 0.7 %copy-done.3 = s32[128]{0:T(128)S(1)} copy-done((s32[128]{0:T(128)S(1)}, s32[128]{0:T(128)}, u32[]{:S(2)}) %copy-start.3) | copy-done | bytes 536
  12.5 0.7 %copy-done.4 = s32[8]{0:T(128)S(1)} copy-done((s32[8]{0:T(128)S(1)}, s32[8]{0:T(128)}, u32[]{:S(2)}) %copy-start.4) | copy-done | bytes 56
  13.1 0.7 %ids.1 = (f32[128,2]{1,0:T(8,128)S(1)}, bf16[64,128]{1,0:T(8,128)(2,1)S(1)}, bf16[128,256]{1,0:T(8,128)(2,1)S(1)}, bf16[64,64]{1,0:T(8,128)(2,1)S(1)}) custom-call(s32[1,128]{1,0:T(1,128)S(1)} %bitcast.3, s32[8]{0:T(128)S(1)} %copy-done.4), custom_call_target="tpu_custom_call" | custom-call | tf_op jit(solution)/shard_map/ids/pallas_call | solution.py:347
  13.8 0.1 collective-permute-done.1.refs_1_
  14.0 1.0 %copy-done = bf16[2,2048,64]{1,2,0:T(8,128)(2,1)S(1)} copy-done((bf16[2,2048,64]{1,2,0:T(8,128)(2,1)S(1)}, bf16[2,2048,64]{1,2,0:T(8,128)(2,1)}, u32[]{:S(2)}) %copy-start) | copy-done | bytes 524312
  15.0 0.9 %copy-done.2 = bf16[32,2048]{1,0:T(8,128)(2,1)S(1)} copy-done((bf16[32,2048]{1,0:T(8,128)(2,1)S(1)}, bf16[32,2048]{1,0:T(8,128)(2,1)}, u32[]{:S(2)}) %copy-start.2) | copy-done | bytes 131096
  15.9 3.5 %load.1 = (bf16[32,2048]{1,0:T(8,128)(2,1)S(1)}, bf16[2048,2048]{1,0:T(8,128)(2,1)S(1)}, bf16[2,64,2048]{2,1,0:T(8,128)(2,1)S(1)}) custom-call(bf16[32,2048]{1,0:T(8,128)(2,1)S(1)} %copy-done.2, bf16[2048,2048]{1,0:T(8,128)(2,1)} %refs_1_, bf16[2,64,2048]{2,1,0:T(8,128)(2,1)S(1)} %bitcast.2), custom_call_target="tpu_custom_call" | custom-call | bytes 16777216 | tf_op jit(solution)/shard_map/load/pallas_call | solution.py:364
  19.5 1.1 %collective-permute-done.2.refs_2_ = bf16[32,2048]{1,0:T(8,128)(2,1)S(1)} collective-permute-done((bf16[32,2048]{1,0:T(8,128)(2,1)}, bf16[32,2048]{1,0:T(8,128)(2,1)S(1)}, u32[]{:S(2)}, u32[]{:S(2)}) %collective-permute-start.2) | collective-permute-done | bytes 131104 | tf_op jit(solution)/shard_map/ppermute | solution.py:305
  20.6 0.5 %shrink.1.refs_0_ = bf16[64,128]{1,0:T(8,128)(2,1)S(1)} custom-call(bf16[32,2048]{1,0:T(8,128)(2,1)S(1)} %get-tuple-element.49.refs_0_, bf16[32,2048]{1,0:T(8,128)(2,1)S(1)} %collective-permute-done.1.refs_1_, bf16[32,2048]{1,0:T(8,128)(2,1)S(1)} %collective-permute-done.2.refs_2_, bf16[32,2048]{1,0:T(8,128)(2,1)S(1)} %collective-permute-done.3.refs_3_, ...), custom_call_target="tpu_custom_call" | custom-call | tf_op jit(solution)/shard_map/shrink/pallas_call | solution.py:378
  21.1 0.8 %project.3 = bf16[128,1024]{1,0:T(8,128)(2,1)S(1)} custom-call(bf16[32,2048]{1,0:T(8,128)(2,1)S(1)} %get-tuple-element.49.refs_0_, bf16[32,2048]{1,0:T(8,128)(2,1)S(1)} %collective-permute-done.1.refs_1_, bf16[32,2048]{1,0:T(8,128)(2,1)S(1)} %collective-permute-done.2.refs_2_, bf16[32,2048]{1,0:T(8,128)(2,1)S(1)} %collective-permute-done.3.refs_3_, ...), custom_call_target="tpu_custom_call" | custom-call | flops 536870912 | bytes 8388608 | tf_op jit(solution)/shard_map/project/pallas_call | solution.py:392
  21.9 0.5 %collective-permute-start.7 = (bf16[64,128]{1,0:T(8,128)(2,1)S(1)}, bf16[64,128]{1,0:T(8,128)(2,1)S(1)}, u32[]{:S(2)}, u32[]{:S(2)}) collective-permute-start(bf16[64,128]{1,0:T(8,128)(2,1)S(1)} %shrink.1.refs_0_), channel_id=1, source_target_pairs={{0,1},{1,0},{2,3},{3,2},{4,5},{5,4},{6,7},{7,6},{8,9},{9,8},{10,11... | collective-permute-start | bytes 49160 | tf_op jit(solution)/shard_map/ppermute | solution.py:305
  22.4 1.5 %collective-permute-start.8 = (bf16[64,128]{1,0:T(8,128)(2,1)S(1)}, bf16[64,128]{1,0:T(8,128)(2,1)S(1)}, u32[]{:S(2)}, u32[]{:S(2)}) collective-permute-start(bf16[64,128]{1,0:T(8,128)(2,1)S(1)} %shrink.1.refs_0_), channel_id=1, source_target_pairs={{0,2},{1,3},{2,0},{3,1},{4,6},{5,7},{6,4},{7,5},{8,10},{9,11},{10,... | collective-permute-start | bytes 49160 | tf_op jit(solution)/shard_map/ppermute | solution.py:305
  23.9 0.6 %collective-permute-done.4.refs_8_ = bf16[4,2,16,1024]{3,2,1,0:T(8,128)(2,1)S(1)} collective-permute-done((bf16[4,2,16,1024]{3,2,1,0:T(8,128)(2,1)}, bf16[4,2,16,1024]{3,2,1,0:T(8,128)(2,1)S(1)}, u32[]{:S(2)}, u32[]{:S(2)}) %collective-permute-start.4) | collective-permute-done | bytes 262176 | tf_op jit(solution)/shard_map/ppermute | solution.py:305
  24.5 1.1 %collective-permute-start.9 = (bf16[64,128]{1,0:T(8,128)(2,1)S(1)}, bf16[64,128]{1,0:T(8,128)(2,1)S(1)}, u32[]{:S(2)}, u32[]{:S(2)}) collective-permute-start(bf16[64,128]{1,0:T(8,128)(2,1)S(1)} %shrink.1.refs_0_), channel_id=1, source_target_pairs={{0,3},{1,2},{2,1},{3,0},{4,7},{5,6},{6,5},{7,4},{8,11},{9,10},{10,... | collective-permute-start | bytes 49160 | tf_op jit(solution)/shard_map/ppermute | solution.py:305
  25.6 0.8 %project.2.keep_ref = f32[128,1024]{1,0:T(8,128)S(1)} custom-call(bf16[32,2048]{1,0:T(8,128)(2,1)S(1)} %get-tuple-element.49.refs_0_, bf16[32,2048]{1,0:T(8,128)(2,1)S(1)} %collective-permute-done.1.refs_1_, bf16[32,2048]{1,0:T(8,128)(2,1)S(1)} %collective-permute-done.2.refs_2_, bf16[32,2048]{1,0:T(8,128)(2,1)S(1)} %collective-permute-done.3.refs_3_, ...), custom_call_target="tpu_custom_call" | custom-call | flops 536870912 | bytes 8388608 | tf_op jit(solution)/shard_map/project/pallas_call | solution.py:392
  26.5 1.3 %collective-permute-done.9.refs_3_ = bf16[64,128]{1,0:T(8,128)(2,1)S(1)} collective-permute-done((bf16[64,128]{1,0:T(8,128)(2,1)S(1)}, bf16[64,128]{1,0:T(8,128)(2,1)S(1)}, u32[]{:S(2)}, u32[]{:S(2)}) %collective-permute-start.9) | collective-permute-done | bytes 16416 | tf_op jit(solution)/shard_map/ppermute | solution.py:305
  27.8 1.3 %collective-permute-start.10 = (bf16[128,1024]{1,0:T(8,128)(2,1)S(1)}, bf16[128,1024]{1,0:T(8,128)(2,1)S(1)}, u32[]{:S(2)}, u32[]{:S(2)}) collective-permute-start(bf16[128,1024]{1,0:T(8,128)(2,1)S(1)} %join.1.refs_0_), channel_id=1, source_target_pairs={{0,2},{1,3},{2,0},{3,1},{4,6},{5,7},{6,4},{7,5},{8,10},{9,11},{10,... | collective-permute-start | bytes 786440 | tf_op jit(solution)/shard_map/ppermute | solution.py:305
  29.0 0.7 %terms.1 = (bf16[64,1024]{1,0:T(8,128)(2,1)S(1)}, bf16[64,1024]{1,0:T(8,128)(2,1)S(1)}, bf16[64,1024]{1,0:T(8,128)(2,1)S(1)}, bf16[64,1024]{1,0:T(8,128)(2,1)S(1)}) custom-call(bf16[64,128]{1,0:T(8,128)(2,1)S(1)} %shrink.1.refs_0_, bf16[64,128]{1,0:T(8,128)(2,1)S(1)} %collective-permute-done.7.refs_1_, bf16[64,128]{1,0:T(8,128)(2,1)S(1)} %collective-permute-done.8.refs_2_, ...), custom_call_target="tpu_custom_call" | custom-call | tf_op jit(solution)/shard_map/terms/pallas_call | solution.py:424
  29.7 1.4 %collective-permute-start.11 = (bf16[64,1024]{1,0:T(8,128)(2,1)S(1)}, bf16[64,1024]{1,0:T(8,128)(2,1)S(1)}, u32[]{:S(2)}, u32[]{:S(2)}) collective-permute-start(bf16[64,1024]{1,0:T(8,128)(2,1)S(1)} %get-tuple-element.66), channel_id=1, source_target_pairs={{0,4},{4,0},{8,12},{12,8},{1,5},{5,1},{9,13},{13,9},{2,6},{6,2},{1... | collective-permute-start | bytes 393224 | tf_op jit(solution)/shard_map/ppermute | solution.py:305
  31.2 2.7 %collective-permute-start.12 = (bf16[64,1024]{1,0:T(8,128)(2,1)S(1)}, bf16[64,1024]{1,0:T(8,128)(2,1)S(1)}, u32[]{:S(2)}, u32[]{:S(2)}) collective-permute-start(bf16[64,1024]{1,0:T(8,128)(2,1)S(1)} %get-tuple-element.67), channel_id=1, source_target_pairs={{0,8},{4,12},{8,0},{12,4},{1,9},{5,13},{9,1},{13,5},{2,10},{6,14},... | collective-permute-start | bytes 393224 | tf_op jit(solution)/shard_map/ppermute | solution.py:305
  33.8 0.3 collective-permute-start.13
  34.2 2.5 %collective-permute-done.11.refs_3_ = bf16[64,1024]{1,0:T(8,128)(2,1)S(1)} collective-permute-done((bf16[64,1024]{1,0:T(8,128)(2,1)S(1)}, bf16[64,1024]{1,0:T(8,128)(2,1)S(1)}, u32[]{:S(2)}, u32[]{:S(2)}) %collective-permute-start.11) | collective-permute-done | bytes 131104 | tf_op jit(solution)/shard_map/ppermute | solution.py:305
  36.7 7.4 %collective-permute-done.12.refs_4_ = bf16[64,1024]{1,0:T(8,128)(2,1)S(1)} collective-permute-done((bf16[64,1024]{1,0:T(8,128)(2,1)S(1)}, bf16[64,1024]{1,0:T(8,128)(2,1)S(1)}, u32[]{:S(2)}, u32[]{:S(2)}) %collective-permute-start.12) | collective-permute-done | bytes 131104 | tf_op jit(solution)/shard_map/ppermute | solution.py:305
  44.1 0.2 finish.1
  44.4 1.5 %collective-permute-done.14 = bf16[128,1024]{1,0:T(8,128)(2,1)S(1)} collective-permute-done((bf16[128,1024]{1,0:T(8,128)(2,1)S(1)}, bf16[128,1024]{1,0:T(8,128)(2,1)S(1)}, u32[]{:S(2)}, u32[]{:S(2)}) %collective-permute-start.14) | collective-permute-done | bytes 262176 | tf_op jit(solution)/shard_map/ppermute | solution.py:305
  46.0 0.9 %maximum_select_fusion = bf16[128,2048]{1,0:T(8,128)(2,1)} fusion(bf16[128,1024]{1,0:T(8,128)(2,1)S(1)} %collective-permute-done.14, bf16[128,1024]{1,0:T(8,128)(2,1)S(1)} %finish.1, pred[]{:T(512)S(6)} %eq.5), kind=kLoop, calls=%fused_computation | loop fusion | flops 2359296 | bytes 1048577 | tf_op jit(solution)/shard_map/jit(_where)/select_n | solution.py:445
  (18 shorter events, 0.2 us)
Async XLA Ops:
  4.3 6.7 %collective-permute-start = (bf16[4,2,16,1024]{3,2,1,0:T(8,128)(2,1)}, bf16[4,2,16,1024]{3,2,1,0:T(8,128)(2,1)S(1)}, u32[]{:S(2)}, u32[]{:S(2)}) collective-permute-start(bf16[4,2,16,1024]{3,2,1,0:T(8,128)(2,1)} %get-tuple-element.37), channel_id=1, source_target_pairs={{0,1},{1,0},{2,3},{3,2},{4,5},{5,4},{6,7},{7,6},{8,9},{9,8},{10,11... | collective-permute-start | bytes 786440 | tf_op jit(solution)/shard_map/ppermute | solution.py:305
  4.8 9.2 %collective-permute-start.1 = (bf16[32,2048]{1,0:T(8,128)(2,1)}, bf16[32,2048]{1,0:T(8,128)(2,1)S(1)}, u32[]{:S(2)}, u32[]{:S(2)}) collective-permute-start(bf16[32,2048]{1,0:T(8,128)(2,1)} %get-tuple-element.40.refs_0_), channel_id=1, source_target_pairs={{0,4},{4,0},{8,12},{12,8},{1,5},{5,1},{9,13},{13,9},{2,6},{6,2},{1... | collective-permute-start | bytes 393224 | tf_op jit(solution)/shard_map/ppermute | solution.py:305
  7.5 13.1 %collective-permute-start.2 = (bf16[32,2048]{1,0:T(8,128)(2,1)}, bf16[32,2048]{1,0:T(8,128)(2,1)S(1)}, u32[]{:S(2)}, u32[]{:S(2)}) collective-permute-start(bf16[32,2048]{1,0:T(8,128)(2,1)} %get-tuple-element.40.refs_0_), channel_id=1, source_target_pairs={{0,8},{4,12},{8,0},{12,4},{1,9},{5,13},{9,1},{13,5},{2,10},{6,14},... | collective-permute-start | bytes 393224 | tf_op jit(solution)/shard_map/ppermute | solution.py:305
  10.0 10.5 %collective-permute-start.3 = (bf16[32,2048]{1,0:T(8,128)(2,1)}, bf16[32,2048]{1,0:T(8,128)(2,1)S(1)}, u32[]{:S(2)}, u32[]{:S(2)}) collective-permute-start(bf16[32,2048]{1,0:T(8,128)(2,1)} %get-tuple-element.40.refs_0_), channel_id=1, source_target_pairs={{0,12},{4,8},{8,4},{12,0},{1,13},{5,9},{9,5},{13,1},{2,14},{6,10},... | collective-permute-start | bytes 393224 | tf_op jit(solution)/shard_map/ppermute | solution.py:305
  10.0 15.6 %collective-permute-start.5 = (bf16[4,2,16,1024]{3,2,1,0:T(8,128)(2,1)}, bf16[4,2,16,1024]{3,2,1,0:T(8,128)(2,1)S(1)}, u32[]{:S(2)}, u32[]{:S(2)}) collective-permute-start(bf16[4,2,16,1024]{3,2,1,0:T(8,128)(2,1)} %get-tuple-element.37), channel_id=1, source_target_pairs={{0,3},{1,2},{2,1},{3,0},{4,7},{5,6},{6,5},{7,4},{8,11},{9,10},{10,... | collective-permute-start | bytes 786440 | tf_op jit(solution)/shard_map/ppermute | solution.py:305
  11.0 13.4 %collective-permute-start.4 = (bf16[4,2,16,1024]{3,2,1,0:T(8,128)(2,1)}, bf16[4,2,16,1024]{3,2,1,0:T(8,128)(2,1)S(1)}, u32[]{:S(2)}, u32[]{:S(2)}) collective-permute-start(bf16[4,2,16,1024]{3,2,1,0:T(8,128)(2,1)} %get-tuple-element.48.refs_6_), channel_id=1, source_target_pairs={{0,2},{1,3},{2,0},{3,1},{4,6},{5,7},{6,4},{7,5},{8,10},{9,11},{10,... | collective-permute-start | bytes 786440 | tf_op jit(solution)/shard_map/ppermute | solution.py:305
  11.8 0.7 %copy-start.3 = (s32[128]{0:T(128)S(1)}, s32[128]{0:T(128)}, u32[]{:S(2)}) copy-start(s32[128]{0:T(128)} %param.17) | copy-start | bytes 1540
  12.4 0.7 %copy-start.4 = (s32[8]{0:T(128)S(1)}, s32[8]{0:T(128)}, u32[]{:S(2)}) copy-start(s32[8]{0:T(128)} %slots_ref.1) | copy-start | bytes 100
  14.0 1.0 %copy-start = (bf16[2,2048,64]{1,2,0:T(8,128)(2,1)S(1)}, bf16[2,2048,64]{1,2,0:T(8,128)(2,1)}, u32[]{:S(2)}) copy-start(bf16[2,2048,64]{1,2,0:T(8,128)(2,1)} %param.20) | copy-start | bytes 1572868
  15.0 0.9 %copy-start.2 = (bf16[32,2048]{1,0:T(8,128)(2,1)S(1)}, bf16[32,2048]{1,0:T(8,128)(2,1)}, u32[]{:S(2)}) copy-start(bf16[32,2048]{1,0:T(8,128)(2,1)} %get-tuple-element.40.refs_0_) | copy-start | bytes 393220
  21.1 8.0 %copy-start.1 = (bf16[4,2,16,1024]{3,2,1,0:T(8,128)(2,1)S(1)}, bf16[4,2,16,1024]{3,2,1,0:T(8,128)(2,1)}, u32[]{:S(2)}) copy-start(bf16[4,2,16,1024]{3,2,1,0:T(8,128)(2,1)} %get-tuple-element.48.refs_6_) | copy-start | bytes 786436
  21.8 4.5 %collective-permute-start.6 = (bf16[128,1024]{1,0:T(8,128)(2,1)S(1)}, bf16[128,1024]{1,0:T(8,128)(2,1)S(1)}, u32[]{:S(2)}, u32[]{:S(2)}) collective-permute-start(bf16[128,1024]{1,0:T(8,128)(2,1)S(1)} %project.3), channel_id=1, source_target_pairs={{0,1},{1,0},{2,3},{3,2},{4,5},{5,4},{6,7},{7,6},{8,9},{9,8},{10,11... | collective-permute-start | bytes 786440 | tf_op jit(solution)/shard_map/ppermute | solution.py:305
  21.9 4.5 %collective-permute-start.7 = (bf16[64,128]{1,0:T(8,128)(2,1)S(1)}, bf16[64,128]{1,0:T(8,128)(2,1)S(1)}, u32[]{:S(2)}, u32[]{:S(2)}) collective-permute-start(bf16[64,128]{1,0:T(8,128)(2,1)S(1)} %shrink.1.refs_0_), channel_id=1, source_target_pairs={{0,1},{1,0},{2,3},{3,2},{4,5},{5,4},{6,7},{7,6},{8,9},{9,8},{10,11... | collective-permute-start | bytes 49160 | tf_op jit(solution)/shard_map/ppermute | solution.py:305
  22.4 4.0 %collective-permute-start.8 = (bf16[64,128]{1,0:T(8,128)(2,1)S(1)}, bf16[64,128]{1,0:T(8,128)(2,1)S(1)}, u32[]{:S(2)}, u32[]{:S(2)}) collective-permute-start(bf16[64,128]{1,0:T(8,128)(2,1)S(1)} %shrink.1.refs_0_), channel_id=1, source_target_pairs={{0,2},{1,3},{2,0},{3,1},{4,6},{5,7},{6,4},{7,5},{8,10},{9,11},{10,... | collective-permute-start | bytes 49160 | tf_op jit(solution)/shard_map/ppermute | solution.py:305
  24.5 3.3 %collective-permute-start.9 = (bf16[64,128]{1,0:T(8,128)(2,1)S(1)}, bf16[64,128]{1,0:T(8,128)(2,1)S(1)}, u32[]{:S(2)}, u32[]{:S(2)}) collective-permute-start(bf16[64,128]{1,0:T(8,128)(2,1)S(1)} %shrink.1.refs_0_), channel_id=1, source_target_pairs={{0,3},{1,2},{2,1},{3,0},{4,7},{5,6},{6,5},{7,4},{8,11},{9,10},{10,... | collective-permute-start | bytes 49160 | tf_op jit(solution)/shard_map/ppermute | solution.py:305
  27.8 16.3 %collective-permute-start.10 = (bf16[128,1024]{1,0:T(8,128)(2,1)S(1)}, bf16[128,1024]{1,0:T(8,128)(2,1)S(1)}, u32[]{:S(2)}, u32[]{:S(2)}) collective-permute-start(bf16[128,1024]{1,0:T(8,128)(2,1)S(1)} %join.1.refs_0_), channel_id=1, source_target_pairs={{0,2},{1,3},{2,0},{3,1},{4,6},{5,7},{6,4},{7,5},{8,10},{9,11},{10,... | collective-permute-start | bytes 786440 | tf_op jit(solution)/shard_map/ppermute | solution.py:305
  29.7 7.0 %collective-permute-start.11 = (bf16[64,1024]{1,0:T(8,128)(2,1)S(1)}, bf16[64,1024]{1,0:T(8,128)(2,1)S(1)}, u32[]{:S(2)}, u32[]{:S(2)}) collective-permute-start(bf16[64,1024]{1,0:T(8,128)(2,1)S(1)} %get-tuple-element.66), channel_id=1, source_target_pairs={{0,4},{4,0},{8,12},{12,8},{1,5},{5,1},{9,13},{13,9},{2,6},{6,2},{1... | collective-permute-start | bytes 393224 | tf_op jit(solution)/shard_map/ppermute | solution.py:305
  31.2 12.9 %collective-permute-start.12 = (bf16[64,1024]{1,0:T(8,128)(2,1)S(1)}, bf16[64,1024]{1,0:T(8,128)(2,1)S(1)}, u32[]{:S(2)}, u32[]{:S(2)}) collective-permute-start(bf16[64,1024]{1,0:T(8,128)(2,1)S(1)} %get-tuple-element.67), channel_id=1, source_target_pairs={{0,8},{4,12},{8,0},{12,4},{1,9},{5,13},{9,1},{13,5},{2,10},{6,14},... | collective-permute-start | bytes 393224 | tf_op jit(solution)/shard_map/ppermute | solution.py:305
  33.8 10.3 %collective-permute-start.13 = (bf16[64,1024]{1,0:T(8,128)(2,1)S(1)}, bf16[64,1024]{1,0:T(8,128)(2,1)S(1)}, u32[]{:S(2)}, u32[]{:S(2)}) collective-permute-start(bf16[64,1024]{1,0:T(8,128)(2,1)S(1)} %get-tuple-element.68), channel_id=1, source_target_pairs={{0,12},{4,8},{8,4},{12,0},{1,13},{5,9},{9,5},{13,1},{2,14},{6,10},... | collective-permute-start | bytes 393224 | tf_op jit(solution)/shard_map/ppermute | solution.py:305
  44.4 1.6 %collective-permute-start.14 = (bf16[128,1024]{1,0:T(8,128)(2,1)S(1)}, bf16[128,1024]{1,0:T(8,128)(2,1)S(1)}, u32[]{:S(2)}, u32[]{:S(2)}) collective-permute-start(bf16[128,1024]{1,0:T(8,128)(2,1)S(1)} %finish.1), channel_id=1, source_target_pairs={{0,1},{1,0},{2,3},{3,2},{4,5},{5,4},{6,7},{7,6},{8,9},{9,8},{10,11... | collective-permute-start | bytes 786440 | tf_op jit(solution)/shard_map/ppermute | solution.py:305

commit v4 on v3

--- a/solution.py
+++ b/solution.py
@@ -232,7 +232,7 @@
     for k in range(len(blocks)):
         total_ref[block_rows(k, requests), :] = total[k * requests : (k + 1) * requests]
     middle = total.shape[0] // 2
-    out_ref[...] = jnp.concatenate([total_ref[:middle], total_ref[middle:]], axis=1).astype(BF)
+    out_ref[...] = jnp.concatenate([total_ref[:middle], total_ref[middle:]], axis=1)
 
 
 def load_kernel(*refs):
@@ -260,14 +260,17 @@
         out_ref[:, i * tile : (i + 1) * tile] = part.astype(out_ref.dtype)
 
 
-def join_kernel(keep_ref, came_ref, out_ref):
-    out_ref[...] = (keep_ref[...] + came_ref[...].astype(F32)).astype(BF)
-
-
-def terms_kernel(n_adapter, n_tensor, *refs):
-    parts = refs[:n_tensor]
-    select_ref, order_ref = refs[n_tensor : n_tensor + 2]
-    maps = refs[n_tensor + 2 : -n_adapter]
+def join_kernel(keep_ref, came_ref, *out_refs):
+    rows = out_refs[0].shape[0]
+    for i, out_ref in enumerate(out_refs):
+        part = slice(i * rows, (i + 1) * rows)
+        out_ref[...] = (keep_ref[part] + came_ref[part].astype(F32)).astype(BF)
+
+
+def terms_kernel(n_adapter, n_parts, *refs):
+    parts = refs[:n_parts]
+    select_ref, order_ref = refs[n_parts : n_parts + 2]
+    maps = refs[n_parts + 2 : -n_adapter]
     outs = refs[-n_adapter:]
     per_owner = maps[0].shape[1]
     a = lax.axis_index("adapter")
@@ -289,12 +292,13 @@
 
 def finish_kernel(requests, place_ref, *refs):
     *base, out_ref = refs
-    base, pieces = base[:2], base[2:]
+    base, pieces = base[:4], base[4:]
     blocks = range(out_ref.shape[0] // requests)
     received = jnp.concatenate([p[...] for p in pieces], axis=0)
     place = jnp.concatenate([place_ref[block_rows(k, requests), :] for k in blocks], axis=0)
     delta = jnp.dot(place, received, preferred_element_type=F32)
-    total = base[0][...].astype(F32) + base[1][...].astype(F32)
+    base = [b[...].astype(F32) for b in base]
+    total = jnp.concatenate([base[0] + base[1], base[2] + base[3]], axis=0)
     total = (total + ADAPTER_SCALE * delta).astype(BF)
     for k in blocks:
         out_ref[block_rows(k, requests), :] = total[k * requests : (k + 1) * requests]
@@ -377,7 +381,7 @@
 
         shrunk = pl.pallas_call(
             shrink_kernel,
-            out_shape=jax.ShapeDtypeStruct((tokens // 2, 2 * rank), BF),
+            out_shape=jax.ShapeDtypeStruct((tokens // 2, 2 * rank), F32),
             in_specs=[VMEM] * (n_adapter + 2),
             out_specs=VMEM,
             scratch_shapes=[pltpu.VMEM((tokens, rank), F32)],
@@ -385,7 +389,8 @@
             name="shrink",
         )(*blocks, here, down)
         shrunk, *blocks = lax.optimization_barrier((shrunk, *blocks))
-        shrunk = [shrunk] + [swap(shrunk, "tensor", n_tensor, k) for k in range(1, n_tensor)]
+        shrunk = (shrunk + swap(shrunk, "tensor", n_tensor, 1)).astype(BF)
+        shrunk = [shrunk] + [swap(shrunk, "tensor", n_tensor, k) for k in range(2, n_tensor, 2)]
 
 
         def project(other, dtype):
@@ -404,27 +409,21 @@
             )(*blocks, weight)
 
         came = swap(project(1, BF), "tensor", n_tensor, 1)
-        blocks[0], *maps[2:] = lax.optimization_barrier((blocks[0], *maps[2:]))
         base = pl.pallas_call(
             join_kernel,
-            out_shape=jax.ShapeDtypeStruct((tokens, half), BF),
+            out_shape=[jax.ShapeDtypeStruct((tokens // 2, half), BF)] * 2,
             in_specs=[VMEM] * 2,
-            out_specs=VMEM,
+            out_specs=[VMEM] * 2,
             compiler_params=pltpu.CompilerParams(vmem_limit_bytes=16 << 20),
             name="join",
         )(project(0, F32), came)
-        base, *shrunk = lax.optimization_barrier((base, *shrunk))
-        step = 2
-        while step * 2 < n_tensor:
-            other = swap(base, "tensor", n_tensor, step)
-            base = (base.astype(F32) + other.astype(F32)).astype(BF)
-            step *= 2
-        base = [base, swap(base, "tensor", n_tensor, step)]
+        base = list(lax.optimization_barrier((*base, *shrunk)))
+        base, shrunk = base[:2], base[2:]
 
         terms = pl.pallas_call(
-            functools.partial(terms_kernel, n_adapter, n_tensor),
+            functools.partial(terms_kernel, n_adapter, len(shrunk)),
             out_shape=[jax.ShapeDtypeStruct((owned, half), BF)] * n_adapter,
-            in_specs=[VMEM] * (2 + n_tensor + len(maps)),
+            in_specs=[VMEM] * (2 + len(shrunk) + len(maps)),
             out_specs=[VMEM] * n_adapter,
             compiler_params=pltpu.CompilerParams(vmem_limit_bytes=24 << 20),
             name="terms",
@@ -433,14 +432,23 @@
             swap(terms[k], "adapter", n_adapter, k) for k in range(1, n_adapter)
         ]
 
+        sums = []
+        for part in base:
+            step = 2
+            while step * 2 < n_tensor:
+                other = swap(part, "tensor", n_tensor, step)
+                part = (part.astype(F32) + other.astype(F32)).astype(BF)
+                step *= 2
+            sums += [part, swap(part, "tensor", n_tensor, step)]
+
         mine = pl.pallas_call(
             functools.partial(finish_kernel, requests),
             out_shape=jax.ShapeDtypeStruct((tokens, half), BF),
-            in_specs=[VMEM] * (3 + n_adapter),
+            in_specs=[VMEM] * (5 + n_adapter),
             out_specs=VMEM,
             compiler_params=pltpu.CompilerParams(vmem_limit_bytes=24 << 20),
             name="finish",
-        )(place, *base, *received)
+        )(place, *sums, *received)
         other = swap(mine, "tensor", n_tensor, 1)
         return jnp.where(
             low == 0,

time: 47.1 us -> 44.7 us (0.949)
  waiting for transfers between devices: 14.6 us -> 11.7 us
    ppermute x15, waiting for transfers between devices: 14.6 us -> 11.7 us  [swap(): return lax.ppermute(x, axis, [(i, i ^ k) for i in range(n)])]
  transfers between devices with their start and end apart: 15 -> 15, of which waited for: 7 -> 5; matrix products, arithmetic and copies ran while one was open for 0% -> 0% of each run, Pallas kernels for 15% -> 14%
where the time goes in v4:
time: 44.7 us; the launch traced here: 44.4 us
  starting transfers between devices  16.8 us (38%)
  waiting for transfers between devices  11.7 us (26%)
  Pallas kernels  11.6 us (26%)
  local copies, waits for them, and re-layouts  3.26 us (7%)
  other arithmetic  0.93 us (2%)
    ppermute x15, starting transfers between devices, swap(): return lax.ppermute(x, axis, [(i, i ^ k) for i in range(n)])  16.8 us
    ppermute x15, waiting for transfers between devices, swap(): return lax.ppermute(x, axis, [(i, i ^ k) for i in range(n)])  11.7 us
    pallas_call x1, Pallas kernels, attend(): pl.pallas_call(functools.partial(attend_kernel, chunk), out_shape=[jax.Sh...  4.31 us
    pallas_call x1, Pallas kernels, shards(): pl.pallas_call(load_kernel, out_shape=[jax.ShapeDtypeStruct(x.shape, BF)...  3.54 us
    unnamed x10, local copies, waits for them, and re-layouts  3.26 us
    pallas_call x2, Pallas kernels, project(): pl.pallas_call(functools.partial(project_kernel, other), out_shape=jax.Sh...  1.54 us
    select_n x1, other arithmetic, shards(): jnp.where(low == 0, jnp.concatenate([mine, other], axis=1), jnp.concatena...  0.92 us
  transfers between devices with their start and end apart: 15, of which 5 were waited for; matrix products, arithmetic and copies ran while one was open for 0% of the time, Pallas kernels for 14%

profile of v4, /device:TPU:0, one launch (start us, length us, event | category | flops | bytes accessed | tf_op | source)
XLA Modules:
  0.0 44.4 jit_solution(2947847003550011437)
XLA Ops:
  0.0 4.3 %attend.1 = (bf16[32,2048]{1,0:T(8,128)(2,1)}, bf16[4,2,16,1024]{3,2,1,0:T(8,128)(2,1)}, bf16[4,2,16,1024]{3,2,1,0:T(8,128)(2,1)}) custom-call(s32[32]{0:T(128)} %length_ref.1, bf16[32,2048]{1,0:T(8,128)(2,1)} %q_hbm.1, bf16[32,64,256]{2,1,0:T(8,128)(2,1)} %k_hbm.1, bf16[32,64,256]{2,1,0:T(8,128)(2,1)} %v_hbm.1, bf16[32,256]{1,0:T(8,128)(2,1)} %nk_hbm.1, ...), custom_call_target="tpu_custom_call" | custom-call | flops 33554432 | bytes 2097152 | tf_op jit(solution)/shard_map/attend/pallas_call | solution.py:151
  4.3 0.5 %collective-permute-start = (bf16[4,2,16,1024]{3,2,1,0:T(8,128)(2,1)}, bf16[4,2,16,1024]{3,2,1,0:T(8,128)(2,1)S(1)}, u32[]{:S(2)}, u32[]{:S(2)}) collective-permute-start(bf16[4,2,16,1024]{3,2,1,0:T(8,128)(2,1)} %get-tuple-element.35), channel_id=1, source_target_pairs={{0,1},{1,0},{2,3},{3,2},{4,5},{5,4},{6,7},{7,6},{8,9},{9,8},{10,11... | collective-permute-start | bytes 786440 | tf_op jit(solution)/shard_map/ppermute | solution.py:309
  4.8 2.6 %collective-permute-start.1 = (bf16[32,2048]{1,0:T(8,128)(2,1)}, bf16[32,2048]{1,0:T(8,128)(2,1)S(1)}, u32[]{:S(2)}, u32[]{:S(2)}) collective-permute-start(bf16[32,2048]{1,0:T(8,128)(2,1)} %get-tuple-element.38.refs_0_), channel_id=1, source_target_pairs={{0,4},{4,0},{8,12},{12,8},{1,5},{5,1},{9,13},{13,9},{2,6},{6,2},{1... | collective-permute-start | bytes 393224 | tf_op jit(solution)/shard_map/ppermute | solution.py:309
  7.5 2.6 %collective-permute-start.2 = (bf16[32,2048]{1,0:T(8,128)(2,1)}, bf16[32,2048]{1,0:T(8,128)(2,1)S(1)}, u32[]{:S(2)}, u32[]{:S(2)}) collective-permute-start(bf16[32,2048]{1,0:T(8,128)(2,1)} %get-tuple-element.38.refs_0_), channel_id=1, source_target_pairs={{0,8},{4,12},{8,0},{12,4},{1,9},{5,13},{9,1},{13,5},{2,10},{6,14},... | collective-permute-start | bytes 393224 | tf_op jit(solution)/shard_map/ppermute | solution.py:309
  10.1 1.0 %collective-permute-start.10 = (bf16[4,2,16,1024]{3,2,1,0:T(8,128)(2,1)}, bf16[4,2,16,1024]{3,2,1,0:T(8,128)(2,1)S(1)}, u32[]{:S(2)}, u32[]{:S(2)}) collective-permute-start(bf16[4,2,16,1024]{3,2,1,0:T(8,128)(2,1)} %get-tuple-element.35), channel_id=1, source_target_pairs={{0,3},{1,2},{2,1},{3,0},{4,7},{5,6},{6,5},{7,4},{8,11},{9,10},{10,... | collective-permute-start | bytes 786440 | tf_op jit(solution)/shard_map/ppermute | solution.py:309
  11.1 0.8 %collective-permute-start.9 = (bf16[4,2,16,1024]{3,2,1,0:T(8,128)(2,1)}, bf16[4,2,16,1024]{3,2,1,0:T(8,128)(2,1)S(1)}, u32[]{:S(2)}, u32[]{:S(2)}) collective-permute-start(bf16[4,2,16,1024]{3,2,1,0:T(8,128)(2,1)} %get-tuple-element.59.refs_4_), channel_id=1, source_target_pairs={{0,2},{1,3},{2,0},{3,1},{4,6},{5,7},{6,4},{7,5},{8,10},{9,11},{10,... | collective-permute-start | bytes 786440 | tf_op jit(solution)/shard_map/ppermute | solution.py:309
  11.8 0.7 %copy-done.3 = s32[128]{0:T(128)S(1)} copy-done((s32[128]{0:T(128)S(1)}, s32[128]{0:T(128)}, u32[]{:S(2)}) %copy-start.3) | copy-done | bytes 536
  12.5 0.7 %copy-done.4 = s32[8]{0:T(128)S(1)} copy-done((s32[8]{0:T(128)S(1)}, s32[8]{0:T(128)}, u32[]{:S(2)}) %copy-start.4) | copy-done | bytes 56
  13.1 0.7 %ids.1 = (f32[128,2]{1,0:T(8,128)S(1)}, bf16[64,128]{1,0:T(8,128)(2,1)S(1)}, bf16[128,256]{1,0:T(8,128)(2,1)S(1)}, bf16[64,64]{1,0:T(8,128)(2,1)S(1)}) custom-call(s32[1,128]{1,0:T(1,128)S(1)} %bitcast.3, s32[8]{0:T(128)S(1)} %copy-done.4), custom_call_target="tpu_custom_call" | custom-call | tf_op jit(solution)/shard_map/ids/pallas_call | solution.py:351
  13.9 0.1 collective-permute-done.1.refs_1_
  14.0 1.0 %copy-done = bf16[2,2048,64]{1,2,0:T(8,128)(2,1)S(1)} copy-done((bf16[2,2048,64]{1,2,0:T(8,128)(2,1)S(1)}, bf16[2,2048,64]{1,2,0:T(8,128)(2,1)}, u32[]{:S(2)}) %copy-start) | copy-done | bytes 524312
  15.0 0.9 %copy-done.2 = bf16[32,2048]{1,0:T(8,128)(2,1)S(1)} copy-done((bf16[32,2048]{1,0:T(8,128)(2,1)S(1)}, bf16[32,2048]{1,0:T(8,128)(2,1)}, u32[]{:S(2)}) %copy-start.2) | copy-done | bytes 131096
  15.9 3.5 %load.1 = (bf16[32,2048]{1,0:T(8,128)(2,1)S(1)}, bf16[2048,2048]{1,0:T(8,128)(2,1)S(1)}, bf16[2,64,2048]{2,1,0:T(8,128)(2,1)S(1)}) custom-call(bf16[32,2048]{1,0:T(8,128)(2,1)S(1)} %copy-done.2, bf16[2048,2048]{1,0:T(8,128)(2,1)} %refs_1_, bf16[2,64,2048]{2,1,0:T(8,128)(2,1)S(1)} %bitcast.2), custom_call_target="tpu_custom_call" | custom-call | bytes 16777216 | tf_op jit(solution)/shard_map/load/pallas_call | solution.py:368
  19.5 1.1 %collective-permute-done.2.refs_2_ = bf16[32,2048]{1,0:T(8,128)(2,1)S(1)} collective-permute-done((bf16[32,2048]{1,0:T(8,128)(2,1)}, bf16[32,2048]{1,0:T(8,128)(2,1)S(1)}, u32[]{:S(2)}, u32[]{:S(2)}) %collective-permute-start.2) | collective-permute-done | bytes 131104 | tf_op jit(solution)/shard_map/ppermute | solution.py:309
  20.6 0.5 %shrink.1 = f32[64,128]{1,0:T(8,128)S(1)} custom-call(bf16[32,2048]{1,0:T(8,128)(2,1)S(1)} %get-tuple-element.45.refs_0_, bf16[32,2048]{1,0:T(8,128)(2,1)S(1)} %collective-permute-done.1.refs_1_, bf16[32,2048]{1,0:T(8,128)(2,1)S(1)} %collective-permute-done.2.refs_2_, bf16[32,2048]{1,0:T(8,128)(2,1)S(1)} %collective-permute-done.3.refs_3_, ...), custom_call_target="tpu_custom_call" | custom-call | tf_op jit(solution)/shard_map/shrink/pallas_call | solution.py:382
  21.1 0.0 collective-permute-start.5
  21.1 0.8 %project.3 = bf16[128,1024]{1,0:T(8,128)(2,1)S(1)} custom-call(bf16[32,2048]{1,0:T(8,128)(2,1)S(1)} %get-tuple-element.45.refs_0_, bf16[32,2048]{1,0:T(8,128)(2,1)S(1)} %collective-permute-done.1.refs_1_, bf16[32,2048]{1,0:T(8,128)(2,1)S(1)} %collective-permute-done.2.refs_2_, bf16[32,2048]{1,0:T(8,128)(2,1)S(1)} %collective-permute-done.3.refs_3_, ...), custom_call_target="tpu_custom_call" | custom-call | flops 536870912 | bytes 8388608 | tf_op jit(solution)/shard_map/project/pallas_call | solution.py:397
  21.9 0.5 %collective-permute-start.4 = (bf16[128,1024]{1,0:T(8,128)(2,1)S(1)}, bf16[128,1024]{1,0:T(8,128)(2,1)S(1)}, u32[]{:S(2)}, u32[]{:S(2)}) collective-permute-start(bf16[128,1024]{1,0:T(8,128)(2,1)S(1)} %project.3), channel_id=1, source_target_pairs={{0,1},{1,0},{2,3},{3,2},{4,5},{5,4},{6,7},{7,6},{8,9},{9,8},{10,11... | collective-permute-start | bytes 786440 | tf_op jit(solution)/shard_map/ppermute | solution.py:309
  22.5 1.6 %collective-permute-start.6 = (bf16[64,128]{1,0:T(8,128)(2,1)S(1)}, bf16[64,128]{1,0:T(8,128)(2,1)S(1)}, u32[]{:S(2)}, u32[]{:S(2)}) collective-permute-start(bf16[64,128]{1,0:T(8,128)(2,1)S(1)} %add_convert_fusion.refs_0_), channel_id=1, source_target_pairs={{0,2},{1,3},{2,0},{3,1},{4,6},{5,7},{6,4},{7,5},{8,10},{9,11},{10,... | collective-permute-start | bytes 49160 | tf_op jit(solution)/shard_map/ppermute | solution.py:309
  24.0 0.8 %project.2.keep_ref = f32[128,1024]{1,0:T(8,128)S(1)} custom-call(bf16[32,2048]{1,0:T(8,128)(2,1)S(1)} %get-tuple-element.45.refs_0_, bf16[32,2048]{1,0:T(8,128)(2,1)S(1)} %collective-permute-done.1.refs_1_, bf16[32,2048]{1,0:T(8,128)(2,1)S(1)} %collective-permute-done.2.refs_2_, bf16[32,2048]{1,0:T(8,128)(2,1)S(1)} %collective-permute-done.3.refs_3_, ...), custom_call_target="tpu_custom_call" | custom-call | flops 536870912 | bytes 8388608 | tf_op jit(solution)/shard_map/project/pallas_call | solution.py:397
  24.9 1.4 %collective-permute-done.6.refs_1_ = bf16[64,128]{1,0:T(8,128)(2,1)S(1)} collective-permute-done((bf16[64,128]{1,0:T(8,128)(2,1)S(1)}, bf16[64,128]{1,0:T(8,128)(2,1)S(1)}, u32[]{:S(2)}, u32[]{:S(2)}) %collective-permute-start.6) | collective-permute-done | bytes 16416 | tf_op jit(solution)/shard_map/ppermute | solution.py:309
  26.3 0.7 %terms.1 = (bf16[64,1024]{1,0:T(8,128)(2,1)S(1)}, bf16[64,1024]{1,0:T(8,128)(2,1)S(1)}, bf16[64,1024]{1,0:T(8,128)(2,1)S(1)}, bf16[64,1024]{1,0:T(8,128)(2,1)S(1)}) custom-call(bf16[64,128]{1,0:T(8,128)(2,1)S(1)} %add_convert_fusion.refs_0_, bf16[64,128]{1,0:T(8,128)(2,1)S(1)} %collective-permute-done.6.refs_1_, ...), custom_call_target="tpu_custom_call" | custom-call | tf_op jit(solution)/shard_map/terms/pallas_call | solution.py:423
  27.0 2.7 %collective-permute-start.11 = (bf16[64,1024]{1,0:T(8,128)(2,1)S(1)}, bf16[64,1024]{1,0:T(8,128)(2,1)S(1)}, u32[]{:S(2)}, u32[]{:S(2)}) collective-permute-start(bf16[64,1024]{1,0:T(8,128)(2,1)S(1)} %get-tuple-element.62), channel_id=1, source_target_pairs={{0,4},{4,0},{8,12},{12,8},{1,5},{5,1},{9,13},{13,9},{2,6},{6,2},{1... | collective-permute-start | bytes 393224 | tf_op jit(solution)/shard_map/ppermute | solution.py:309
  29.6 1.1 %collective-permute-start.12 = (bf16[64,1024]{1,0:T(8,128)(2,1)S(1)}, bf16[64,1024]{1,0:T(8,128)(2,1)S(1)}, u32[]{:S(2)}, u32[]{:S(2)}) collective-permute-start(bf16[64,1024]{1,0:T(8,128)(2,1)S(1)} %get-tuple-element.63), channel_id=1, source_target_pairs={{0,8},{4,12},{8,0},{12,4},{1,9},{5,13},{9,1},{13,5},{2,10},{6,14},... | collective-permute-start | bytes 393224 | tf_op jit(solution)/shard_map/ppermute | solution.py:309
  30.7 1.4 %collective-permute-start.13 = (bf16[64,1024]{1,0:T(8,128)(2,1)S(1)}, bf16[64,1024]{1,0:T(8,128)(2,1)S(1)}, u32[]{:S(2)}, u32[]{:S(2)}) collective-permute-start(bf16[64,1024]{1,0:T(8,128)(2,1)S(1)} %get-tuple-element.64), channel_id=1, source_target_pairs={{0,12},{4,8},{8,4},{12,0},{1,13},{5,9},{9,5},{13,1},{2,14},{6,10},... | collective-permute-start | bytes 393224 | tf_op jit(solution)/shard_map/ppermute | solution.py:309
  32.1 1.5 %collective-permute-start.7 = (bf16[64,1024]{1,0:T(8,128)(2,1)S(1)}, bf16[64,1024]{1,0:T(8,128)(2,1)S(1)}, u32[]{:S(2)}, u32[]{:S(2)}) collective-permute-start(bf16[64,1024]{1,0:T(8,128)(2,1)S(1)} %get-tuple-element.53.refs_0_), channel_id=1, source_target_pairs={{0,2},{1,3},{2,0},{3,1},{4,6},{5,7},{6,4},{7,5},{8,10},{9,11},{10,... | collective-permute-start | bytes 393224 | tf_op jit(solution)/shard_map/ppermute | solution.py:309
  33.6 0.5 %collective-permute-start.8 = (bf16[64,1024]{1,0:T(8,128)(2,1)S(1)}, bf16[64,1024]{1,0:T(8,128)(2,1)S(1)}, u32[]{:S(2)}, u32[]{:S(2)}) collective-permute-start(bf16[64,1024]{1,0:T(8,128)(2,1)S(1)} %get-tuple-element.54.refs_2_), channel_id=1, source_target_pairs={{0,2},{1,3},{2,0},{3,1},{4,6},{5,7},{6,4},{7,5},{8,10},{9,11},{10,... | collective-permute-start | bytes 393224 | tf_op jit(solution)/shard_map/ppermute | solution.py:309
  34.1 7.5 %collective-permute-done.12.refs_6_ = bf16[64,1024]{1,0:T(8,128)(2,1)S(1)} collective-permute-done((bf16[64,1024]{1,0:T(8,128)(2,1)S(1)}, bf16[64,1024]{1,0:T(8,128)(2,1)S(1)}, u32[]{:S(2)}, u32[]{:S(2)}) %collective-permute-start.12) | collective-permute-done | bytes 131104 | tf_op jit(solution)/shard_map/ppermute | solution.py:309
  41.6 0.2 finish.1
  41.9 0.1 collective-permute-start.14
  42.0 1.5 %collective-permute-done.14 = bf16[128,1024]{1,0:T(8,128)(2,1)S(1)} collective-permute-done((bf16[128,1024]{1,0:T(8,128)(2,1)S(1)}, bf16[128,1024]{1,0:T(8,128)(2,1)S(1)}, u32[]{:S(2)}, u32[]{:S(2)}) %collective-permute-start.14) | collective-permute-done | bytes 262176 | tf_op jit(solution)/shard_map/ppermute | solution.py:309
  43.5 0.9 %maximum_select_fusion = bf16[128,2048]{1,0:T(8,128)(2,1)} fusion(bf16[128,1024]{1,0:T(8,128)(2,1)S(1)} %collective-permute-done.14, bf16[128,1024]{1,0:T(8,128)(2,1)S(1)} %finish.1, pred[]{:T(512)S(6)} %eq.5), kind=kLoop, calls=%fused_computation | loop fusion | flops 2359296 | bytes 1048577 | tf_op jit(solution)/shard_map/jit(_where)/select_n | solution.py:453
  (19 shorter events, 0.1 us)
Async XLA Ops:
  4.3 6.7 %collective-permute-start = (bf16[4,2,16,1024]{3,2,1,0:T(8,128)(2,1)}, bf16[4,2,16,1024]{3,2,1,0:T(8,128)(2,1)S(1)}, u32[]{:S(2)}, u32[]{:S(2)}) collective-permute-start(bf16[4,2,16,1024]{3,2,1,0:T(8,128)(2,1)} %get-tuple-element.35), channel_id=1, source_target_pairs={{0,1},{1,0},{2,3},{3,2},{4,5},{5,4},{6,7},{7,6},{8,9},{9,8},{10,11... | collective-permute-start | bytes 786440 | tf_op jit(solution)/shard_map/ppermute | solution.py:309
  4.8 9.2 %collective-permute-start.1 = (bf16[32,2048]{1,0:T(8,128)(2,1)}, bf16[32,2048]{1,0:T(8,128)(2,1)S(1)}, u32[]{:S(2)}, u32[]{:S(2)}) collective-permute-start(bf16[32,2048]{1,0:T(8,128)(2,1)} %get-tuple-element.38.refs_0_), channel_id=1, source_target_pairs={{0,4},{4,0},{8,12},{12,8},{1,5},{5,1},{9,13},{13,9},{2,6},{6,2},{1... | collective-permute-start | bytes 393224 | tf_op jit(solution)/shard_map/ppermute | solution.py:309
  7.5 13.1 %collective-permute-start.2 = (bf16[32,2048]{1,0:T(8,128)(2,1)}, bf16[32,2048]{1,0:T(8,128)(2,1)S(1)}, u32[]{:S(2)}, u32[]{:S(2)}) collective-permute-start(bf16[32,2048]{1,0:T(8,128)(2,1)} %get-tuple-element.38.refs_0_), channel_id=1, source_target_pairs={{0,8},{4,12},{8,0},{12,4},{1,9},{5,13},{9,1},{13,5},{2,10},{6,14},... | collective-permute-start | bytes 393224 | tf_op jit(solution)/shard_map/ppermute | solution.py:309
  10.1 10.5 %collective-permute-start.3 = (bf16[32,2048]{1,0:T(8,128)(2,1)}, bf16[32,2048]{1,0:T(8,128)(2,1)S(1)}, u32[]{:S(2)}, u32[]{:S(2)}) collective-permute-start(bf16[32,2048]{1,0:T(8,128)(2,1)} %get-tuple-element.38.refs_0_), channel_id=1, source_target_pairs={{0,12},{4,8},{8,4},{12,0},{1,13},{5,9},{9,5},{13,1},{2,14},{6,10},... | collective-permute-start | bytes 393224 | tf_op jit(solution)/shard_map/ppermute | solution.py:309
  10.1 16.2 %collective-permute-start.10 = (bf16[4,2,16,1024]{3,2,1,0:T(8,128)(2,1)}, bf16[4,2,16,1024]{3,2,1,0:T(8,128)(2,1)S(1)}, u32[]{:S(2)}, u32[]{:S(2)}) collective-permute-start(bf16[4,2,16,1024]{3,2,1,0:T(8,128)(2,1)} %get-tuple-element.35), channel_id=1, source_target_pairs={{0,3},{1,2},{2,1},{3,0},{4,7},{5,6},{6,5},{7,4},{8,11},{9,10},{10,... | collective-permute-start | bytes 786440 | tf_op jit(solution)/shard_map/ppermute | solution.py:309
  11.1 15.2 %collective-permute-start.9 = (bf16[4,2,16,1024]{3,2,1,0:T(8,128)(2,1)}, bf16[4,2,16,1024]{3,2,1,0:T(8,128)(2,1)S(1)}, u32[]{:S(2)}, u32[]{:S(2)}) collective-permute-start(bf16[4,2,16,1024]{3,2,1,0:T(8,128)(2,1)} %get-tuple-element.59.refs_4_), channel_id=1, source_target_pairs={{0,2},{1,3},{2,0},{3,1},{4,6},{5,7},{6,4},{7,5},{8,10},{9,11},{10,... | collective-permute-start | bytes 786440 | tf_op jit(solution)/shard_map/ppermute | solution.py:309
  11.8 0.7 %copy-start.3 = (s32[128]{0:T(128)S(1)}, s32[128]{0:T(128)}, u32[]{:S(2)}) copy-start(s32[128]{0:T(128)} %param.17) | copy-start | bytes 1540
  12.5 0.7 %copy-start.4 = (s32[8]{0:T(128)S(1)}, s32[8]{0:T(128)}, u32[]{:S(2)}) copy-start(s32[8]{0:T(128)} %slots_ref.1) | copy-start | bytes 100
  14.0 1.0 %copy-start = (bf16[2,2048,64]{1,2,0:T(8,128)(2,1)S(1)}, bf16[2,2048,64]{1,2,0:T(8,128)(2,1)}, u32[]{:S(2)}) copy-start(bf16[2,2048,64]{1,2,0:T(8,128)(2,1)} %param.20) | copy-start | bytes 1572868
  15.0 0.9 %copy-start.2 = (bf16[32,2048]{1,0:T(8,128)(2,1)S(1)}, bf16[32,2048]{1,0:T(8,128)(2,1)}, u32[]{:S(2)}) copy-start(bf16[32,2048]{1,0:T(8,128)(2,1)} %get-tuple-element.38.refs_0_) | copy-start | bytes 393220
  21.1 1.4 %collective-permute-start.5 = (f32[64,128]{1,0:T(8,128)S(1)}, f32[64,128]{1,0:T(8,128)S(1)}, u32[]{:S(2)}, u32[]{:S(2)}) collective-permute-start(f32[64,128]{1,0:T(8,128)S(1)} %shrink.1), channel_id=1, source_target_pairs={{0,1},{1,0},{2,3},{3,2},{4,5},{5,4},{6,7},{7,6},{8,9},{9,8},{10,11... | collective-permute-start | bytes 98312 | tf_op jit(solution)/shard_map/ppermute | solution.py:309
  21.1 5.2 %copy-start.1 = (bf16[4,2,16,1024]{3,2,1,0:T(8,128)(2,1)S(1)}, bf16[4,2,16,1024]{3,2,1,0:T(8,128)(2,1)}, u32[]{:S(2)}) copy-start(bf16[4,2,16,1024]{3,2,1,0:T(8,128)(2,1)} %get-tuple-element.59.refs_4_) | copy-start | bytes 786436
  21.9 2.9 %collective-permute-start.4 = (bf16[128,1024]{1,0:T(8,128)(2,1)S(1)}, bf16[128,1024]{1,0:T(8,128)(2,1)S(1)}, u32[]{:S(2)}, u32[]{:S(2)}) collective-permute-start(bf16[128,1024]{1,0:T(8,128)(2,1)S(1)} %project.3), channel_id=1, source_target_pairs={{0,1},{1,0},{2,3},{3,2},{4,5},{5,4},{6,7},{7,6},{8,9},{9,8},{10,11... | collective-permute-start | bytes 786440 | tf_op jit(solution)/shard_map/ppermute | solution.py:309
  22.5 3.8 %collective-permute-start.6 = (bf16[64,128]{1,0:T(8,128)(2,1)S(1)}, bf16[64,128]{1,0:T(8,128)(2,1)S(1)}, u32[]{:S(2)}, u32[]{:S(2)}) collective-permute-start(bf16[64,128]{1,0:T(8,128)(2,1)S(1)} %add_convert_fusion.refs_0_), channel_id=1, source_target_pairs={{0,2},{1,3},{2,0},{3,1},{4,6},{5,7},{6,4},{7,5},{8,10},{9,11},{10,... | collective-permute-start | bytes 49160 | tf_op jit(solution)/shard_map/ppermute | solution.py:309
  27.0 7.2 %collective-permute-start.11 = (bf16[64,1024]{1,0:T(8,128)(2,1)S(1)}, bf16[64,1024]{1,0:T(8,128)(2,1)S(1)}, u32[]{:S(2)}, u32[]{:S(2)}) collective-permute-start(bf16[64,1024]{1,0:T(8,128)(2,1)S(1)} %get-tuple-element.62), channel_id=1, source_target_pairs={{0,4},{4,0},{8,12},{12,8},{1,5},{5,1},{9,13},{13,9},{2,6},{6,2},{1... | collective-permute-start | bytes 393224 | tf_op jit(solution)/shard_map/ppermute | solution.py:309
  29.6 12.0 %collective-permute-start.12 = (bf16[64,1024]{1,0:T(8,128)(2,1)S(1)}, bf16[64,1024]{1,0:T(8,128)(2,1)S(1)}, u32[]{:S(2)}, u32[]{:S(2)}) collective-permute-start(bf16[64,1024]{1,0:T(8,128)(2,1)S(1)} %get-tuple-element.63), channel_id=1, source_target_pairs={{0,8},{4,12},{8,0},{12,4},{1,9},{5,13},{9,1},{13,5},{2,10},{6,14},... | collective-permute-start | bytes 393224 | tf_op jit(solution)/shard_map/ppermute | solution.py:309
  30.7 10.9 %collective-permute-start.13 = (bf16[64,1024]{1,0:T(8,128)(2,1)S(1)}, bf16[64,1024]{1,0:T(8,128)(2,1)S(1)}, u32[]{:S(2)}, u32[]{:S(2)}) collective-permute-start(bf16[64,1024]{1,0:T(8,128)(2,1)S(1)} %get-tuple-element.64), channel_id=1, source_target_pairs={{0,12},{4,8},{8,4},{12,0},{1,13},{5,9},{9,5},{13,1},{2,14},{6,10},... | collective-permute-start | bytes 393224 | tf_op jit(solution)/shard_map/ppermute | solution.py:309
  32.1 9.5 %collective-permute-start.7 = (bf16[64,1024]{1,0:T(8,128)(2,1)S(1)}, bf16[64,1024]{1,0:T(8,128)(2,1)S(1)}, u32[]{:S(2)}, u32[]{:S(2)}) collective-permute-start(bf16[64,1024]{1,0:T(8,128)(2,1)S(1)} %get-tuple-element.53.refs_0_), channel_id=1, source_target_pairs={{0,2},{1,3},{2,0},{3,1},{4,6},{5,7},{6,4},{7,5},{8,10},{9,11},{10,... | collective-permute-start | bytes 393224 | tf_op jit(solution)/shard_map/ppermute | solution.py:309
  33.6 8.0 %collective-permute-start.8 = (bf16[64,1024]{1,0:T(8,128)(2,1)S(1)}, bf16[64,1024]{1,0:T(8,128)(2,1)S(1)}, u32[]{:S(2)}, u32[]{:S(2)}) collective-permute-start(bf16[64,1024]{1,0:T(8,128)(2,1)S(1)} %get-tuple-element.54.refs_2_), channel_id=1, source_target_pairs={{0,2},{1,3},{2,0},{3,1},{4,6},{5,7},{6,4},{7,5},{8,10},{9,11},{10,... | collective-permute-start | bytes 393224 | tf_op jit(solution)/shard_map/ppermute | solution.py:309
  41.9 1.6 %collective-permute-start.14 = (bf16[128,1024]{1,0:T(8,128)(2,1)S(1)}, bf16[128,1024]{1,0:T(8,128)(2,1)S(1)}, u32[]{:S(2)}, u32[]{:S(2)}) collective-permute-start(bf16[128,1024]{1,0:T(8,128)(2,1)S(1)} %finish.1), channel_id=1, source_target_pairs={{0,1},{1,0},{2,3},{3,2},{4,5},{5,4},{6,7},{7,6},{8,9},{9,8},{10,11... | collective-permute-start | bytes 786440 | tf_op jit(solution)/shard_map/ppermute | solution.py:309

commit v5 on v4

--- a/solution.py
+++ b/solution.py
@@ -169,15 +169,15 @@
     )(lengths, *moved, up)
 
 
-def blockwise(position, count, size, index):
+def blockwise(position, order, size, index):
     moved = jnp.zeros_like(position)
-    for k in range(count):
-        inside = (position >= k * size) & (position < (k + 1) * size)
-        moved = jnp.where(inside, position + ((index ^ k) - k) * size, moved)
+    for i, k in enumerate(order):
+        inside = (position >= i * size) & (position < (i + 1) * size)
+        moved = jnp.where(inside, position + ((index ^ k) - i) * size, moved)
     return moved
 
 
-def ids_kernel(n_adapter, n_tensor, ids_ref, slots_ref, here_ref, select_ref, place_ref, order_ref):
+def ids_kernel(order, n_tensor, ids_ref, slots_ref, here_ref, select_ref, place_ref, order_ref):
     tokens, per_owner = here_ref.shape
     owned = select_ref.shape[0]
     rank = order_ref.shape[0]
@@ -205,10 +205,10 @@
     slot = lax.broadcasted_iota(jnp.int32, select_ref.shape, 0) + a * owned
     select_ref[...] = jnp.where(slot == key_row, 1.0, 0.0).astype(BF)
     slot = lax.broadcasted_iota(jnp.int32, place_ref.shape, 1)
-    slot = blockwise(slot, n_adapter, owned, a)
+    slot = blockwise(slot, order, owned, a)
     place_ref[...] = jnp.where(slot == key_column, 1.0, 0.0).astype(BF)
     source = lax.broadcasted_iota(jnp.int32, order_ref.shape, 1)
-    source = blockwise(source, n_tensor, rank // n_tensor, t)
+    source = blockwise(source, range(n_tensor), rank // n_tensor, t)
     target = lax.broadcasted_iota(jnp.int32, order_ref.shape, 0)
     order_ref[...] = jnp.where(source == target, 1.0, 0.0).astype(BF)
 
@@ -217,20 +217,20 @@
     return pl.ds(pl.multiple_of((lax.axis_index("adapter") ^ k) * requests, requests), requests)
 
 
-def shrink_kernel(*refs):
+def shrink_kernel(order, *refs):
     *blocks, mask_ref, maps_ref, out_ref, total_ref = refs
     requests = blocks[0].shape[0]
     x = jnp.concatenate([b[...] for b in blocks], axis=0)
     mask = jnp.concatenate(
-        [mask_ref[block_rows(k, requests), :] for k in range(len(blocks))], axis=0
+        [mask_ref[block_rows(k, requests), :] for k in order], axis=0
     )
     total = None
     for j in range(maps_ref.shape[0]):
         part = lax.dot_general(x, maps_ref[j], (((1,), (1,)), ((), ())), preferred_element_type=F32)
         part = jnp.where(mask[:, j : j + 1] > 0, part, 0.0)
         total = part if total is None else total + part
-    for k in range(len(blocks)):
-        total_ref[block_rows(k, requests), :] = total[k * requests : (k + 1) * requests]
+    for i, k in enumerate(order):
+        total_ref[block_rows(k, requests), :] = total[i * requests : (i + 1) * requests]
     middle = total.shape[0] // 2
     out_ref[...] = jnp.concatenate([total_ref[:middle], total_ref[middle:]], axis=1)
 
@@ -267,7 +267,8 @@
         out_ref[...] = (keep_ref[part] + came_ref[part].astype(F32)).astype(BF)
 
 
-def terms_kernel(n_adapter, n_parts, *refs):
+def terms_kernel(order, n_parts, *refs):
+    n_adapter = len(order)
     parts = refs[:n_parts]
     select_ref, order_ref = refs[n_parts : n_parts + 2]
     maps = refs[n_parts + 2 : -n_adapter]
@@ -285,23 +286,22 @@
     wide = jnp.concatenate(
         [jnp.where(slot_of == j, held, 0.0) for j in range(per_owner)], axis=1
     ).astype(BF)
-    for k in range(n_adapter):
+    for out, k in zip(outs, order):
         up = jnp.concatenate([m[a ^ k, j] for j in range(per_owner) for m in maps], axis=0)
-        outs[k][...] = jnp.dot(wide, up, preferred_element_type=F32).astype(BF)
-
-
-def finish_kernel(requests, place_ref, *refs):
+        out[...] = jnp.dot(wide, up, preferred_element_type=F32).astype(BF)
+
+
+def finish_kernel(requests, order, place_ref, *refs):
     *base, out_ref = refs
     base, pieces = base[:4], base[4:]
-    blocks = range(out_ref.shape[0] // requests)
     received = jnp.concatenate([p[...] for p in pieces], axis=0)
-    place = jnp.concatenate([place_ref[block_rows(k, requests), :] for k in blocks], axis=0)
+    place = jnp.concatenate([place_ref[block_rows(k, requests), :] for k in order], axis=0)
     delta = jnp.dot(place, received, preferred_element_type=F32)
     base = [b[...].astype(F32) for b in base]
     total = jnp.concatenate([base[0] + base[1], base[2] + base[3]], axis=0)
     total = (total + ADAPTER_SCALE * delta).astype(BF)
-    for k in blocks:
-        out_ref[block_rows(k, requests), :] = total[k * requests : (k + 1) * requests]
+    for i, k in enumerate(order):
+        out_ref[block_rows(k, requests), :] = total[i * requests : (i + 1) * requests]
 
 
 def make_shards(n_adapter, n_tensor):
@@ -329,6 +329,7 @@
         requests = queries.shape[0]
         tokens = adapter_ids.shape[0]
         owned = per_owner * SLOTS
+        order = sorted(range(n_adapter), key=lambda k: (k != 0, k != 2, k))
 
         attended, up_low, up_high = attend(
             queries,
@@ -340,7 +341,7 @@
             expand_weight,
             n_adapter,
         )
-        blocks = [swap(attended, "adapter", n_adapter, k) for k in range(1, n_adapter)]
+        blocks = [swap(attended, "adapter", n_adapter, k) for k in order[1:]]
 
         maps = [up_low] + [
             swap((up_low, up_high)[k % 2], "tensor", n_tensor, k) for k in range(1, n_tensor)
@@ -349,7 +350,7 @@
         ids, maps[1] = lax.optimization_barrier((ids, maps[1]))
 
         here, select, place, reorder = pl.pallas_call(
-            functools.partial(ids_kernel, n_adapter, n_tensor),
+            functools.partial(ids_kernel, order, n_tensor),
             out_shape=[
                 jax.ShapeDtypeStruct((tokens, per_owner), F32),
                 jax.ShapeDtypeStruct((owned, tokens), BF),
@@ -362,7 +363,7 @@
             name="ids",
         )(ids, adapter_slots)
 
-        out_weight, here, blocks[0] = lax.optimization_barrier((out_weight, here, blocks[0]))
+        out_weight, here = lax.optimization_barrier((out_weight, here))
 
         loads = (attended, out_weight, jnp.swapaxes(shrink_weight, 1, 2))
         here_block, weight, down = pl.pallas_call(
@@ -380,7 +381,7 @@
         blocks = [here_block] + blocks
 
         shrunk = pl.pallas_call(
-            shrink_kernel,
+            functools.partial(shrink_kernel, order),
             out_shape=jax.ShapeDtypeStruct((tokens // 2, 2 * rank), F32),
             in_specs=[VMEM] * (n_adapter + 2),
             out_specs=VMEM,
@@ -421,7 +422,7 @@
         base, shrunk = base[:2], base[2:]
 
         terms = pl.pallas_call(
-            functools.partial(terms_kernel, n_adapter, len(shrunk)),
+            functools.partial(terms_kernel, order, len(shrunk)),
             out_shape=[jax.ShapeDtypeStruct((owned, half), BF)] * n_adapter,
             in_specs=[VMEM] * (2 + len(shrunk) + len(maps)),
             out_specs=[VMEM] * n_adapter,
@@ -429,7 +430,7 @@
             name="terms",
         )(*shrunk, select, reorder, *maps)
         received = [terms[0]] + [
-            swap(terms[k], "adapter", n_adapter, k) for k in range(1, n_adapter)
+            swap(term, "adapter", n_adapter, k) for term, k in zip(terms[1:], order[1:])
         ]
 
         sums = []
@@ -442,7 +443,7 @@
             sums += [part, swap(part, "tensor", n_tensor, step)]
 
         mine = pl.pallas_call(
-            functools.partial(finish_kernel, requests),
+            functools.partial(finish_kernel, requests, order),
             out_shape=jax.ShapeDtypeStruct((tokens, half), BF),
             in_specs=[VMEM] * (5 + n_adapter),
             out_specs=VMEM,

time: 44.7 us -> 42.6 us (0.953)
  waiting for transfers between devices: 11.7 us -> 8.92 us
  starting transfers between devices: 16.8 us -> 17.5 us
    ppermute x15, waiting for transfers between devices: 11.7 us -> 8.92 us  [swap(): return lax.ppermute(x, axis, [(i, i ^ k) for i in range(n)])]
    ppermute x15, starting transfers between devices: 16.8 us -> 17.5 us  [swap(): return lax.ppermute(x, axis, [(i, i ^ k) for i in range(n)])]
  transfers between devices with their start and end apart: 15 -> 15, of which waited for: 5 -> 5; matrix products, arithmetic and copies ran while one was open for 0% -> 0% of each run, Pallas kernels for 14% -> 15%
where the time goes in v5:
time: 42.6 us; the launch traced here: 42.4 us
  starting transfers between devices  17.5 us (41%)
  Pallas kernels  11.6 us (27%)
  waiting for transfers between devices  8.92 us (21%)
  local copies, waits for them, and re-layouts  3.26 us (8%)
  other arithmetic  0.93 us (2%)
    ppermute x15, starting transfers between devices, swap(): return lax.ppermute(x, axis, [(i, i ^ k) for i in range(n)])  17.5 us
    ppermute x15, waiting for transfers between devices, swap(): return lax.ppermute(x, axis, [(i, i ^ k) for i in range(n)])  8.92 us
    pallas_call x1, Pallas kernels, attend(): pl.pallas_call(functools.partial(attend_kernel, chunk), out_shape=[jax.Sh...  4.31 us
    pallas_call x1, Pallas kernels, shards(): pl.pallas_call(load_kernel, out_shape=[jax.ShapeDtypeStruct(x.shape, BF)...  3.54 us
    unnamed x10, local copies, waits for them, and re-layouts  3.26 us
    pallas_call x2, Pallas kernels, project(): pl.pallas_call(functools.partial(project_kernel, other), out_shape=jax.Sh...  1.54 us
    select_n x1, other arithmetic, shards(): jnp.where(low == 0, jnp.concatenate([mine, other], axis=1), jnp.concatena...  0.92 us
  transfers between devices with their start and end apart: 15, of which 5 were waited for; matrix products, arithmetic and copies ran while one was open for 0% of the time, Pallas kernels for 15%

profile of v5, /device:TPU:0, one launch (start us, length us, event | category | flops | bytes accessed | tf_op | source)
XLA Modules:
  0.0 42.4 jit_solution(17398181209033624045)
XLA Ops:
  0.0 4.3 %attend.1 = (bf16[32,2048]{1,0:T(8,128)(2,1)}, bf16[4,2,16,1024]{3,2,1,0:T(8,128)(2,1)}, bf16[4,2,16,1024]{3,2,1,0:T(8,128)(2,1)}) custom-call(s32[32]{0:T(128)} %length_ref.1, bf16[32,2048]{1,0:T(8,128)(2,1)} %q_hbm.1, bf16[32,64,256]{2,1,0:T(8,128)(2,1)} %k_hbm.1, bf16[32,64,256]{2,1,0:T(8,128)(2,1)} %v_hbm.1, bf16[32,256]{1,0:T(8,128)(2,1)} %nk_hbm.1, ...), custom_call_target="tpu_custom_call" | custom-call | flops 33554432 | bytes 2097152 | tf_op jit(solution)/shard_map/attend/pallas_call | solution.py:151
  4.3 0.5 %collective-permute-start = (bf16[4,2,16,1024]{3,2,1,0:T(8,128)(2,1)}, bf16[4,2,16,1024]{3,2,1,0:T(8,128)(2,1)S(1)}, u32[]{:S(2)}, u32[]{:S(2)}) collective-permute-start(bf16[4,2,16,1024]{3,2,1,0:T(8,128)(2,1)} %get-tuple-element.34), channel_id=1, source_target_pairs={{0,1},{1,0},{2,3},{3,2},{4,5},{5,4},{6,7},{7,6},{8,9},{9,8},{10,11... | collective-permute-start | bytes 786440 | tf_op jit(solution)/shard_map/ppermute | solution.py:309
  4.8 3.7 %collective-permute-start.1 = (bf16[32,2048]{1,0:T(8,128)(2,1)}, bf16[32,2048]{1,0:T(8,128)(2,1)S(1)}, u32[]{:S(2)}, u32[]{:S(2)}) collective-permute-start(bf16[32,2048]{1,0:T(8,128)(2,1)} %get-tuple-element.37.refs_0_), channel_id=1, source_target_pairs={{0,8},{4,12},{8,0},{12,4},{1,9},{5,13},{9,1},{13,5},{2,10},{6,14},... | collective-permute-start | bytes 393224 | tf_op jit(solution)/shard_map/ppermute | solution.py:309
  8.5 1.6 %collective-permute-start.2 = (bf16[32,2048]{1,0:T(8,128)(2,1)}, bf16[32,2048]{1,0:T(8,128)(2,1)S(1)}, u32[]{:S(2)}, u32[]{:S(2)}) collective-permute-start(bf16[32,2048]{1,0:T(8,128)(2,1)} %get-tuple-element.37.refs_0_), channel_id=1, source_target_pairs={{0,4},{4,0},{8,12},{12,8},{1,5},{5,1},{9,13},{13,9},{2,6},{6,2},{1... | collective-permute-start | bytes 393224 | tf_op jit(solution)/shard_map/ppermute | solution.py:309
  10.1 1.0 %collective-permute-start.10 = (bf16[4,2,16,1024]{3,2,1,0:T(8,128)(2,1)}, bf16[4,2,16,1024]{3,2,1,0:T(8,128)(2,1)S(1)}, u32[]{:S(2)}, u32[]{:S(2)}) collective-permute-start(bf16[4,2,16,1024]{3,2,1,0:T(8,128)(2,1)} %get-tuple-element.34), channel_id=1, source_target_pairs={{0,3},{1,2},{2,1},{3,0},{4,7},{5,6},{6,5},{7,4},{8,11},{9,10},{10,... | collective-permute-start | bytes 786440 | tf_op jit(solution)/shard_map/ppermute | solution.py:309
  11.1 0.8 %collective-permute-start.9 = (bf16[4,2,16,1024]{3,2,1,0:T(8,128)(2,1)}, bf16[4,2,16,1024]{3,2,1,0:T(8,128)(2,1)S(1)}, u32[]{:S(2)}, u32[]{:S(2)}) collective-permute-start(bf16[4,2,16,1024]{3,2,1,0:T(8,128)(2,1)} %get-tuple-element.57.refs_4_), channel_id=1, source_target_pairs={{0,2},{1,3},{2,0},{3,1},{4,6},{5,7},{6,4},{7,5},{8,10},{9,11},{10,... | collective-permute-start | bytes 786440 | tf_op jit(solution)/shard_map/ppermute | solution.py:309
  11.8 0.7 %copy-done.3 = s32[128]{0:T(128)S(1)} copy-done((s32[128]{0:T(128)S(1)}, s32[128]{0:T(128)}, u32[]{:S(2)}) %copy-start.3) | copy-done | bytes 536
  12.5 0.7 %copy-done.4 = s32[8]{0:T(128)S(1)} copy-done((s32[8]{0:T(128)S(1)}, s32[8]{0:T(128)}, u32[]{:S(2)}) %copy-start.4) | copy-done | bytes 56
  13.1 0.7 %ids.1 = (f32[128,2]{1,0:T(8,128)S(1)}, bf16[64,128]{1,0:T(8,128)(2,1)S(1)}, bf16[128,256]{1,0:T(8,128)(2,1)S(1)}, bf16[64,64]{1,0:T(8,128)(2,1)S(1)}) custom-call(s32[1,128]{1,0:T(1,128)S(1)} %bitcast.3, s32[8]{0:T(128)S(1)} %copy-done.4), custom_call_target="tpu_custom_call" | custom-call | tf_op jit(solution)/shard_map/ids/pallas_call | solution.py:352
  13.9 0.0 copy-start
  13.9 1.0 %copy-done = bf16[2,2048,64]{1,2,0:T(8,128)(2,1)S(1)} copy-done((bf16[2,2048,64]{1,2,0:T(8,128)(2,1)S(1)}, bf16[2,2048,64]{1,2,0:T(8,128)(2,1)}, u32[]{:S(2)}) %copy-start) | copy-done | bytes 524312
  14.9 0.9 %copy-done.2 = bf16[32,2048]{1,0:T(8,128)(2,1)S(1)} copy-done((bf16[32,2048]{1,0:T(8,128)(2,1)S(1)}, bf16[32,2048]{1,0:T(8,128)(2,1)}, u32[]{:S(2)}) %copy-start.2) | copy-done | bytes 131096
  15.8 3.5 %load.1 = (bf16[32,2048]{1,0:T(8,128)(2,1)S(1)}, bf16[2048,2048]{1,0:T(8,128)(2,1)S(1)}, bf16[2,64,2048]{2,1,0:T(8,128)(2,1)S(1)}) custom-call(bf16[32,2048]{1,0:T(8,128)(2,1)S(1)} %copy-done.2, bf16[2048,2048]{1,0:T(8,128)(2,1)} %refs_1_, bf16[2,64,2048]{2,1,0:T(8,128)(2,1)S(1)} %bitcast.2), custom_call_target="tpu_custom_call" | custom-call | bytes 16777216 | tf_op jit(solution)/shard_map/load/pallas_call | solution.py:369
  19.4 0.3 collective-permute-done.3.refs_3_
  19.6 0.5 %shrink.1 = f32[64,128]{1,0:T(8,128)S(1)} custom-call(bf16[32,2048]{1,0:T(8,128)(2,1)S(1)} %get-tuple-element.43.refs_0_, bf16[32,2048]{1,0:T(8,128)(2,1)S(1)} %collective-permute-done.1.refs_1_, bf16[32,2048]{1,0:T(8,128)(2,1)S(1)} %collective-permute-done.2.refs_2_, bf16[32,2048]{1,0:T(8,128)(2,1)S(1)} %collective-permute-done.3.refs_3_, ...), custom_call_target="tpu_custom_call" | custom-call | tf_op jit(solution)/shard_map/shrink/pallas_call | solution.py:383
  20.1 0.0 collective-permute-start.5
  20.2 0.8 %project.3 = bf16[128,1024]{1,0:T(8,128)(2,1)S(1)} custom-call(bf16[32,2048]{1,0:T(8,128)(2,1)S(1)} %get-tuple-element.43.refs_0_, bf16[32,2048]{1,0:T(8,128)(2,1)S(1)} %collective-permute-done.1.refs_1_, bf16[32,2048]{1,0:T(8,128)(2,1)S(1)} %collective-permute-done.2.refs_2_, bf16[32,2048]{1,0:T(8,128)(2,1)S(1)} %collective-permute-done.3.refs_3_, ...), custom_call_target="tpu_custom_call" | custom-call | flops 536870912 | bytes 8388608 | tf_op jit(solution)/shard_map/project/pallas_call | solution.py:398
  21.0 0.5 %collective-permute-start.4 = (bf16[128,1024]{1,0:T(8,128)(2,1)S(1)}, bf16[128,1024]{1,0:T(8,128)(2,1)S(1)}, u32[]{:S(2)}, u32[]{:S(2)}) collective-permute-start(bf16[128,1024]{1,0:T(8,128)(2,1)S(1)} %project.3), channel_id=1, source_target_pairs={{0,1},{1,0},{2,3},{3,2},{4,5},{5,4},{6,7},{7,6},{8,9},{9,8},{10,11... | collective-permute-start | bytes 786440 | tf_op jit(solution)/shard_map/ppermute | solution.py:309
  21.5 1.6 %collective-permute-start.6 = (bf16[64,128]{1,0:T(8,128)(2,1)S(1)}, bf16[64,128]{1,0:T(8,128)(2,1)S(1)}, u32[]{:S(2)}, u32[]{:S(2)}) collective-permute-start(bf16[64,128]{1,0:T(8,128)(2,1)S(1)} %add_convert_fusion.refs_0_), channel_id=1, source_target_pairs={{0,2},{1,3},{2,0},{3,1},{4,6},{5,7},{6,4},{7,5},{8,10},{9,11},{10,... | collective-permute-start | bytes 49160 | tf_op jit(solution)/shard_map/ppermute | solution.py:309
  23.1 0.8 %project.2.keep_ref = f32[128,1024]{1,0:T(8,128)S(1)} custom-call(bf16[32,2048]{1,0:T(8,128)(2,1)S(1)} %get-tuple-element.43.refs_0_, bf16[32,2048]{1,0:T(8,128)(2,1)S(1)} %collective-permute-done.1.refs_1_, bf16[32,2048]{1,0:T(8,128)(2,1)S(1)} %collective-permute-done.2.refs_2_, bf16[32,2048]{1,0:T(8,128)(2,1)S(1)} %collective-permute-done.3.refs_3_, ...), custom_call_target="tpu_custom_call" | custom-call | flops 536870912 | bytes 8388608 | tf_op jit(solution)/shard_map/project/pallas_call | solution.py:398
  23.9 1.4 %collective-permute-done.6.refs_1_ = bf16[64,128]{1,0:T(8,128)(2,1)S(1)} collective-permute-done((bf16[64,128]{1,0:T(8,128)(2,1)S(1)}, bf16[64,128]{1,0:T(8,128)(2,1)S(1)}, u32[]{:S(2)}, u32[]{:S(2)}) %collective-permute-start.6) | collective-permute-done | bytes 16416 | tf_op jit(solution)/shard_map/ppermute | solution.py:309
  25.3 0.7 %terms.1 = (bf16[64,1024]{1,0:T(8,128)(2,1)S(1)}, bf16[64,1024]{1,0:T(8,128)(2,1)S(1)}, bf16[64,1024]{1,0:T(8,128)(2,1)S(1)}, bf16[64,1024]{1,0:T(8,128)(2,1)S(1)}) custom-call(bf16[64,128]{1,0:T(8,128)(2,1)S(1)} %add_convert_fusion.refs_0_, bf16[64,128]{1,0:T(8,128)(2,1)S(1)} %collective-permute-done.6.refs_1_, ...), custom_call_target="tpu_custom_call" | custom-call | tf_op jit(solution)/shard_map/terms/pallas_call | solution.py:424
  26.0 4.3 %collective-permute-start.11 = (bf16[64,1024]{1,0:T(8,128)(2,1)S(1)}, bf16[64,1024]{1,0:T(8,128)(2,1)S(1)}, u32[]{:S(2)}, u32[]{:S(2)}) collective-permute-start(bf16[64,1024]{1,0:T(8,128)(2,1)S(1)} %get-tuple-element.60), channel_id=1, source_target_pairs={{0,8},{4,12},{8,0},{12,4},{1,9},{5,13},{9,1},{13,5},{2,10},{6,14},... | collective-permute-start | bytes 393224 | tf_op jit(solution)/shard_map/ppermute | solution.py:309
  30.3 1.5 %collective-permute-start.13 = (bf16[64,1024]{1,0:T(8,128)(2,1)S(1)}, bf16[64,1024]{1,0:T(8,128)(2,1)S(1)}, u32[]{:S(2)}, u32[]{:S(2)}) collective-permute-start(bf16[64,1024]{1,0:T(8,128)(2,1)S(1)} %get-tuple-element.62), channel_id=1, source_target_pairs={{0,12},{4,8},{8,4},{12,0},{1,13},{5,9},{9,5},{13,1},{2,14},{6,10},... | collective-permute-start | bytes 393224 | tf_op jit(solution)/shard_map/ppermute | solution.py:309
  31.8 1.5 %collective-permute-start.7 = (bf16[64,1024]{1,0:T(8,128)(2,1)S(1)}, bf16[64,1024]{1,0:T(8,128)(2,1)S(1)}, u32[]{:S(2)}, u32[]{:S(2)}) collective-permute-start(bf16[64,1024]{1,0:T(8,128)(2,1)S(1)} %get-tuple-element.51.refs_0_), channel_id=1, source_target_pairs={{0,2},{1,3},{2,0},{3,1},{4,6},{5,7},{6,4},{7,5},{8,10},{9,11},{10,... | collective-permute-start | bytes 393224 | tf_op jit(solution)/shard_map/ppermute | solution.py:309
  33.3 0.5 %collective-permute-start.8 = (bf16[64,1024]{1,0:T(8,128)(2,1)S(1)}, bf16[64,1024]{1,0:T(8,128)(2,1)S(1)}, u32[]{:S(2)}, u32[]{:S(2)}) collective-permute-start(bf16[64,1024]{1,0:T(8,128)(2,1)S(1)} %get-tuple-element.52.refs_2_), channel_id=1, source_target_pairs={{0,2},{1,3},{2,0},{3,1},{4,6},{5,7},{6,4},{7,5},{8,10},{9,11},{10,... | collective-permute-start | bytes 393224 | tf_op jit(solution)/shard_map/ppermute | solution.py:309
  33.9 3.7 %collective-permute-done.11.refs_5_ = bf16[64,1024]{1,0:T(8,128)(2,1)S(1)} collective-permute-done((bf16[64,1024]{1,0:T(8,128)(2,1)S(1)}, bf16[64,1024]{1,0:T(8,128)(2,1)S(1)}, u32[]{:S(2)}, u32[]{:S(2)}) %collective-permute-start.11) | collective-permute-done | bytes 131104 | tf_op jit(solution)/shard_map/ppermute | solution.py:309
  37.5 2.0 %collective-permute-done.12.refs_6_ = bf16[64,1024]{1,0:T(8,128)(2,1)S(1)} collective-permute-done((bf16[64,1024]{1,0:T(8,128)(2,1)S(1)}, bf16[64,1024]{1,0:T(8,128)(2,1)S(1)}, u32[]{:S(2)}, u32[]{:S(2)}) %collective-permute-start.12) | collective-permute-done | bytes 131104 | tf_op jit(solution)/shard_map/ppermute | solution.py:309
  39.6 0.2 finish.1
  39.8 0.1 collective-permute-start.14
  39.9 1.5 %collective-permute-done.14 = bf16[128,1024]{1,0:T(8,128)(2,1)S(1)} collective-permute-done((bf16[128,1024]{1,0:T(8,128)(2,1)S(1)}, bf16[128,1024]{1,0:T(8,128)(2,1)S(1)}, u32[]{:S(2)}, u32[]{:S(2)}) %collective-permute-start.14) | collective-permute-done | bytes 262176 | tf_op jit(solution)/shard_map/ppermute | solution.py:309
  41.4 0.9 %maximum_select_fusion = bf16[128,2048]{1,0:T(8,128)(2,1)} fusion(bf16[128,1024]{1,0:T(8,128)(2,1)S(1)} %collective-permute-done.14, bf16[128,1024]{1,0:T(8,128)(2,1)S(1)} %finish.1, pred[]{:T(512)S(6)} %eq.5), kind=kLoop, calls=%fused_computation | loop fusion | flops 2359296 | bytes 1048577 | tf_op jit(solution)/shard_map/jit(_where)/select_n | solution.py:454
  (19 shorter events, 0.1 us)
Async XLA Ops:
  4.3 6.7 %collective-permute-start = (bf16[4,2,16,1024]{3,2,1,0:T(8,128)(2,1)}, bf16[4,2,16,1024]{3,2,1,0:T(8,128)(2,1)S(1)}, u32[]{:S(2)}, u32[]{:S(2)}) collective-permute-start(bf16[4,2,16,1024]{3,2,1,0:T(8,128)(2,1)} %get-tuple-element.34), channel_id=1, source_target_pairs={{0,1},{1,0},{2,3},{3,2},{4,5},{5,4},{6,7},{7,6},{8,9},{9,8},{10,11... | collective-permute-start | bytes 786440 | tf_op jit(solution)/shard_map/ppermute | solution.py:309
  4.8 14.5 %collective-permute-start.1 = (bf16[32,2048]{1,0:T(8,128)(2,1)}, bf16[32,2048]{1,0:T(8,128)(2,1)S(1)}, u32[]{:S(2)}, u32[]{:S(2)}) collective-permute-start(bf16[32,2048]{1,0:T(8,128)(2,1)} %get-tuple-element.37.refs_0_), channel_id=1, source_target_pairs={{0,8},{4,12},{8,0},{12,4},{1,9},{5,13},{9,1},{13,5},{2,10},{6,14},... | collective-permute-start | bytes 393224 | tf_op jit(solution)/shard_map/ppermute | solution.py:309
  8.5 10.9 %collective-permute-start.2 = (bf16[32,2048]{1,0:T(8,128)(2,1)}, bf16[32,2048]{1,0:T(8,128)(2,1)S(1)}, u32[]{:S(2)}, u32[]{:S(2)}) collective-permute-start(bf16[32,2048]{1,0:T(8,128)(2,1)} %get-tuple-element.37.refs_0_), channel_id=1, source_target_pairs={{0,4},{4,0},{8,12},{12,8},{1,5},{5,1},{9,13},{13,9},{2,6},{6,2},{1... | collective-permute-start | bytes 393224 | tf_op jit(solution)/shard_map/ppermute | solution.py:309
  10.1 9.6 %collective-permute-start.3 = (bf16[32,2048]{1,0:T(8,128)(2,1)}, bf16[32,2048]{1,0:T(8,128)(2,1)S(1)}, u32[]{:S(2)}, u32[]{:S(2)}) collective-permute-start(bf16[32,2048]{1,0:T(8,128)(2,1)} %get-tuple-element.37.refs_0_), channel_id=1, source_target_pairs={{0,12},{4,8},{8,4},{12,0},{1,13},{5,9},{9,5},{13,1},{2,14},{6,10},... | collective-permute-start | bytes 393224 | tf_op jit(solution)/shard_map/ppermute | solution.py:309
  10.1 15.2 %collective-permute-start.10 = (bf16[4,2,16,1024]{3,2,1,0:T(8,128)(2,1)}, bf16[4,2,16,1024]{3,2,1,0:T(8,128)(2,1)S(1)}, u32[]{:S(2)}, u32[]{:S(2)}) collective-permute-start(bf16[4,2,16,1024]{3,2,1,0:T(8,128)(2,1)} %get-tuple-element.34), channel_id=1, source_target_pairs={{0,3},{1,2},{2,1},{3,0},{4,7},{5,6},{6,5},{7,4},{8,11},{9,10},{10,... | collective-permute-start | bytes 786440 | tf_op jit(solution)/shard_map/ppermute | solution.py:309
  11.1 14.3 %collective-permute-start.9 = (bf16[4,2,16,1024]{3,2,1,0:T(8,128)(2,1)}, bf16[4,2,16,1024]{3,2,1,0:T(8,128)(2,1)S(1)}, u32[]{:S(2)}, u32[]{:S(2)}) collective-permute-start(bf16[4,2,16,1024]{3,2,1,0:T(8,128)(2,1)} %get-tuple-element.57.refs_4_), channel_id=1, source_target_pairs={{0,2},{1,3},{2,0},{3,1},{4,6},{5,7},{6,4},{7,5},{8,10},{9,11},{10,... | collective-permute-start | bytes 786440 | tf_op jit(solution)/shard_map/ppermute | solution.py:309
  11.8 0.7 %copy-start.3 = (s32[128]{0:T(128)S(1)}, s32[128]{0:T(128)}, u32[]{:S(2)}) copy-start(s32[128]{0:T(128)} %param.17) | copy-start | bytes 1540
  12.5 0.7 %copy-start.4 = (s32[8]{0:T(128)S(1)}, s32[8]{0:T(128)}, u32[]{:S(2)}) copy-start(s32[8]{0:T(128)} %slots_ref.1) | copy-start | bytes 100
  13.9 1.0 %copy-start = (bf16[2,2048,64]{1,2,0:T(8,128)(2,1)S(1)}, bf16[2,2048,64]{1,2,0:T(8,128)(2,1)}, u32[]{:S(2)}) copy-start(bf16[2,2048,64]{1,2,0:T(8,128)(2,1)} %param.20) | copy-start | bytes 1572868
  14.9 0.9 %copy-start.2 = (bf16[32,2048]{1,0:T(8,128)(2,1)S(1)}, bf16[32,2048]{1,0:T(8,128)(2,1)}, u32[]{:S(2)}) copy-start(bf16[32,2048]{1,0:T(8,128)(2,1)} %get-tuple-element.37.refs_0_) | copy-start | bytes 393220
  20.1 1.4 %collective-permute-start.5 = (f32[64,128]{1,0:T(8,128)S(1)}, f32[64,128]{1,0:T(8,128)S(1)}, u32[]{:S(2)}, u32[]{:S(2)}) collective-permute-start(f32[64,128]{1,0:T(8,128)S(1)} %shrink.1), channel_id=1, source_target_pairs={{0,1},{1,0},{2,3},{3,2},{4,5},{5,4},{6,7},{7,6},{8,9},{9,8},{10,11... | collective-permute-start | bytes 98312 | tf_op jit(solution)/shard_map/ppermute | solution.py:309
  20.2 5.2 %copy-start.1 = (bf16[4,2,16,1024]{3,2,1,0:T(8,128)(2,1)S(1)}, bf16[4,2,16,1024]{3,2,1,0:T(8,128)(2,1)}, u32[]{:S(2)}) copy-start(bf16[4,2,16,1024]{3,2,1,0:T(8,128)(2,1)} %get-tuple-element.57.refs_4_) | copy-start | bytes 786436
  21.0 2.9 %collective-permute-start.4 = (bf16[128,1024]{1,0:T(8,128)(2,1)S(1)}, bf16[128,1024]{1,0:T(8,128)(2,1)S(1)}, u32[]{:S(2)}, u32[]{:S(2)}) collective-permute-start(bf16[128,1024]{1,0:T(8,128)(2,1)S(1)} %project.3), channel_id=1, source_target_pairs={{0,1},{1,0},{2,3},{3,2},{4,5},{5,4},{6,7},{7,6},{8,9},{9,8},{10,11... | collective-permute-start | bytes 786440 | tf_op jit(solution)/shard_map/ppermute | solution.py:309
  21.5 3.8 %collective-permute-start.6 = (bf16[64,128]{1,0:T(8,128)(2,1)S(1)}, bf16[64,128]{1,0:T(8,128)(2,1)S(1)}, u32[]{:S(2)}, u32[]{:S(2)}) collective-permute-start(bf16[64,128]{1,0:T(8,128)(2,1)S(1)} %add_convert_fusion.refs_0_), channel_id=1, source_target_pairs={{0,2},{1,3},{2,0},{3,1},{4,6},{5,7},{6,4},{7,5},{8,10},{9,11},{10,... | collective-permute-start | bytes 49160 | tf_op jit(solution)/shard_map/ppermute | solution.py:309
  26.0 11.5 %collective-permute-start.11 = (bf16[64,1024]{1,0:T(8,128)(2,1)S(1)}, bf16[64,1024]{1,0:T(8,128)(2,1)S(1)}, u32[]{:S(2)}, u32[]{:S(2)}) collective-permute-start(bf16[64,1024]{1,0:T(8,128)(2,1)S(1)} %get-tuple-element.60), channel_id=1, source_target_pairs={{0,8},{4,12},{8,0},{12,4},{1,9},{5,13},{9,1},{13,5},{2,10},{6,14},... | collective-permute-start | bytes 393224 | tf_op jit(solution)/shard_map/ppermute | solution.py:309
  30.3 9.3 %collective-permute-start.12 = (bf16[64,1024]{1,0:T(8,128)(2,1)S(1)}, bf16[64,1024]{1,0:T(8,128)(2,1)S(1)}, u32[]{:S(2)}, u32[]{:S(2)}) collective-permute-start(bf16[64,1024]{1,0:T(8,128)(2,1)S(1)} %get-tuple-element.61), channel_id=1, source_target_pairs={{0,4},{4,0},{8,12},{12,8},{1,5},{5,1},{9,13},{13,9},{2,6},{6,2},{1... | collective-permute-start | bytes 393224 | tf_op jit(solution)/shard_map/ppermute | solution.py:309
  30.3 9.3 %collective-permute-start.13 = (bf16[64,1024]{1,0:T(8,128)(2,1)S(1)}, bf16[64,1024]{1,0:T(8,128)(2,1)S(1)}, u32[]{:S(2)}, u32[]{:S(2)}) collective-permute-start(bf16[64,1024]{1,0:T(8,128)(2,1)S(1)} %get-tuple-element.62), channel_id=1, source_target_pairs={{0,12},{4,8},{8,4},{12,0},{1,13},{5,9},{9,5},{13,1},{2,14},{6,10},... | collective-permute-start | bytes 393224 | tf_op jit(solution)/shard_map/ppermute | solution.py:309
  31.8 7.7 %collective-permute-start.7 = (bf16[64,1024]{1,0:T(8,128)(2,1)S(1)}, bf16[64,1024]{1,0:T(8,128)(2,1)S(1)}, u32[]{:S(2)}, u32[]{:S(2)}) collective-permute-start(bf16[64,1024]{1,0:T(8,128)(2,1)S(1)} %get-tuple-element.51.refs_0_), channel_id=1, source_target_pairs={{0,2},{1,3},{2,0},{3,1},{4,6},{5,7},{6,4},{7,5},{8,10},{9,11},{10,... | collective-permute-start | bytes 393224 | tf_op jit(solution)/shard_map/ppermute | solution.py:309
  33.3 6.2 %collective-permute-start.8 = (bf16[64,1024]{1,0:T(8,128)(2,1)S(1)}, bf16[64,1024]{1,0:T(8,128)(2,1)S(1)}, u32[]{:S(2)}, u32[]{:S(2)}) collective-permute-start(bf16[64,1024]{1,0:T(8,128)(2,1)S(1)} %get-tuple-element.52.refs_2_), channel_id=1, source_target_pairs={{0,2},{1,3},{2,0},{3,1},{4,6},{5,7},{6,4},{7,5},{8,10},{9,11},{10,... | collective-permute-start | bytes 393224 | tf_op jit(solution)/shard_map/ppermute | solution.py:309
  39.8 1.6 %collective-permute-start.14 = (bf16[128,1024]{1,0:T(8,128)(2,1)S(1)}, bf16[128,1024]{1,0:T(8,128)(2,1)S(1)}, u32[]{:S(2)}, u32[]{:S(2)}) collective-permute-start(bf16[128,1024]{1,0:T(8,128)(2,1)S(1)} %finish.1), channel_id=1, source_target_pairs={{0,1},{1,0},{2,3},{3,2},{4,5},{5,4},{6,7},{7,6},{8,9},{9,8},{10,11... | collective-permute-start | bytes 786440 | tf_op jit(solution)/shard_map/ppermute | solution.py:309

commit v6 on v5

--- a/solution.py
+++ b/solution.py
@@ -72,11 +72,11 @@
         pltpu.make_async_copy(v_hbm.at[part], v_ref.at[part], sems.at[1, i])
         for i, part in enumerate(parts)
     ]
+    keys[0].start()
     for copy in small:
         copy.start()
-    for key, value in zip(keys, values):
-        key.start()
-        value.start()
+    for copy in keys[1:] + values:
+        copy.start()
     for copy in cuts:
         copy.start()
 
@@ -92,11 +92,6 @@
         pltpu.make_async_copy(high_ref, high_hbm, put_sems.at[1]),
     ]
     for c, first in enumerate(range(0, requests, chunk)):
-        if first + chunk >= requests:
-            for copy in cuts:
-                copy.wait()
-            for copy in puts:
-                copy.start()
         q = q_ref[first : first + chunk].reshape(chunk, heads, HEAD_SIZE)
         new_keys = nk_ref[first : first + chunk]
         new_values = nv_ref[first : first + chunk]
@@ -118,6 +113,11 @@
         scores = jnp.stack(scores).reshape(chunk * heads, extended)
         powers = jnp.exp(scores - jnp.max(scores, axis=1, keepdims=True)).astype(BF)
         inverse = 1.0 / jnp.dot(powers, ones, preferred_element_type=F32)
+        if c == 0:
+            for copy in cuts:
+                copy.wait()
+            for copy in puts:
+                copy.start()
         values[c].wait()
         outs = []
         for i in range(chunk):
@@ -304,6 +304,18 @@
         out_ref[block_rows(k, requests), :] = total[i * requests : (i + 1) * requests]
 
 
+def beside_kernel(mine_ref, other_ref, out_ref):
+    own = pl.program_id(0) == lax.rem(lax.axis_index("tensor"), 2)
+
+    @pl.when(own)
+    def _():
+        out_ref[...] = mine_ref[...]
+
+    @pl.when(jnp.logical_not(own))
+    def _():
+        out_ref[...] = other_ref[...]
+
+
 def make_shards(n_adapter, n_tensor):
     def swap(x, axis, n, k):
         return lax.ppermute(x, axis, [(i, i ^ k) for i in range(n)])
@@ -321,7 +333,6 @@
         shrink_weight,
         expand_weight,
     ):
-        low = lax.axis_index("tensor") % 2
         per_owner = expand_weight.shape[0]
         rank = shrink_weight.shape[2]
         columns = out_weight.shape[1]
@@ -451,11 +462,15 @@
             name="finish",
         )(place, *sums, *received)
         other = swap(mine, "tensor", n_tensor, 1)
-        return jnp.where(
-            low == 0,
-            jnp.concatenate([mine, other], axis=1),
-            jnp.concatenate([other, mine], axis=1),
-        )
+        return pl.pallas_call(
+            beside_kernel,
+            out_shape=jax.ShapeDtypeStruct((tokens, columns), BF),
+            grid=(2,),
+            in_specs=[VMEM] * 2,
+            out_specs=pl.BlockSpec((tokens, half), lambda i: (0, i)),
+            compiler_params=pltpu.CompilerParams(vmem_limit_bytes=16 << 20),
+            name="beside",
+        )(mine, other)
 
     return shards
 

time: 42.6 us -> 42.4 us (level)
  other arithmetic: 0.93 us -> 0.01 us
  Pallas kernels: 11.6 us -> 12.2 us
    select_n x1 -> x0, other arithmetic: 0.92 us -> none  [shards(): jnp.where(low == 0, jnp.concatenate([mine, other], axis=1), jnp.concatena...]
    pallas_call x0 -> x1, Pallas kernels: none -> 0.81 us  [shards(): pl.pallas_call(beside_kernel, out_shape=jax.ShapeDtypeStruct((tokens, col...]
where the time goes in v6:
time: 42.4 us; the launch traced here: 42.1 us
  starting transfers between devices  17.5 us (41%)
  Pallas kernels  12.2 us (29%)
  waiting for transfers between devices  8.94 us (21%)
  local copies, waits for them, and re-layouts  3.26 us (8%)
    ppermute x15, starting transfers between devices, swap(): return lax.ppermute(x, axis, [(i, i ^ k) for i in range(n)])  17.5 us
    ppermute x15, waiting for transfers between devices, swap(): return lax.ppermute(x, axis, [(i, i ^ k) for i in range(n)])  8.94 us
    pallas_call x1, Pallas kernels, attend(): pl.pallas_call(functools.partial(attend_kernel, chunk), out_shape=[jax.Sh...  4.14 us
    pallas_call x1, Pallas kernels, shards(): pl.pallas_call(load_kernel, out_shape=[jax.ShapeDtypeStruct(x.shape, BF)...  3.54 us
    unnamed x10, local copies, waits for them, and re-layouts  3.26 us
    pallas_call x2, Pallas kernels, project(): pl.pallas_call(functools.partial(project_kernel, other), out_shape=jax.Sh...  1.54 us
  transfers between devices with their start and end apart: 15, of which 5 were waited for; matrix products, arithmetic and copies ran while one was open for 0% of the time, Pallas kernels for 15%

profile of v6, /device:TPU:0, one launch (start us, length us, event | category | flops | bytes accessed | tf_op | source)
XLA Modules:
  0.0 42.1 jit_solution(17252252638157931921)
XLA Ops:
  0.0 4.1 %attend.1 = (bf16[32,2048]{1,0:T(8,128)(2,1)}, bf16[4,2,16,1024]{3,2,1,0:T(8,128)(2,1)}, bf16[4,2,16,1024]{3,2,1,0:T(8,128)(2,1)}) custom-call(s32[32]{0:T(128)} %length_ref.1, bf16[32,2048]{1,0:T(8,128)(2,1)} %q_hbm.1, bf16[32,64,256]{2,1,0:T(8,128)(2,1)} %k_hbm.1, bf16[32,64,256]{2,1,0:T(8,128)(2,1)} %v_hbm.1, bf16[32,256]{1,0:T(8,128)(2,1)} %nk_hbm.1, ...), custom_call_target="tpu_custom_call" | custom-call | flops 33554432 | bytes 2097152 | tf_op jit(solution)/shard_map/attend/pallas_call | solution.py:151
  4.2 0.5 %collective-permute-start = (bf16[4,2,16,1024]{3,2,1,0:T(8,128)(2,1)}, bf16[4,2,16,1024]{3,2,1,0:T(8,128)(2,1)S(1)}, u32[]{:S(2)}, u32[]{:S(2)}) collective-permute-start(bf16[4,2,16,1024]{3,2,1,0:T(8,128)(2,1)} %get-tuple-element.34), channel_id=1, source_target_pairs={{0,1},{1,0},{2,3},{3,2},{4,5},{5,4},{6,7},{7,6},{8,9},{9,8},{10,11... | collective-permute-start | bytes 786440 | tf_op jit(solution)/shard_map/ppermute | solution.py:321
  4.7 3.7 %collective-permute-start.1 = (bf16[32,2048]{1,0:T(8,128)(2,1)}, bf16[32,2048]{1,0:T(8,128)(2,1)S(1)}, u32[]{:S(2)}, u32[]{:S(2)}) collective-permute-start(bf16[32,2048]{1,0:T(8,128)(2,1)} %get-tuple-element.37.refs_0_), channel_id=1, source_target_pairs={{0,8},{4,12},{8,0},{12,4},{1,9},{5,13},{9,1},{13,5},{2,10},{6,14},... | collective-permute-start | bytes 393224 | tf_op jit(solution)/shard_map/ppermute | solution.py:321
  8.3 1.6 %collective-permute-start.2 = (bf16[32,2048]{1,0:T(8,128)(2,1)}, bf16[32,2048]{1,0:T(8,128)(2,1)S(1)}, u32[]{:S(2)}, u32[]{:S(2)}) collective-permute-start(bf16[32,2048]{1,0:T(8,128)(2,1)} %get-tuple-element.37.refs_0_), channel_id=1, source_target_pairs={{0,4},{4,0},{8,12},{12,8},{1,5},{5,1},{9,13},{13,9},{2,6},{6,2},{1... | collective-permute-start | bytes 393224 | tf_op jit(solution)/shard_map/ppermute | solution.py:321
  9.9 1.0 %collective-permute-start.10 = (bf16[4,2,16,1024]{3,2,1,0:T(8,128)(2,1)}, bf16[4,2,16,1024]{3,2,1,0:T(8,128)(2,1)S(1)}, u32[]{:S(2)}, u32[]{:S(2)}) collective-permute-start(bf16[4,2,16,1024]{3,2,1,0:T(8,128)(2,1)} %get-tuple-element.34), channel_id=1, source_target_pairs={{0,3},{1,2},{2,1},{3,0},{4,7},{5,6},{6,5},{7,4},{8,11},{9,10},{10,... | collective-permute-start | bytes 786440 | tf_op jit(solution)/shard_map/ppermute | solution.py:321
  10.9 0.8 %collective-permute-start.9 = (bf16[4,2,16,1024]{3,2,1,0:T(8,128)(2,1)}, bf16[4,2,16,1024]{3,2,1,0:T(8,128)(2,1)S(1)}, u32[]{:S(2)}, u32[]{:S(2)}) collective-permute-start(bf16[4,2,16,1024]{3,2,1,0:T(8,128)(2,1)} %get-tuple-element.57.refs_4_), channel_id=1, source_target_pairs={{0,2},{1,3},{2,0},{3,1},{4,6},{5,7},{6,4},{7,5},{8,10},{9,11},{10,... | collective-permute-start | bytes 786440 | tf_op jit(solution)/shard_map/ppermute | solution.py:321
  11.7 0.7 %copy-done.3 = s32[128]{0:T(128)S(1)} copy-done((s32[128]{0:T(128)S(1)}, s32[128]{0:T(128)}, u32[]{:S(2)}) %copy-start.3) | copy-done | bytes 536
  12.3 0.7 %copy-done.4 = s32[8]{0:T(128)S(1)} copy-done((s32[8]{0:T(128)S(1)}, s32[8]{0:T(128)}, u32[]{:S(2)}) %copy-start.4) | copy-done | bytes 56
  13.0 0.7 %ids.1 = (f32[128,2]{1,0:T(8,128)S(1)}, bf16[64,128]{1,0:T(8,128)(2,1)S(1)}, bf16[128,256]{1,0:T(8,128)(2,1)S(1)}, bf16[64,64]{1,0:T(8,128)(2,1)S(1)}) custom-call(s32[1,128]{1,0:T(1,128)S(1)} %bitcast.3, s32[8]{0:T(128)S(1)} %copy-done.4), custom_call_target="tpu_custom_call" | custom-call | tf_op jit(solution)/shard_map/ids/pallas_call | solution.py:363
  13.7 0.0 copy-start
  13.7 1.0 %copy-done = bf16[2,2048,64]{1,2,0:T(8,128)(2,1)S(1)} copy-done((bf16[2,2048,64]{1,2,0:T(8,128)(2,1)S(1)}, bf16[2,2048,64]{1,2,0:T(8,128)(2,1)}, u32[]{:S(2)}) %copy-start) | copy-done | bytes 524312
  14.7 0.9 %copy-done.2 = bf16[32,2048]{1,0:T(8,128)(2,1)S(1)} copy-done((bf16[32,2048]{1,0:T(8,128)(2,1)S(1)}, bf16[32,2048]{1,0:T(8,128)(2,1)}, u32[]{:S(2)}) %copy-start.2) | copy-done | bytes 131096
  15.6 3.5 %load.1 = (bf16[32,2048]{1,0:T(8,128)(2,1)S(1)}, bf16[2048,2048]{1,0:T(8,128)(2,1)S(1)}, bf16[2,64,2048]{2,1,0:T(8,128)(2,1)S(1)}) custom-call(bf16[32,2048]{1,0:T(8,128)(2,1)S(1)} %copy-done.2, bf16[2048,2048]{1,0:T(8,128)(2,1)} %refs_1_, bf16[2,64,2048]{2,1,0:T(8,128)(2,1)S(1)} %bitcast.2), custom_call_target="tpu_custom_call" | custom-call | bytes 16777216 | tf_op jit(solution)/shard_map/load/pallas_call | solution.py:380
  19.2 0.3 collective-permute-done.3.refs_3_
  19.5 0.5 %shrink.1 = f32[64,128]{1,0:T(8,128)S(1)} custom-call(bf16[32,2048]{1,0:T(8,128)(2,1)S(1)} %get-tuple-element.43.refs_0_, bf16[32,2048]{1,0:T(8,128)(2,1)S(1)} %collective-permute-done.1.refs_1_, bf16[32,2048]{1,0:T(8,128)(2,1)S(1)} %collective-permute-done.2.refs_2_, bf16[32,2048]{1,0:T(8,128)(2,1)S(1)} %collective-permute-done.3.refs_3_, ...), custom_call_target="tpu_custom_call" | custom-call | tf_op jit(solution)/shard_map/shrink/pallas_call | solution.py:394
  20.0 0.0 collective-permute-start.5
  20.0 0.8 %project.3 = bf16[128,1024]{1,0:T(8,128)(2,1)S(1)} custom-call(bf16[32,2048]{1,0:T(8,128)(2,1)S(1)} %get-tuple-element.43.refs_0_, bf16[32,2048]{1,0:T(8,128)(2,1)S(1)} %collective-permute-done.1.refs_1_, bf16[32,2048]{1,0:T(8,128)(2,1)S(1)} %collective-permute-done.2.refs_2_, bf16[32,2048]{1,0:T(8,128)(2,1)S(1)} %collective-permute-done.3.refs_3_, ...), custom_call_target="tpu_custom_call" | custom-call | flops 536870912 | bytes 8388608 | tf_op jit(solution)/shard_map/project/pallas_call | solution.py:409
  20.8 0.5 %collective-permute-start.4 = (bf16[128,1024]{1,0:T(8,128)(2,1)S(1)}, bf16[128,1024]{1,0:T(8,128)(2,1)S(1)}, u32[]{:S(2)}, u32[]{:S(2)}) collective-permute-start(bf16[128,1024]{1,0:T(8,128)(2,1)S(1)} %project.3), channel_id=1, source_target_pairs={{0,1},{1,0},{2,3},{3,2},{4,5},{5,4},{6,7},{7,6},{8,9},{9,8},{10,11... | collective-permute-start | bytes 786440 | tf_op jit(solution)/shard_map/ppermute | solution.py:321
  21.3 1.6 %collective-permute-start.6 = (bf16[64,128]{1,0:T(8,128)(2,1)S(1)}, bf16[64,128]{1,0:T(8,128)(2,1)S(1)}, u32[]{:S(2)}, u32[]{:S(2)}) collective-permute-start(bf16[64,128]{1,0:T(8,128)(2,1)S(1)} %add_convert_fusion.refs_0_), channel_id=1, source_target_pairs={{0,2},{1,3},{2,0},{3,1},{4,6},{5,7},{6,4},{7,5},{8,10},{9,11},{10,... | collective-permute-start | bytes 49160 | tf_op jit(solution)/shard_map/ppermute | solution.py:321
  22.9 0.8 %project.2.keep_ref = f32[128,1024]{1,0:T(8,128)S(1)} custom-call(bf16[32,2048]{1,0:T(8,128)(2,1)S(1)} %get-tuple-element.43.refs_0_, bf16[32,2048]{1,0:T(8,128)(2,1)S(1)} %collective-permute-done.1.refs_1_, bf16[32,2048]{1,0:T(8,128)(2,1)S(1)} %collective-permute-done.2.refs_2_, bf16[32,2048]{1,0:T(8,128)(2,1)S(1)} %collective-permute-done.3.refs_3_, ...), custom_call_target="tpu_custom_call" | custom-call | flops 536870912 | bytes 8388608 | tf_op jit(solution)/shard_map/project/pallas_call | solution.py:409
  23.7 1.4 %collective-permute-done.6.refs_1_ = bf16[64,128]{1,0:T(8,128)(2,1)S(1)} collective-permute-done((bf16[64,128]{1,0:T(8,128)(2,1)S(1)}, bf16[64,128]{1,0:T(8,128)(2,1)S(1)}, u32[]{:S(2)}, u32[]{:S(2)}) %collective-permute-start.6) | collective-permute-done | bytes 16416 | tf_op jit(solution)/shard_map/ppermute | solution.py:321
  25.2 0.7 %terms.1 = (bf16[64,1024]{1,0:T(8,128)(2,1)S(1)}, bf16[64,1024]{1,0:T(8,128)(2,1)S(1)}, bf16[64,1024]{1,0:T(8,128)(2,1)S(1)}, bf16[64,1024]{1,0:T(8,128)(2,1)S(1)}) custom-call(bf16[64,128]{1,0:T(8,128)(2,1)S(1)} %add_convert_fusion.refs_0_, bf16[64,128]{1,0:T(8,128)(2,1)S(1)} %collective-permute-done.6.refs_1_, ...), custom_call_target="tpu_custom_call" | custom-call | tf_op jit(solution)/shard_map/terms/pallas_call | solution.py:435
  25.8 4.3 %collective-permute-start.11 = (bf16[64,1024]{1,0:T(8,128)(2,1)S(1)}, bf16[64,1024]{1,0:T(8,128)(2,1)S(1)}, u32[]{:S(2)}, u32[]{:S(2)}) collective-permute-start(bf16[64,1024]{1,0:T(8,128)(2,1)S(1)} %get-tuple-element.60), channel_id=1, source_target_pairs={{0,8},{4,12},{8,0},{12,4},{1,9},{5,13},{9,1},{13,5},{2,10},{6,14},... | collective-permute-start | bytes 393224 | tf_op jit(solution)/shard_map/ppermute | solution.py:321
  30.1 1.5 %collective-permute-start.13 = (bf16[64,1024]{1,0:T(8,128)(2,1)S(1)}, bf16[64,1024]{1,0:T(8,128)(2,1)S(1)}, u32[]{:S(2)}, u32[]{:S(2)}) collective-permute-start(bf16[64,1024]{1,0:T(8,128)(2,1)S(1)} %get-tuple-element.62), channel_id=1, source_target_pairs={{0,12},{4,8},{8,4},{12,0},{1,13},{5,9},{9,5},{13,1},{2,14},{6,10},... | collective-permute-start | bytes 393224 | tf_op jit(solution)/shard_map/ppermute | solution.py:321
  31.7 1.5 %collective-permute-start.7 = (bf16[64,1024]{1,0:T(8,128)(2,1)S(1)}, bf16[64,1024]{1,0:T(8,128)(2,1)S(1)}, u32[]{:S(2)}, u32[]{:S(2)}) collective-permute-start(bf16[64,1024]{1,0:T(8,128)(2,1)S(1)} %get-tuple-element.51.refs_0_), channel_id=1, source_target_pairs={{0,2},{1,3},{2,0},{3,1},{4,6},{5,7},{6,4},{7,5},{8,10},{9,11},{10,... | collective-permute-start | bytes 393224 | tf_op jit(solution)/shard_map/ppermute | solution.py:321
  33.2 0.5 %collective-permute-start.8 = (bf16[64,1024]{1,0:T(8,128)(2,1)S(1)}, bf16[64,1024]{1,0:T(8,128)(2,1)S(1)}, u32[]{:S(2)}, u32[]{:S(2)}) collective-permute-start(bf16[64,1024]{1,0:T(8,128)(2,1)S(1)} %get-tuple-element.52.refs_2_), channel_id=1, source_target_pairs={{0,2},{1,3},{2,0},{3,1},{4,6},{5,7},{6,4},{7,5},{8,10},{9,11},{10,... | collective-permute-start | bytes 393224 | tf_op jit(solution)/shard_map/ppermute | solution.py:321
  33.7 3.7 %collective-permute-done.11.refs_5_ = bf16[64,1024]{1,0:T(8,128)(2,1)S(1)} collective-permute-done((bf16[64,1024]{1,0:T(8,128)(2,1)S(1)}, bf16[64,1024]{1,0:T(8,128)(2,1)S(1)}, u32[]{:S(2)}, u32[]{:S(2)}) %collective-permute-start.11) | collective-permute-done | bytes 131104 | tf_op jit(solution)/shard_map/ppermute | solution.py:321
  37.4 2.0 %collective-permute-done.12.refs_6_ = bf16[64,1024]{1,0:T(8,128)(2,1)S(1)} collective-permute-done((bf16[64,1024]{1,0:T(8,128)(2,1)S(1)}, bf16[64,1024]{1,0:T(8,128)(2,1)S(1)}, u32[]{:S(2)}, u32[]{:S(2)}) %collective-permute-start.12) | collective-permute-done | bytes 131104 | tf_op jit(solution)/shard_map/ppermute | solution.py:321
  39.4 0.2 finish.1.mine_ref
  39.7 0.1 collective-permute-start.14
  39.8 1.5 %collective-permute-done.14.other_ref = bf16[128,1024]{1,0:T(8,128)(2,1)S(1)} collective-permute-done((bf16[128,1024]{1,0:T(8,128)(2,1)S(1)}, bf16[128,1024]{1,0:T(8,128)(2,1)S(1)}, u32[]{:S(2)}, u32[]{:S(2)}) %collective-permute-start.14) | collective-permute-done | bytes 262176 | tf_op jit(solution)/shard_map/ppermute | solution.py:321
  41.3 0.8 %beside.1 = bf16[128,2048]{1,0:T(8,128)(2,1)} custom-call(bf16[128,1024]{1,0:T(8,128)(2,1)S(1)} %finish.1.mine_ref, bf16[128,1024]{1,0:T(8,128)(2,1)S(1)} %collective-permute-done.14.other_ref), custom_call_target="tpu_custom_call" | custom-call | tf_op jit(solution)/shard_map/beside/pallas_call | solution.py:465
  (19 shorter events, 0.1 us)
Async XLA Ops:
  4.2 6.7 %collective-permute-start = (bf16[4,2,16,1024]{3,2,1,0:T(8,128)(2,1)}, bf16[4,2,16,1024]{3,2,1,0:T(8,128)(2,1)S(1)}, u32[]{:S(2)}, u32[]{:S(2)}) collective-permute-start(bf16[4,2,16,1024]{3,2,1,0:T(8,128)(2,1)} %get-tuple-element.34), channel_id=1, source_target_pairs={{0,1},{1,0},{2,3},{3,2},{4,5},{5,4},{6,7},{7,6},{8,9},{9,8},{10,11... | collective-permute-start | bytes 786440 | tf_op jit(solution)/shard_map/ppermute | solution.py:321
  4.7 14.5 %collective-permute-start.1 = (bf16[32,2048]{1,0:T(8,128)(2,1)}, bf16[32,2048]{1,0:T(8,128)(2,1)S(1)}, u32[]{:S(2)}, u32[]{:S(2)}) collective-permute-start(bf16[32,2048]{1,0:T(8,128)(2,1)} %get-tuple-element.37.refs_0_), channel_id=1, source_target_pairs={{0,8},{4,12},{8,0},{12,4},{1,9},{5,13},{9,1},{13,5},{2,10},{6,14},... | collective-permute-start | bytes 393224 | tf_op jit(solution)/shard_map/ppermute | solution.py:321
  8.3 10.9 %collective-permute-start.2 = (bf16[32,2048]{1,0:T(8,128)(2,1)}, bf16[32,2048]{1,0:T(8,128)(2,1)S(1)}, u32[]{:S(2)}, u32[]{:S(2)}) collective-permute-start(bf16[32,2048]{1,0:T(8,128)(2,1)} %get-tuple-element.37.refs_0_), channel_id=1, source_target_pairs={{0,4},{4,0},{8,12},{12,8},{1,5},{5,1},{9,13},{13,9},{2,6},{6,2},{1... | collective-permute-start | bytes 393224 | tf_op jit(solution)/shard_map/ppermute | solution.py:321
  9.9 9.6 %collective-permute-start.3 = (bf16[32,2048]{1,0:T(8,128)(2,1)}, bf16[32,2048]{1,0:T(8,128)(2,1)S(1)}, u32[]{:S(2)}, u32[]{:S(2)}) collective-permute-start(bf16[32,2048]{1,0:T(8,128)(2,1)} %get-tuple-element.37.refs_0_), channel_id=1, source_target_pairs={{0,12},{4,8},{8,4},{12,0},{1,13},{5,9},{9,5},{13,1},{2,14},{6,10},... | collective-permute-start | bytes 393224 | tf_op jit(solution)/shard_map/ppermute | solution.py:321
  9.9 15.2 %collective-permute-start.10 = (bf16[4,2,16,1024]{3,2,1,0:T(8,128)(2,1)}, bf16[4,2,16,1024]{3,2,1,0:T(8,128)(2,1)S(1)}, u32[]{:S(2)}, u32[]{:S(2)}) collective-permute-start(bf16[4,2,16,1024]{3,2,1,0:T(8,128)(2,1)} %get-tuple-element.34), channel_id=1, source_target_pairs={{0,3},{1,2},{2,1},{3,0},{4,7},{5,6},{6,5},{7,4},{8,11},{9,10},{10,... | collective-permute-start | bytes 786440 | tf_op jit(solution)/shard_map/ppermute | solution.py:321
  10.9 14.3 %collective-permute-start.9 = (bf16[4,2,16,1024]{3,2,1,0:T(8,128)(2,1)}, bf16[4,2,16,1024]{3,2,1,0:T(8,128)(2,1)S(1)}, u32[]{:S(2)}, u32[]{:S(2)}) collective-permute-start(bf16[4,2,16,1024]{3,2,1,0:T(8,128)(2,1)} %get-tuple-element.57.refs_4_), channel_id=1, source_target_pairs={{0,2},{1,3},{2,0},{3,1},{4,6},{5,7},{6,4},{7,5},{8,10},{9,11},{10,... | collective-permute-start | bytes 786440 | tf_op jit(solution)/shard_map/ppermute | solution.py:321
  11.7 0.7 %copy-start.3 = (s32[128]{0:T(128)S(1)}, s32[128]{0:T(128)}, u32[]{:S(2)}) copy-start(s32[128]{0:T(128)} %param.17) | copy-start | bytes 1540
  12.3 0.7 %copy-start.4 = (s32[8]{0:T(128)S(1)}, s32[8]{0:T(128)}, u32[]{:S(2)}) copy-start(s32[8]{0:T(128)} %slots_ref.1) | copy-start | bytes 100
  13.7 1.0 %copy-start = (bf16[2,2048,64]{1,2,0:T(8,128)(2,1)S(1)}, bf16[2,2048,64]{1,2,0:T(8,128)(2,1)}, u32[]{:S(2)}) copy-start(bf16[2,2048,64]{1,2,0:T(8,128)(2,1)} %param.20) | copy-start | bytes 1572868
  14.7 0.9 %copy-start.2 = (bf16[32,2048]{1,0:T(8,128)(2,1)S(1)}, bf16[32,2048]{1,0:T(8,128)(2,1)}, u32[]{:S(2)}) copy-start(bf16[32,2048]{1,0:T(8,128)(2,1)} %get-tuple-element.37.refs_0_) | copy-start | bytes 393220
  20.0 1.4 %collective-permute-start.5 = (f32[64,128]{1,0:T(8,128)S(1)}, f32[64,128]{1,0:T(8,128)S(1)}, u32[]{:S(2)}, u32[]{:S(2)}) collective-permute-start(f32[64,128]{1,0:T(8,128)S(1)} %shrink.1), channel_id=1, source_target_pairs={{0,1},{1,0},{2,3},{3,2},{4,5},{5,4},{6,7},{7,6},{8,9},{9,8},{10,11... | collective-permute-start | bytes 98312 | tf_op jit(solution)/shard_map/ppermute | solution.py:321
  20.0 5.2 %copy-start.1 = (bf16[4,2,16,1024]{3,2,1,0:T(8,128)(2,1)S(1)}, bf16[4,2,16,1024]{3,2,1,0:T(8,128)(2,1)}, u32[]{:S(2)}) copy-start(bf16[4,2,16,1024]{3,2,1,0:T(8,128)(2,1)} %get-tuple-element.57.refs_4_) | copy-start | bytes 786436
  20.8 2.9 %collective-permute-start.4 = (bf16[128,1024]{1,0:T(8,128)(2,1)S(1)}, bf16[128,1024]{1,0:T(8,128)(2,1)S(1)}, u32[]{:S(2)}, u32[]{:S(2)}) collective-permute-start(bf16[128,1024]{1,0:T(8,128)(2,1)S(1)} %project.3), channel_id=1, source_target_pairs={{0,1},{1,0},{2,3},{3,2},{4,5},{5,4},{6,7},{7,6},{8,9},{9,8},{10,11... | collective-permute-start | bytes 786440 | tf_op jit(solution)/shard_map/ppermute | solution.py:321
  21.3 3.8 %collective-permute-start.6 = (bf16[64,128]{1,0:T(8,128)(2,1)S(1)}, bf16[64,128]{1,0:T(8,128)(2,1)S(1)}, u32[]{:S(2)}, u32[]{:S(2)}) collective-permute-start(bf16[64,128]{1,0:T(8,128)(2,1)S(1)} %add_convert_fusion.refs_0_), channel_id=1, source_target_pairs={{0,2},{1,3},{2,0},{3,1},{4,6},{5,7},{6,4},{7,5},{8,10},{9,11},{10,... | collective-permute-start | bytes 49160 | tf_op jit(solution)/shard_map/ppermute | solution.py:321
  25.8 11.5 %collective-permute-start.11 = (bf16[64,1024]{1,0:T(8,128)(2,1)S(1)}, bf16[64,1024]{1,0:T(8,128)(2,1)S(1)}, u32[]{:S(2)}, u32[]{:S(2)}) collective-permute-start(bf16[64,1024]{1,0:T(8,128)(2,1)S(1)} %get-tuple-element.60), channel_id=1, source_target_pairs={{0,8},{4,12},{8,0},{12,4},{1,9},{5,13},{9,1},{13,5},{2,10},{6,14},... | collective-permute-start | bytes 393224 | tf_op jit(solution)/shard_map/ppermute | solution.py:321
  30.1 9.3 %collective-permute-start.12 = (bf16[64,1024]{1,0:T(8,128)(2,1)S(1)}, bf16[64,1024]{1,0:T(8,128)(2,1)S(1)}, u32[]{:S(2)}, u32[]{:S(2)}) collective-permute-start(bf16[64,1024]{1,0:T(8,128)(2,1)S(1)} %get-tuple-element.61), channel_id=1, source_target_pairs={{0,4},{4,0},{8,12},{12,8},{1,5},{5,1},{9,13},{13,9},{2,6},{6,2},{1... | collective-permute-start | bytes 393224 | tf_op jit(solution)/shard_map/ppermute | solution.py:321
  30.1 9.3 %collective-permute-start.13 = (bf16[64,1024]{1,0:T(8,128)(2,1)S(1)}, bf16[64,1024]{1,0:T(8,128)(2,1)S(1)}, u32[]{:S(2)}, u32[]{:S(2)}) collective-permute-start(bf16[64,1024]{1,0:T(8,128)(2,1)S(1)} %get-tuple-element.62), channel_id=1, source_target_pairs={{0,12},{4,8},{8,4},{12,0},{1,13},{5,9},{9,5},{13,1},{2,14},{6,10},... | collective-permute-start | bytes 393224 | tf_op jit(solution)/shard_map/ppermute | solution.py:321
  31.7 7.7 %collective-permute-start.7 = (bf16[64,1024]{1,0:T(8,128)(2,1)S(1)}, bf16[64,1024]{1,0:T(8,128)(2,1)S(1)}, u32[]{:S(2)}, u32[]{:S(2)}) collective-permute-start(bf16[64,1024]{1,0:T(8,128)(2,1)S(1)} %get-tuple-element.51.refs_0_), channel_id=1, source_target_pairs={{0,2},{1,3},{2,0},{3,1},{4,6},{5,7},{6,4},{7,5},{8,10},{9,11},{10,... | collective-permute-start | bytes 393224 | tf_op jit(solution)/shard_map/ppermute | solution.py:321
  33.2 6.3 %collective-permute-start.8 = (bf16[64,1024]{1,0:T(8,128)(2,1)S(1)}, bf16[64,1024]{1,0:T(8,128)(2,1)S(1)}, u32[]{:S(2)}, u32[]{:S(2)}) collective-permute-start(bf16[64,1024]{1,0:T(8,128)(2,1)S(1)} %get-tuple-element.52.refs_2_), channel_id=1, source_target_pairs={{0,2},{1,3},{2,0},{3,1},{4,6},{5,7},{6,4},{7,5},{8,10},{9,11},{10,... | collective-permute-start | bytes 393224 | tf_op jit(solution)/shard_map/ppermute | solution.py:321
  39.7 1.6 %collective-permute-start.14 = (bf16[128,1024]{1,0:T(8,128)(2,1)S(1)}, bf16[128,1024]{1,0:T(8,128)(2,1)S(1)}, u32[]{:S(2)}, u32[]{:S(2)}) collective-permute-start(bf16[128,1024]{1,0:T(8,128)(2,1)S(1)} %finish.1.mine_ref), channel_id=1, source_target_pairs={{0,1},{1,0},{2,3},{3,2},{4,5},{5,4},{6,7},{7,6},{8,9},{9,8},{10,11... | collective-permute-start | bytes 786440 | tf_op jit(solution)/shard_map/ppermute | solution.py:321
